TPU v7x, 256 devices: a whole 4x4x8 slice. The times are simulated.
256 devices in a mesh: dp: 16 (over x_lo, y, core), tensor: 16 (over z, x_hi).
Axes of the slice: x: 4 (x_hi: 2, x_lo: 2; x = x_hi * 2 + x_lo), y: 4, z: 8, core: 2. Of those that a mesh axis runs over, the one named last changes fastest.
Arguments:
- layer_input: bfloat16 [16384, 4096], P(('dp', 'tensor')), parts along dimension 0, may hold values from -6 to 10
- norm_gain: float32 [4096], replicated, may hold values from 0.25 to 1.75
- query_weight: bfloat16 [4096, 4096], P(None, 'tensor'), may hold values from -1 to 1
- key_weight: bfloat16 [4096, 1024], P(None, 'tensor'), may hold values from -1 to 1
- value_matrix: bfloat16 [4096, 1024], P(None, 'tensor'), may hold values from -0.09375 to 0.09375
- output_weight: bfloat16 [4096, 4096], P('tensor'), may hold values from -0.09375 to 0.09375
- keep_bits: int32 [512, 16, 16], P(('dp', 'tensor')), parts along dimension 0, may hold values 0 or 1
Outputs:
- layer_output: bfloat16 [16384, 4096], P(('dp', 'tensor')), parts along dimension 0
There are 16 independent parts, one for each index of `dp`. A program takes and returns all parts, laid end to end along the dimension named above; an argument that names none is the same for every part. Nothing has to cross between parts.
All inputs are finite; a program needn't handle non-finite values. No bound on the sum of `keep_bits` on one device may be relied on, other than what follows from the above.
Results may differ from a plain program's by a relative error of at most 0.0095.
Values may be sent and summed in bfloat16 or wider, within the bound.
No kernel may reach another device: no remote copies, remote signals or barrier semaphores. Data moves between devices by JAX's collectives and lax.ppermute only.
A program may use at most 128 MiB of HBM per device.

v0:
```python
import jax
import jax.numpy as jnp
from jax import lax
from jax.sharding import Mesh
from jax.sharding import PartitionSpec as P

HEAD_SIZE = 128
BLOCK = 64
TENSOR = ("tensor_0", "tensor_1")
DP_TENSOR = ("dp", "tensor_0", "tensor_1")


theta_base = 1000000.0


def from_partner(array, axis, distance):
    return lax.ppermute(array, axis, [(i, i ^ 1 << distance) for i in range(lax.axis_size(axis))])


def sum_by_axis(array, axes, dim):
    for axis in axes:
        array = lax.psum_scatter(array, axis, scatter_dimension=dim, tiled=True)
    return array


def apply_rotary(block, token_positions):
    half = block.shape[-1] // 2
    freqs = theta_base ** (-(jnp.arange(half, dtype=jnp.float32) * 2.0) / block.shape[-1])
    angles = token_positions[:, None] * freqs[None, :]
    cosine = jnp.cos(angles)
    sine = jnp.sin(angles)
    first = block[..., :half]
    second = block[..., half:]
    return jnp.concatenate(
        [first * cosine - second * sine, second * cosine + first * sine], axis=-1
    )


def join_pairs(mine, other, lowbit):
    ahead = jnp.concatenate([mine, other], axis=-1)
    behind = jnp.concatenate([other, mine], axis=-1)
    return jnp.where(lowbit, ahead, behind)


def attend(query, key_rows, value_rows, keep_bits):
    heads, sequence_length, width = query.shape
    count = min(8, max(1, sequence_length // 512))
    height = sequence_length // count
    divisor = jnp.sqrt(jnp.float32(HEAD_SIZE))
    results = []
    for number in range(count):
        first_row = number * height
        last_row = first_row + height
        scores = (
            jnp.einsum(
                "hqd,hkd->hqk",
                query[:, first_row:last_row],
                key_rows[:, :last_row],
                preferred_element_type=jnp.float32,
            )
            / divisor
        )
        causal = jnp.arange(last_row)[None, :] <= jnp.arange(first_row, last_row)[:, None]
        scores = jnp.where(causal[None], scores, jnp.float32(-1e30))
        highest = jnp.max(scores, axis=-1, keepdims=True)
        expo_terms = jnp.exp(scores - highest)
        weights = expo_terms / jnp.sum(expo_terms, axis=-1, keepdims=True)
        chosen_bits = keep_bits[
            :, first_row // BLOCK : last_row // BLOCK, : last_row // BLOCK
        ].astype(jnp.float32)
        keeper = jnp.broadcast_to(
            chosen_bits[:, :, None, :, None],
            (heads, height // BLOCK, BLOCK, last_row // BLOCK, BLOCK),
        ).reshape(heads, height, last_row)
        dropped = (weights * keeper / 0.9).astype(jnp.bfloat16)
        outcome = jnp.einsum(
            "hqk,hkd->hqd", dropped, value_rows[:, :last_row], preferred_element_type=jnp.float32
        )
        results.append(outcome.astype(jnp.bfloat16))
    return jnp.concatenate(results, axis=1)


def on_device(
    layer_input, norm_gain, query_weight, key_weight, value_matrix, output_weight, keep_bits
):
    position = lax.axis_index(TENSOR)
    inputs = layer_input.astype(jnp.float32)
    scaled = lax.rsqrt(jnp.mean(inputs * inputs, axis=-1, keepdims=True) + 1e-05)
    normed = (inputs * scaled * norm_gain[None, :]).astype(jnp.bfloat16)
    query_cols = query_weight.shape[1]
    kv_cols = key_weight.shape[1]
    piece = lax.all_gather(normed, TENSOR, axis=0, tiled=True)
    projected = jnp.concatenate(
        [
            jnp.dot(piece, query_weight, preferred_element_type=jnp.float32),
            jnp.dot(piece, key_weight, preferred_element_type=jnp.float32),
            jnp.dot(piece, value_matrix, preferred_element_type=jnp.float32),
        ],
        axis=1,
    )
    query_raw = projected[:, :query_cols]
    paired = jnp.stack(
        [projected[:, query_cols : query_cols + kv_cols], projected[:, query_cols + kv_cols :]]
    ).astype(jnp.bfloat16)
    other = from_partner(paired, TENSOR, 0)
    paired = join_pairs(paired, other, position >> 0 & 1 == 0)
    sequence_length = query_raw.shape[0]
    local_heads = query_cols // HEAD_SIZE
    local_kv = paired.shape[2] // HEAD_SIZE
    token_positions = jnp.arange(sequence_length).astype(jnp.float32)
    query = apply_rotary(
        query_raw.reshape(sequence_length, local_heads, HEAD_SIZE).transpose(1, 0, 2),
        token_positions,
    ).astype(jnp.bfloat16)
    key_rows = apply_rotary(
        paired[0]
        .astype(jnp.float32)
        .reshape(sequence_length, local_kv, HEAD_SIZE)
        .transpose(1, 0, 2),
        token_positions,
    ).astype(jnp.bfloat16)
    value_rows = paired[1].reshape(sequence_length, local_kv, HEAD_SIZE).transpose(1, 0, 2)
    key_rows = jnp.broadcast_to(key_rows, (local_heads, sequence_length, HEAD_SIZE))
    value_rows = jnp.broadcast_to(value_rows, (local_heads, sequence_length, HEAD_SIZE))
    heads = attend(query, key_rows, value_rows, keep_bits)
    heads_out = heads.transpose(1, 0, 2).reshape(sequence_length, query_cols)
    terms = jnp.dot(heads_out, output_weight, preferred_element_type=jnp.float32).astype(
        jnp.bfloat16
    )
    total = sum_by_axis(terms, TENSOR, 0).astype(jnp.float32)
    return (inputs + total).astype(jnp.bfloat16)


def solution(mesh):
    split = Mesh(mesh.devices.reshape(mesh.shape["dp"], 8, 2), ("dp", "tensor_0", "tensor_1"))
    return jax.shard_map(
        on_device,
        mesh=split,
        in_specs=(
            P(DP_TENSOR, None),
            P(),
            P(None, TENSOR),
            P(None, TENSOR),
            P(None, TENSOR),
            P(TENSOR, None),
            P(DP_TENSOR, None, None),
        ),
        out_specs=P(DP_TENSOR, None),
        check_vma=False,
    )
```

profile of v0, /device:TPU:6, one launch (start us, length us, event | category | flops | bytes accessed | tf_op | source)
XLA Modules:
  0.0 323.7 jit_solution(4279456169730043281)
XLA Ops:
  6.5 0.0 copy-start
  6.5 0.0 all-gather.2.cloned.1.call-start
  6.5 1.4 fusion.15
  7.9 2.0 fusion.17
  10.0 0.0 all-gather.2.cloned.1.call-update
  10.0 0.0 reduce-scatter.3.cloned.1.call-start
  10.1 0.7 slice_convert_fusion.2
  10.8 0.1 copy.17
  10.8 2.3 broadcast_in_dim.37
  13.1 4.8 %reshape.211 = f32[2,512,512]{1,2,0:T(8,128)} reshape(f32[2,8,64,8,64]{2,1,4,3,0:T(8,128)} %broadcast_in_dim.37) | data formatting | bytes 4194304 | tf_op jit(solution)/shard_map/reshape | solution.py:74
  17.9 0.0 copy-done.9
  17.9 3.8 %broadcast_in_dim.42 = f32[2,8,64,16,64]{4,3,2,1,0:T(8,128)} broadcast(f32[2,8,16]{2,1,0:T(8,128)S(1)} %slice_convert_fusion.1), dimensions={0,1,3} | broadcast | bytes 4195328 | tf_op jit(solution)/shard_map/broadcast_in_dim | solution.py:71
  21.8 7.7 %reshape.212 = f32[2,512,1024]{2,1,0:T(8,128)} reshape(f32[2,8,64,16,64]{4,3,2,1,0:T(8,128)} %broadcast_in_dim.42) | data formatting | bytes 8388608 | tf_op jit(solution)/shard_map/reshape | solution.py:74
  29.5 0.8 iota_compare_fusion.1
  30.3 1.1 iota_compare_fusion
  31.5 3.0 multiply_cosine_fusion
  34.5 112.9 %all-gather.2.cloned.1.call-done = bf16[1024,4096]{1,0:T(8,128)(2,1)} async-done(((bf16[64,4096]{1,0:T(8,128)(2,1)}), bf16[1024,4096]{1,0:T(8,128)(2,1)}) %all-gather.2.cloned.1.call-update) | async-done | bytes 8388624 | tf_op jit(solution)/shard_map/all_gather | solution.py:92
  147.4 7.4 %fusion.88 = f32[1024,256]{0,1:T(8,128)} fusion(bf16[1024,4096]{1,0:T(8,128)(2,1)} %all-gather.2.cloned.1.call-done, bf16[4096,256]{1,0:T(8,128)(2,1)} %param.9), kind=kOutput, calls=%fused_computation.89 | convolution fusion | flops 2147483648 | bytes 11534336 | tf_op jit(solution)/shard_map/dot_general | solution.py:95
  154.8 1.5 copy.15
  156.3 0.0 copy-start.1
  156.3 0.0 copy-start.5
  156.3 6.2 %fusion.14 = bf16[1,1024,64]{1,2,0:T(8,128)(2,1)S(1)} fusion(bf16[1024,4096]{1,0:T(8,128)(2,1)} %all-gather.2.cloned.1.call-done, bf16[4096,64]{0,1:T(8,128)(2,1)} %param.11), kind=kOutput, calls=%fused_computation.27 | convolution fusion | flops 536936448 | bytes 9043968 | tf_op jit(solution)/shard_map/dot_general | solution.py:97
  162.6 0.0 copy-done.1
  162.6 0.0 copy-done.5
  162.6 0.0 copy-start.3
  162.6 2.7 fusion.13
  165.3 2.3 collective-permute-start
  167.7 1.4 subtract_convert_fusion
  169.1 5.6 %collective-permute-done = bf16[2,1024,64]{1,2,0:T(8,128)(2,1)S(1)} collective-permute-done((bf16[2,1024,64]{1,2,0:T(8,128)(2,1)S(1)}, bf16[2,1024,64]{1,2,0:T(8,128)(2,1)S(1)}, u32[]{:S(2)}, u32[]{:S(2)}) %collective-permute-start) | collective-permute-done | bytes 262176 | tf_op jit(solution)/shard_map/ppermute | solution.py:17
  174.7 0.1 maximum_select_fusion
  174.9 0.1 slice_bitcast_fusion
  175.0 0.7 copy.18
  175.7 0.8 copy.21
  176.5 1.1 fusion.30
  177.7 0.1 copy.16
  177.8 0.8 copy.20
  178.7 0.0 copy-done.6
  178.7 4.0 %fusion.11 = bf16[2,512,128]{2,1,0:T(8,128)(2,1)} fusion(f32[2,512,512]{1,2,0:T(8,128)} %reshape.211, bf16[512,128]{1,0:T(8,128)(2,1)} %copy.18, pred[512,512]{0,1:T(8,128)(4,1)} %iota_compare_fusion.1, bf16[2,1024,64]{2,1,0:T(8,128)(2,1)S(1)} %copy-done.6, bf16[2,1024,64]{2,1,0:T(8,128)(2,1)} %get-tuple-element.6, bf16[512,128]{1,0:T(8,128)(2,1)S(1)} %copy.16), kind=kOutput, calls=%fused_computation.22 | convolution fusion | flops 272763904 | bytes 3407872 | tf_op jit(solution)/shard_map/hqk,hkd->hqd/dot_general | solution.py:76
  182.8 5.6 %fusion.12 = bf16[2,512,128]{2,1,0:T(8,128)(2,1)} fusion(f32[2,512,1024]{2,1,0:T(8,128)} %reshape.212, bf16[1024,128]{1,0:T(8,128)(2,1)S(1)} %copy-done.8, pred[512,1024]{1,0:T(8,128)(4,1)} %iota_compare_fusion, bf16[1024,128]{1,0:T(8,128)(2,1)} %copy.20, bf16[2,1024,64]{2,1,0:T(8,128)(2,1)S(1)} %copy-done.7, bf16[2,1024,64]{2,1,0:T(8,128)(2,1)S(1)} %copy-done.6), kind=kOutput, calls=%fused_computation.23 | convolution fusion | flops 544870400 | bytes 6029312 | tf_op jit(solution)/shard_map/hqk,hkd->hqd/dot_general | solution.py:76
  188.3 1.1 maximum_bitcast_fusion
  189.4 0.2 copy.22
  189.6 5.6 %convolution_convert_fusion = bf16[1024,4096]{1,0:T(8,128)(2,1)} fusion(bf16[1024,256]{0,1:T(8,128)(2,1)S(1)} %bitcast.32, bf16[256,4096]{1,0:T(8,128)(2,1)S(1)} %copy-done), kind=kOutput, calls=%fused_computation.4 | convolution fusion | flops 2151677952 | bytes 11010048 | tf_op jit(solution)/shard_map/dot_general | solution.py:127
  195.2 0.0 reduce-scatter.3.cloned.1.call-update
  195.3 0.0 reduce-scatter.5.cloned.1.call-start
  195.3 93.4 %reduce-scatter.3.cloned.1.call-done = bf16[128,4096]{1,0:T(8,128)(2,1)} async-done(((bf16[1024,4096]{1,0:T(8,128)(2,1)}), bf16[128,4096]{1,0:T(8,128)(2,1)}) %reduce-scatter.3.cloned.1.call-update) | async-done | bytes 1048592 | tf_op jit(solution)/shard_map/reduce_scatter | solution.py:22
  288.7 0.0 reduce-scatter.5.cloned.1.call-update
  288.7 26.5 %reduce-scatter.5.cloned.1.call-done = bf16[64,4096]{1,0:T(8,128)(2,1)} async-done(((bf16[128,4096]{1,0:T(8,128)(2,1)}), bf16[64,4096]{1,0:T(8,128)(2,1)}) %reduce-scatter.5.cloned.1.call-update) | async-done | bytes 524304 | tf_op jit(solution)/shard_map/reduce_scatter | solution.py:22
  315.2 2.0 fusion.18
  (21 shorter events, 0.1 us)
Async XLA Ops:
  6.5 183.1 %copy-start = (bf16[256,4096]{1,0:T(8,128)(2,1)S(1)}, bf16[256,4096]{1,0:T(8,128)(2,1)}, u32[]{:S(2)}) copy-start(bf16[256,4096]{1,0:T(8,128)(2,1)} %param.12) | copy-start | bytes 6291460
  6.5 140.8 %all-gather.2.cloned.1.call-start = ((), (), s32[]{:S(2)}) async-start(), calls=%async_computation.2 | async-start | bytes 8912896 | tf_op jit(solution)/shard_map/all_gather | solution.py:92
  10.0 278.7 %reduce-scatter.3.cloned.1.call-start = ((), (), s32[]{:S(2)}) async-start(), calls=%async_computation.3 | async-start | bytes 9437184 | tf_op jit(solution)/shard_map/reduce_scatter | solution.py:22
  13.1 4.8 %copy-start.9 = (s32[2,16,16]{2,1,0:T(8,128)S(1)}, s32[2,16,16]{2,1,0:T(8,128)}, u32[]{:S(2)}) copy-start(s32[2,16,16]{2,1,0:T(8,128)} %param.13) | copy-start | bytes 6148
  156.3 6.3 %copy-start.1 = (bf16[1024,4096]{1,0:T(8,128)(2,1)S(1)}, bf16[1024,4096]{1,0:T(8,128)(2,1)}, u32[]{:S(2)}) copy-start(bf16[1024,4096]{1,0:T(8,128)(2,1)} %all-gather.2.cloned.1.call-done) | copy-start | bytes 25165828
  156.3 6.3 %copy-start.5 = (bf16[4096,64]{0,1:T(8,128)(2,1)S(1)}, bf16[4096,64]{0,1:T(8,128)(2,1)}, u32[]{:S(2)}) copy-start(bf16[4096,64]{0,1:T(8,128)(2,1)} %param.10) | copy-start | bytes 1572868
  162.6 5.1 %copy-start.3 = (f32[1024,64]{1,0:T(8,128)S(1)}, f32[1024,64]{1,0:T(8,128)}, u32[]{:S(2)}) copy-start(f32[1024,64]{1,0:T(8,128)} %get-tuple-element.11) | copy-start | bytes 786436
  162.6 5.1 %copy-start.4 = (f32[1024,64]{1,0:T(8,128)S(1)}, f32[1024,64]{1,0:T(8,128)}, u32[]{:S(2)}) copy-start(f32[1024,64]{1,0:T(8,128)} %get-tuple-element.12) | copy-start | bytes 786436
  165.3 9.4 %collective-permute-start = (bf16[2,1024,64]{1,2,0:T(8,128)(2,1)S(1)}, bf16[2,1024,64]{1,2,0:T(8,128)(2,1)S(1)}, u32[]{:S(2)}, u32[]{:S(2)}) collective-permute-start(bf16[2,1024,64]{1,2,0:T(8,128)(2,1)S(1)} %pad_maximum_fusion.1), channel_id=1, source_target_pairs={{0,1},{1,0},{2,3},{3,2},{4,5},{5,4},{6,7},{7,6},{8,9},{9,8},{10,11... | collective-permute-start | bytes 786440 | tf_op jit(solution)/shard_map/ppermute | solution.py:17
  169.1 9.6 %copy-start.6 = (bf16[2,1024,64]{2,1,0:T(8,128)(2,1)S(1)}, bf16[2,1024,64]{2,1,0:T(8,128)(2,1)}, u32[]{:S(2)}) copy-start(bf16[2,1024,64]{2,1,0:T(8,128)(2,1)} %get-tuple-element.5) | copy-start | bytes 786436
  178.7 4.1 %copy-start.7 = (bf16[2,1024,64]{2,1,0:T(8,128)(2,1)S(1)}, bf16[2,1024,64]{2,1,0:T(8,128)(2,1)}, u32[]{:S(2)}) copy-start(bf16[2,1024,64]{2,1,0:T(8,128)(2,1)} %get-tuple-element.6) | copy-start | bytes 786436
  178.7 4.1 %copy-start.8 = (bf16[1024,128]{1,0:T(8,128)(2,1)S(1)}, bf16[1024,128]{1,0:T(8,128)(2,1)}, u32[]{:S(2)}) copy-start(bf16[1024,128]{1,0:T(8,128)(2,1)} %copy.21) | copy-start | bytes 786436
  195.2 120.0 %copy-start.2 = (bf16[64,4096]{1,0:T(8,128)(2,1)S(1)}, bf16[64,4096]{1,0:T(8,128)(2,1)}, u32[]{:S(2)}) copy-start(bf16[64,4096]{1,0:T(8,128)(2,1)} %param.7) | copy-start | bytes 1572868
  195.3 120.0 %reduce-scatter.5.cloned.1.call-start = ((), (), s32[]{:S(2)}) async-start(), calls=%async_computation.4 | async-start | bytes 1572864 | tf_op jit(solution)/shard_map/reduce_scatter | solution.py:22
Sparse Core Ops, SparseCore 0:
  10.1 137.1 all-gather.1
  195.4 93.2 reduce-scatter.2
  291.2 24.0 reduce-scatter.4
where the time goes:
time: 327 us; the launch traced here: 324 us
  waiting for transfers between devices  238 us (73%)
  matrix products  31.5 us (10%)
  local copies, waits for them, and re-layouts  23.1 us (7%)
  other arithmetic  15 us (5%)
  between operations  13.3 us (4%)
    reduce_scatter x2, waiting for transfers between devices, sum_by_axis(): array = lax.psum_scatter(array, axis, scatter_dimension=dim, tiled=True)  120 us
    all_gather x1, waiting for transfers between devices, on_device(): piece = lax.all_gather(normed, TENSOR, axis=0, tiled=True)  113 us
    reshape x2, local copies, waits for them, and re-layouts, attend(): keeper = jnp.broadcast_to(chosen_bits[:, :, None, :, None], (heads, heigh...  12.5 us
    dot_general x2, matrix products, attend(): jnp.einsum('hqk,hkd->hqd', dropped, value_rows[:, :last_row], preferred_e...  9.62 us
    dot_general x1, matrix products, on_device(): jnp.dot(piece, query_weight, preferred_element_type=jnp.float32)  7.4 us
  transfers between devices with their start and end apart: 4, of which 4 were waited for; matrix products, arithmetic and copies ran while one was open for 8% of the time, Pallas kernels for 0%

commit v1 on v0

v1 whole, which is shorter than its diff:
```python
import functools
import math

import jax
import jax.numpy as jnp
import numpy as np
from jax import lax
from jax.experimental import pallas as pl
from jax.experimental.pallas import tpu as pltpu
from jax.sharding import Mesh
from jax.sharding import PartitionSpec as P

HEAD = 128
BLOCK = 64
WIDTH = 4096
Z = 8
HALF = 32
COLS = 2048
THETA = 1000000.0
RIGHT = [(i, (i + 1) % Z) for i in range(Z)]
LEFT = [(i, (i - 1) % Z) for i in range(Z)]
NEAR = [0, -1, 1, -2, 2, -3, 3]
BF = jnp.bfloat16
F32 = jnp.float32
TINY = pl.CostEstimate(flops=1000, bytes_accessed=1000, transcendentals=0)


def slot_block(slot, z):
    offset = jnp.where(slot % 2 == 1, -((slot + 1) // 2), slot // 2)
    return lax.rem(z + offset + Z, Z)


def tables():
    freqs = THETA ** (-np.arange(HEAD // 2) * 2.0 / HEAD)

    def table(positions):
        angles = positions[:, None] * freqs[None, :]
        cosine, sine = np.cos(angles), np.sin(angles)
        return np.stack(
            [np.concatenate([cosine, cosine], 1), np.concatenate([-sine, sine], 1)]
        ).astype(np.float32)

    return table(np.arange(16) * float(BLOCK))[:, :, None, :], table(np.arange(BLOCK) * 1.0)


def load_tokens(places, pieces, gain, xs, ss, step):
    depth = xs.shape[1]
    g = gain[...]
    for ref, (start, count) in zip(pieces, places):
        x = ref[...].astype(F32)
        sq = x * x
        part = sq[:, :HEAD]
        for i in range(1, depth // HEAD):
            part = part + sq[:, i * HEAD : (i + 1) * HEAD]
        at = slice(start, start + count)
        ss[at] = jnp.where(step == 0, part, ss[at] + part)
        xs[at] = (x * g).astype(BF)


def angles_of(outer, inner, slot, meta):
    block = slot_block(jnp.int32(slot), meta[1]) * 2 + meta[2]
    co = outer[0, block]
    so = outer[1, block]
    return inner[0] * co - inner[1] * so, inner[1] * co + inner[0] * so


def gather_sum(acc, term, step):
    acc[...] = jnp.where(step == 0, term, acc[...] + term)


def kv_kernel(places, slots, waits, meta, *refs):
    n = len(places)
    pieces = refs[:n]
    gain, kt, vt, got, other, outer, inner = refs[n : n + 7]
    kv, xs, kvs, acc, ss = refs[n + 7 + waits :]
    step = pl.program_id(0)
    early = step < pl.num_programs(0) // 2
    load_tokens(places, pieces, gain, xs, ss, step)
    kvs[0:64] = kt[...]
    kvs[128:192] = vt[...]
    for i in range(xs.shape[1] // 256):
        at = slice(i * 256, (i + 1) * 256)
        low = slice(i * 128, i * 128 + 64)
        high = slice(i * 128 + 64, i * 128 + 128)
        kvs[64:128, at] = jnp.where(early, got[low], other[low])
        kvs[192:256, at] = jnp.where(early, got[high], other[high])
    term = lax.dot_general(
        xs[...], kvs[...], (((1,), (1,)), ((), ())), preferred_element_type=F32
    )
    gather_sum(acc, term, step)

    @pl.when(step == pl.num_programs(0) - 1)
    def _():
        first = meta[2] == 0

        def ordered(t):
            return jnp.where(first, t, pltpu.roll(t, HEAD // 2, 1))

        scale = lax.rsqrt(jnp.sum(ss[...], axis=-1, keepdims=True) / WIDTH + 1e-05)
        kv[1] = ordered(acc[:, HEAD:] * scale).astype(BF)
        key = ordered(acc[:, :HEAD] * scale).astype(BF).astype(F32)
        turned = pltpu.roll(key, HEAD // 2, 1)
        for i, slot in enumerate(slots):
            at = slice(i * BLOCK, (i + 1) * BLOCK)
            c, s = angles_of(outer, inner, slot, meta)
            kv[0, at] = (key[at] * c + turned[at] * s).astype(BF)


def q_kernel(places, slots, waits, meta, *refs):
    n = len(places)
    pieces = refs[:n]
    gain, wq, got, other, outer, inner = refs[n : n + 6]
    q, xs, acc, ss = refs[n + 6 + waits :]
    step = pl.program_id(0)
    load_tokens(places, pieces, gain, xs, ss, step)
    x = xs[...]
    gather_sum(acc.at[:, 0:256], jnp.dot(x, wq[...], preferred_element_type=F32), step)
    w = jnp.where(step < pl.num_programs(0) // 2, got[...], other[...])
    gather_sum(acc.at[:, 256:512], jnp.dot(x, w, preferred_element_type=F32), step)

    @pl.when(step == pl.num_programs(0) - 1)
    def _():
        core = meta[0]
        factor = math.log2(math.e) / math.sqrt(HEAD)
        scale = factor * lax.rsqrt(jnp.sum(ss[...], axis=-1, keepdims=True) / WIDTH + 1e-05)
        for i, slot in enumerate(slots):
            at = slice(i * BLOCK, (i + 1) * BLOCK)
            c, s = angles_of(outer, inner, slot, meta)
            c = c * scale[at]
            s = s * scale[at]
            heads = []
            for h in range(4):
                t = acc[at, h * HEAD : (h + 1) * HEAD]
                heads.append((t * c + pltpu.roll(t, HEAD // 2, 1) * s).astype(BF))
            q[i, 0] = heads[0]
            q[i, 1] = heads[1]
            q[i, 2] = jnp.where(core == 0, heads[2], heads[3])
            q[i, 3] = jnp.where(core == 0, heads[3], heads[2])


def project(queries, after, meta, pieces, places, slots, gain, own, got, other):
    n = len(slots)
    rows = n * BLOCK
    depth = 1024 if queries else 2048
    steps = WIDTH // depth
    outer, inner = tables()
    turn = lambda i, m: lax.rem(steps // 2 * m[0] + i, steps)
    across = lambda i, m: (0, turn(i, m))
    soon = lambda i: jnp.minimum(i, steps // 2 - 1)
    late = lambda i: jnp.maximum(i - steps // 2, 0)
    zero = lambda k: lambda i, m: (0,) * k
    if queries:
        weights = [
            pl.BlockSpec((depth, 256), lambda i, m: (turn(i, m), 0)),
            pl.BlockSpec((depth, 256), lambda i, m: (soon(i), 0)),
            pl.BlockSpec((depth, 256), lambda i, m: (late(i), 0)),
        ]
        shape = (n, 4, BLOCK, HEAD)
        scratch = [pltpu.VMEM((rows, depth), BF), pltpu.VMEM((rows, 512), F32)]
    else:
        weights = [
            pl.BlockSpec((64, depth), across),
            pl.BlockSpec((64, depth), across),
            pl.BlockSpec((depth // 2, 256), lambda i, m: (steps + soon(i), 0)),
            pl.BlockSpec((depth // 2, 256), lambda i, m: (steps + late(i), 0)),
        ]
        shape = (2, rows, HEAD)
        scratch = [
            pltpu.VMEM((rows, depth), BF),
            pltpu.VMEM((256, depth), BF),
            pltpu.VMEM((rows, 256), F32),
        ]
    return pl.pallas_call(
        functools.partial(q_kernel if queries else kv_kernel, places, slots, len(after)),
        grid_spec=pltpu.PrefetchScalarGridSpec(
            num_scalar_prefetch=1,
            grid=(steps,),
            in_specs=[pl.BlockSpec((count, depth), across) for _, count in places]
            + [pl.BlockSpec((1, depth), across)]
            + weights
            + [pl.BlockSpec((2, 16, 1, HEAD), zero(4)), pl.BlockSpec((2, BLOCK, HEAD), zero(3))]
            + [pl.BlockSpec(memory_space=pl.ANY)] * len(after),
            out_specs=pl.BlockSpec(shape, zero(len(shape))),
            scratch_shapes=scratch + [pltpu.VMEM((rows, HEAD), F32)],
        ),
        out_shape=jax.ShapeDtypeStruct(shape, BF),
        compiler_params=pltpu.CompilerParams(vmem_limit_bytes=56 << 20),
        cost_estimate=TINY,
        name="queries" if queries else "keys",
    )(meta, *pieces, gain, *own, got, other, outer, inner, *after)


def attend_kernel(slots, waits, meta, q, bits, kv_near, kv_far, their_near, their_far, *refs):
    wo, wp_got, wp_other = refs[:3]
    outs = refs[3 + waits : -3]
    heads, key, value = refs[-3:]
    nb = len(slots)
    for i, target in ((0, key), (1, value)):
        target[0:448] = kv_near[i]
        target[448:512] = kv_far[i]
        target[512:960] = their_near[i * 448 : (i + 1) * 448]
        target[960:1024] = their_far[i]
    z = meta[1]
    xh = meta[2]
    column = lax.broadcasted_iota(jnp.int32, (1, 1024), 1)
    mine = column < 512
    kblock = slot_block((column // BLOCK) % 8, z) * 2 + jnp.where(mine, xh, 1 - xh)
    kpos = kblock * BLOCK + column % BLOCK
    lane = lax.broadcasted_iota(jnp.int32, (HEAD, 1024), 0)
    hot = [(lane == kblock + h * 16).astype(BF) for h in range(2)]
    core = meta[0]
    for b in range(nb):
        block = slot_block(jnp.int32(slots[b]), z) * 2 + xh
        qpos = block * BLOCK + lax.broadcasted_iota(jnp.int32, (BLOCK, 1), 0)
        row = (lax.broadcasted_iota(jnp.int32, (8, 16), 1) == block).astype(BF)
        ours = jnp.dot(row, bits[...], preferred_element_type=F32).astype(BF)
        theirs = jnp.dot(row, their_near[896:912], preferred_element_type=F32).astype(BF)
        keep = [jnp.dot(ours, hot[h], preferred_element_type=F32)[0:1] for h in range(2)]
        pair = [jnp.dot(theirs, hot[h], preferred_element_type=F32)[0:1] for h in range(2)]
        keep.append(jnp.where(core == 0, pair[0], pair[1]))
        keep.append(jnp.where(core == 0, pair[1], pair[0]))
        bias = jnp.where(kpos <= qpos, 0.0, -1e30)
        s = lax.dot_general(
            q[slots[b]].reshape(256, HEAD),
            key[...],
            (((1,), (1,)), ((), ())),
            preferred_element_type=F32,
        )
        s = s.reshape(4, BLOCK, 1024) + bias[None]
        e = jnp.exp2(s - jnp.max(s, axis=-1, keepdims=True))
        total = jnp.sum(e, axis=-1, keepdims=True)
        p = jnp.concatenate([(e[h] * keep[h]).astype(BF) for h in range(4)], axis=0)
        o = jnp.dot(p, value[...], preferred_element_type=F32).reshape(4, BLOCK, HEAD)
        o = (o / (total * 0.9)).astype(BF)
        for h in range(4):
            heads[b * BLOCK : (b + 1) * BLOCK, h * HEAD : (h + 1) * HEAD] = o[h]
    x = heads[...]
    piece = 512
    for c in range(WIDTH // piece):
        cols = slice(c * piece, (c + 1) * piece)
        w = jnp.concatenate([wo[:, cols], wp_got[:, cols], wp_other[:, cols]], axis=0)
        t = jnp.dot(x, w, preferred_element_type=F32).astype(BF)
        half = c // (COLS // piece)
        at = slice(c * piece - half * COLS, (c + 1) * piece - half * COLS)
        for b in range(nb):
            outs[half * nb + b][:, at] = t[b * BLOCK : (b + 1) * BLOCK]


def attend(slots, after, meta, q, *rest):
    nb = len(slots)
    out_shape = [jax.ShapeDtypeStruct((BLOCK, COLS), BF)] * (2 * nb)
    vmem = pl.BlockSpec(memory_space=pltpu.VMEM)
    return pl.pallas_call(
        functools.partial(attend_kernel, slots, len(after)),
        in_specs=[pl.BlockSpec(memory_space=pltpu.SMEM), vmem]
        + [vmem] * 8
        + [pl.BlockSpec(memory_space=pl.ANY)] * len(after),
        out_specs=[vmem] * len(out_shape),
        out_shape=out_shape,
        scratch_shapes=[
            pltpu.VMEM((nb * BLOCK, 512), BF),
            pltpu.VMEM((1024, HEAD), BF),
            pltpu.VMEM((1024, HEAD), BF),
        ],
        compiler_params=pltpu.CompilerParams(vmem_limit_bytes=32 << 20),
        cost_estimate=TINY,
        name="attend",
    )(meta, q, *rest, *after)


def pick_kernel(meta, wq, kt, vt, out):
    half = WIDTH // 2
    out[0:half] = wq[...]
    for i in range(half // 256):
        at = slice(i * 256, (i + 1) * 256)
        row = half + i * 128
        out[row : row + 64] = kt[:, at]
        out[row + 64 : row + 128] = vt[:, at]


def pick(meta, wq, kt, vt):
    half = WIDTH // 2
    return pl.pallas_call(
        pick_kernel,
        grid_spec=pltpu.PrefetchScalarGridSpec(
            num_scalar_prefetch=1,
            grid=(1,),
            in_specs=[
                pl.BlockSpec((half, 256), lambda i, m: (m[0], 0)),
                pl.BlockSpec((64, half), lambda i, m: (0, m[0])),
                pl.BlockSpec((64, half), lambda i, m: (0, m[0])),
            ],
            out_specs=pl.BlockSpec((half + half // 2, 256), lambda i, m: (0, 0)),
        ),
        out_shape=jax.ShapeDtypeStruct((half + half // 2, 256), BF),
        compiler_params=pltpu.CompilerParams(vmem_limit_bytes=56 << 20),
        cost_estimate=TINY,
        name="pick",
    )(meta, wq, kt, vt)


def gate_kernel(*refs):
    pass


def gate(arrays, after):
    n = len(arrays)
    anywhere = pl.BlockSpec(memory_space=pl.ANY)
    return pl.pallas_call(
        gate_kernel,
        in_specs=[anywhere] * (n + len(after)),
        out_specs=[anywhere] * n,
        out_shape=[jax.ShapeDtypeStruct(a.shape, a.dtype) for a in arrays],
        input_output_aliases={i: i for i in range(n)},
        cost_estimate=TINY,
        name="gate",
    )(*arrays, *after)


def from_x(array):
    return lax.ppermute(array, ("xl", "xh"), [(i, 3 - i) for i in range(4)])


def from_core(array):
    return lax.ppermute(array, "c", [(0, 1), (1, 0)])


def pair(array):
    return lax.ppermute(array, "xh", [(0, 1), (1, 0)])


def add(a, b):
    return (a.astype(F32) + b.astype(F32)).astype(BF)


def on_device(
    layer_input, norm_gain, query_weight, key_weight, value_matrix, output_weight, keep_bits
):
    core = lax.axis_index("c")
    z = lax.axis_index("z")
    xh = lax.axis_index("xh")

    pieces = [layer_input]
    places = [(0, BLOCK)]
    r = layer_input
    l = layer_input
    for s in range(3):
        r = lax.ppermute(r, "z", RIGHT)
        l = lax.ppermute(l, "z", LEFT)
        pieces += [r, l]
        at = BLOCK * (1 + 2 * s)
        places += [(at, BLOCK), (at + BLOCK, BLOCK)]
        if s == 1:
            step_two = [r, l]
    step_three = [r, l]
    last = [lax.ppermute(r[:HALF], "z", RIGHT), lax.ppermute(l[HALF:], "z", LEFT)]
    last_places = [(0, HALF), (HALF, HALF)]

    meta = jnp.stack([core, z, xh]).astype(jnp.int32)
    kt = key_weight.T
    vt = value_matrix.T
    got = from_x(pick(meta, query_weight, kt, vt))
    (got,) = gate([got], step_three)
    other = from_core(got)
    wo_mine = lax.dynamic_slice_in_dim(output_weight, core * HEAD, HEAD, 0)
    (wo_mine,) = gate([wo_mine], [step_two[0]])
    wo_got = from_x(wo_mine)

    bits = keep_bits.astype(BF).transpose(1, 0, 2).reshape(16, 32)
    bits = jnp.pad(bits, ((0, 0), (0, HEAD - 32)))

    gain = norm_gain[None, :]
    kv_near = project(False, [], meta, pieces, places, range(7), gain, (kt, vt), got, other)
    their_near = pair(jnp.concatenate([kv_near.reshape(896, HEAD), bits]))
    kv_far = project(False, [kv_near], meta, last, last_places, [7], gain, (kt, vt), got, other)
    their_far = pair(kv_far)
    everything = places + [(448 + start, count) for start, count in last_places]
    q = project(
        True, [kv_far], meta, pieces + last, everything, range(8), gain, (query_weight,), got, other
    )
    (wo_got,) = gate([wo_got], [q])
    wo_other = from_core(wo_got)
    shared = (bits, kv_near, kv_far, their_near, their_far, output_weight, wo_got, wo_other)

    near = {}

    def compute(slots, after):
        got = attend(slots, after, meta, q, *shared)
        for i, slot in enumerate(slots):
            near[(NEAR + [4])[slot]] = (got[i], got[len(slots) + i])
        return got

    block = lambda d, c: near[d][c]
    done = compute([7, 5, 6], [])
    compute([3, 4, 0, 1, 2], [done[0]])
    far = near[4]
    r = [lax.ppermute(far[0], "z", RIGHT), None]
    l = [None, lax.ppermute(far[1], "z", LEFT)]
    r = [add(r[0], block(3, 0)), block(3, 1)]
    l = [block(-3, 0), add(l[1], block(-3, 1))]
    for d in (2, 1):
        for c in range(2):
            r[c] = add(lax.ppermute(r[c], "z", RIGHT), block(d, c))
            l[c] = add(lax.ppermute(l[c], "z", LEFT), block(-d, c))
    total = []
    for c in range(2):
        right = lax.ppermute(r[c], "z", RIGHT)
        left = lax.ppermute(l[c], "z", LEFT)
        total.append(block(0, c).astype(F32) + right.astype(F32) + left.astype(F32))
    total = jnp.concatenate(total, axis=1)
    return (layer_input.astype(F32) + total).astype(BF)


def solution(mesh):
    split = Mesh(mesh.devices.reshape(2, 4, 2, Z, 2), ("xl", "y", "c", "z", "xh"))
    every = ("xl", "y", "c", "z", "xh")
    tensor = ("z", "xh")
    return jax.shard_map(
        on_device,
        mesh=split,
        in_specs=(
            P(every, None),
            P(),
            P(None, tensor),
            P(None, tensor),
            P(None, tensor),
            P(tensor, None),
            P(every, None, None),
        ),
        out_specs=P(every, None),
        check_vma=False,
    )
```

time: 327 us -> 141 us (0.43)
  waiting for transfers between devices: 238 us -> 53 us
  starting transfers between devices: 2.43 us -> 44.9 us
  matrix products: 31.5 us -> 0 us
  Pallas kernels: 0 us -> 30.9 us
  local copies, waits for them, and re-layouts: 23.1 us -> 7.74 us
  between operations: 13.3 us -> 0.39 us
  other arithmetic: 15 us -> 2.3 us
    reduce_scatter x2 -> x0, waiting for transfers between devices: 120 us -> none  [sum_by_axis(): array = lax.psum_scatter(array, axis, scatter_dimension=dim, tiled=True)]
    all_gather x1 -> x0, waiting for transfers between devices: 113 us -> none  [on_device(): piece = lax.all_gather(normed, TENSOR, axis=0, tiled=True)]
    ppermute x1 -> x28, waiting for transfers between devices: 5.64 us -> 53 us  [the longest x3 29.3 us: on_device(): r = lax.ppermute(r, 'z', RIGHT)]
    ppermute x1 -> x28, starting transfers between devices: 2.35 us -> 44.9 us  [the longest x4 13.4 us: on_device(): l[c] = add(lax.ppermute(l[c], 'z', LEFT), block(-d, c))]
    dot_general x6 -> x0, matrix products: 31.5 us -> none  [the longest x2 9.62 us: attend(): jnp.einsum('hqk,hkd->hqd', dropped, value_rows[:, :last_row], preferred_e...]
    pallas_call x0 -> x9, Pallas kernels: none -> 30.9 us  [the longest x3 17.5 us: project(): pl.pallas_call(functools.partial(q_kernel if queries else kv_kernel, plac...]
    reshape x3 -> x1, local copies, waits for them, and re-layouts: 14.1 us -> 0.09 us  [on_device(): bits = keep_bits.astype(BF).transpose(1, 0, 2).reshape(16, 32)]
    broadcast_in_dim x3 -> x0, local copies, waits for them, and re-layouts: 6.95 us -> none  [the longest x2 6.12 us: attend(): jnp.broadcast_to(chosen_bits[:, :, None, :, None], (heads, height // BLOC...]
  transfers between devices with their start and end apart: 4 -> 28, of which waited for: 4 -> 13; matrix products, arithmetic and copies ran while one was open for 8% -> 3% of each run, Pallas kernels for 0% -> 19%
where the time goes in v1:
time: 141 us; the launch traced here: 139 us
  waiting for transfers between devices  53 us (38%)
  starting transfers between devices  44.9 us (32%)
  Pallas kernels  30.9 us (22%)
  local copies, waits for them, and re-layouts  7.74 us (5%)
  other arithmetic  2.3 us (2%)
    ppermute x3, waiting for transfers between devices, on_device(): r = lax.ppermute(r, 'z', RIGHT)  29.3 us
    pallas_call x3, Pallas kernels, project(): pl.pallas_call(functools.partial(q_kernel if queries else kv_kernel, plac...  17.5 us
    ppermute x4, starting transfers between devices, on_device(): l[c] = add(lax.ppermute(l[c], 'z', LEFT), block(-d, c))  13.4 us
    ppermute x3, starting transfers between devices, on_device(): l = lax.ppermute(l, 'z', LEFT)  10.5 us
    pallas_call x2, Pallas kernels, attend(): pl.pallas_call(functools.partial(attend_kernel, slots, len(after)), in_sp...  10 us
    ppermute x4, waiting for transfers between devices, on_device(): r[c] = add(lax.ppermute(r[c], 'z', RIGHT), block(d, c))  7.24 us
    ppermute x2, starting transfers between devices, on_device(): left = lax.ppermute(l[c], 'z', LEFT)  7.18 us
    ppermute x2, waiting for transfers between devices, pair(): return lax.ppermute(array, 'xh', [(0, 1), (1, 0)])  6.77 us
  transfers between devices with their start and end apart: 28, of which 13 were waited for; matrix products, arithmetic and copies ran while one was open for 3% of the time, Pallas kernels for 19%

profile of v1, /device:TPU:6, one launch (start us, length us, event | category | flops | bytes accessed | tf_op | source)
XLA Modules:
  0.0 139.2 jit_solution(7153965710597221853)
XLA Ops:
  0.0 1.9 %collective-permute-start = (bf16[64,4096]{1,0:T(8,128)(2,1)}, bf16[64,4096]{1,0:T(8,128)(2,1)S(1)}, u32[]{:S(2)}, u32[]{:S(2)}) collective-permute-start(bf16[64,4096]{1,0:T(8,128)(2,1)} %refs_0_.5), channel_id=1, source_target_pairs={{0,2},{2,4},{4,6},{6,8},{8,10},{10,12},{12,14},{14,0},{1,3},{3,5},... | collective-permute-start | bytes 1572872 | tf_op jit(solution)/shard_map/ppermute | solution.py:348
  1.9 3.9 %collective-permute-start.1 = (bf16[64,4096]{1,0:T(8,128)(2,1)}, bf16[64,4096]{1,0:T(8,128)(2,1)S(1)}, u32[]{:S(2)}, u32[]{:S(2)}) collective-permute-start(bf16[64,4096]{1,0:T(8,128)(2,1)} %refs_0_.5), channel_id=1, source_target_pairs={{0,14},{2,0},{4,2},{6,4},{8,6},{10,8},{12,10},{14,12},{1,15},{3,1}... | collective-permute-start | bytes 1572872 | tf_op jit(solution)/shard_map/ppermute | solution.py:349
  5.9 0.6 pad_add_fusion.meta
  6.4 3.3 %pick.1 = bf16[3072,256]{1,0:T(8,128)(2,1)} custom-call(s32[3]{0:T(128)} %pad_add_fusion.meta, bf16[4096,256]{1,0:T(8,128)(2,1)} %refs_10_.1, bf16[64,4096]{1,0:T(8,128)(2,1)} %bitcast.10, bf16[64,4096]{1,0:T(8,128)(2,1)} %bitcast.13), custom_call_target="tpu_custom_call" | custom-call | flops 1000 | bytes 1000 | tf_op jit(solution)/shard_map/pick/pallas_call | solution.py:283
  9.7 0.5 collective-permute-start.8
  10.2 7.8 %collective-permute-done.refs_1_ = bf16[64,4096]{1,0:T(8,128)(2,1)S(1)} collective-permute-done((bf16[64,4096]{1,0:T(8,128)(2,1)}, bf16[64,4096]{1,0:T(8,128)(2,1)S(1)}, u32[]{:S(2)}, u32[]{:S(2)}) %collective-permute-start) | collective-permute-done | bytes 524320 | tf_op jit(solution)/shard_map/ppermute | solution.py:348
  18.0 3.2 %collective-permute-start.3 = (bf16[64,4096]{1,0:T(8,128)(2,1)S(1)}, bf16[64,4096]{1,0:T(8,128)(2,1)S(1)}, u32[]{:S(2)}, u32[]{:S(2)}) collective-permute-start(bf16[64,4096]{1,0:T(8,128)(2,1)S(1)} %collective-permute-done.1.refs_2_), channel_id=1, source_target_pairs={{0,14},{2,0},{4,2},{6,4},{8,6},{10,8},{12,10},{14,12},{1,15},{3,1}... | collective-permute-start | bytes 1572872 | tf_op jit(solution)/shard_map/ppermute | solution.py:349
  21.2 11.2 %collective-permute-done.2.refs_3_.refs_1_ = bf16[64,4096]{1,0:T(8,128)(2,1)S(1)} collective-permute-done((bf16[64,4096]{1,0:T(8,128)(2,1)S(1)}, bf16[64,4096]{1,0:T(8,128)(2,1)S(1)}, u32[]{:S(2)}, u32[]{:S(2)}) %collective-permute-start.2) | collective-permute-done | bytes 524320 | tf_op jit(solution)/shard_map/ppermute | solution.py:348
  32.4 3.3 %collective-permute-start.5 = (bf16[64,4096]{1,0:T(8,128)(2,1)S(1)}, bf16[64,4096]{1,0:T(8,128)(2,1)S(1)}, u32[]{:S(2)}, u32[]{:S(2)}) collective-permute-start(bf16[64,4096]{1,0:T(8,128)(2,1)S(1)} %collective-permute-done.3.refs_4_), channel_id=1, source_target_pairs={{0,14},{2,0},{4,2},{6,4},{8,6},{10,8},{12,10},{14,12},{1,15},{3,1}... | collective-permute-start | bytes 1572872 | tf_op jit(solution)/shard_map/ppermute | solution.py:349
  35.7 10.3 %collective-permute-done.4.refs_1_.refs_5_ = bf16[64,4096]{1,0:T(8,128)(2,1)S(1)} collective-permute-done((bf16[64,4096]{1,0:T(8,128)(2,1)S(1)}, bf16[64,4096]{1,0:T(8,128)(2,1)S(1)}, u32[]{:S(2)}, u32[]{:S(2)}) %collective-permute-start.4) | collective-permute-done | bytes 524320 | tf_op jit(solution)/shard_map/ppermute | solution.py:348
  46.1 1.0 collective-permute-done.8.refs_0_
  47.1 1.1 constant_dynamic-slice_fusion.refs_0_
  48.2 0.5 collective-permute-start.12
  48.7 1.0 slice.8
  49.7 1.0 slice.9
  50.7 3.3 %collective-permute-start.7 = (bf16[32,4096]{1,0:T(8,128)(2,1)S(1)}, bf16[32,4096]{1,0:T(8,128)(2,1)S(1)}, u32[]{:S(2)}, u32[]{:S(2)}) collective-permute-start(bf16[32,4096]{1,0:T(8,128)(2,1)S(1)} %slice.9), channel_id=1, source_target_pairs={{0,14},{2,0},{4,2},{6,4},{8,6},{10,8},{12,10},{14,12},{1,15},{3,1}... | collective-permute-start | bytes 786440 | tf_op jit(solution)/shard_map/ppermute | solution.py:356
  54.0 5.5 %keys.2.refs_9_.kv_near = bf16[2,448,128]{2,1,0:T(8,128)(2,1)} custom-call(s32[3]{0:T(128)} %pad_add_fusion.meta, bf16[64,4096]{1,0:T(8,128)(2,1)} %refs_0_.5, bf16[64,4096]{1,0:T(8,128)(2,1)} %copy-done.11, bf16[64,4096]{1,0:T(8,128)(2,1)} %copy-done.12, bf16[64,4096]{1,0:T(8,128)(2,1)} %copy-done.9, bf16[64,4096]{1,0:T(8,128)(2,1)} %copy-done.13, ...), custom_call_target="tpu_custom_call" | custom-call | flops 1000 | bytes 1000 | tf_op jit(solution)/shard_map/keys/pallas_call | solution.py:173
  59.5 0.1 collective-permute-done.7.refs_1_.refs_8_
  59.7 0.6 copy-done.14
  60.3 0.7 copy-done.15
  61.0 4.1 %keys.3.refs_15_.kv_far = bf16[2,64,128]{2,1,0:T(8,128)(2,1)} custom-call(s32[3]{0:T(128)} %pad_add_fusion.meta, bf16[32,4096]{1,0:T(8,128)(2,1)} %copy-done.14, bf16[32,4096]{1,0:T(8,128)(2,1)} %copy-done.15, f32[1,4096]{1,0:T(1,128)} %bitcast.17, bf16[64,4096]{1,0:T(8,128)(2,1)} %bitcast.12, bf16[64,4096]{1,0:T(8,128)(2,1)} %bitcast.15, ...), custom_call_target="tpu_custom_call" | custom-call | flops 1000 | bytes 1000 | tf_op jit(solution)/shard_map/keys/pallas_call | solution.py:173
  65.1 7.9 %queries.1.refs_1_.q = bf16[8,4,64,128]{3,2,1,0:T(8,128)(2,1)} custom-call(s32[3]{0:T(128)} %pad_add_fusion.meta, bf16[64,4096]{1,0:T(8,128)(2,1)} %refs_0_.5, bf16[64,4096]{1,0:T(8,128)(2,1)} %copy-done.11, bf16[64,4096]{1,0:T(8,128)(2,1)} %copy-done.12, bf16[64,4096]{1,0:T(8,128)(2,1)} %copy-done.9, bf16[64,4096]{1,0:T(8,128)(2,1)} %copy-done.13, ...), custom_call_target="tpu_custom_call" | custom-call | flops 1000 | bytes 1000 | tf_op jit(solution)/shard_map/queries/pallas_call | solution.py:173
  73.0 2.1 %collective-permute-done.12.refs_0_ = bf16[128,4096]{1,0:T(8,128)(2,1)S(1)} collective-permute-done((bf16[128,4096]{1,0:T(8,128)(2,1)}, bf16[128,4096]{1,0:T(8,128)(2,1)S(1)}, u32[]{:S(2)}, u32[]{:S(2)}) %collective-permute-start.12) | collective-permute-done | bytes 1048608 | tf_op jit(solution)/shard_map/ppermute | solution.py:321
  75.2 1.0 copy-done.1
  76.2 0.1 reshape.6
  76.3 0.3 collective-permute-start.10
  76.6 3.5 %collective-permute-start.11 = (bf16[2,64,128]{2,1,0:T(8,128)(2,1)S(1)}, bf16[2,64,128]{2,1,0:T(8,128)(2,1)S(1)}, u32[]{:S(2)}, u32[]{:S(2)}) collective-permute-start(bf16[2,64,128]{2,1,0:T(8,128)(2,1)S(1)} %copy-done.5), channel_id=1, source_target_pairs={{0,1},{1,0},{2,3},{3,2},{4,5},{5,4},{6,7},{7,6},{8,9},{9,8},{10,11... | collective-permute-start | bytes 98312 | tf_op jit(solution)/shard_map/ppermute | solution.py:329
  80.1 6.8 %collective-permute-done.11.their_far = bf16[2,64,128]{2,1,0:T(8,128)(2,1)S(1)} collective-permute-done((bf16[2,64,128]{2,1,0:T(8,128)(2,1)S(1)}, bf16[2,64,128]{2,1,0:T(8,128)(2,1)S(1)}, u32[]{:S(2)}, u32[]{:S(2)}) %collective-permute-start.11) | collective-permute-done | bytes 32800 | tf_op jit(solution)/shard_map/ppermute | solution.py:329
  86.9 1.2 copy-done.2
  88.1 1.0 copy-done.3
  89.2 4.0 %attend.2 = (bf16[64,2048]{1,0:T(8,128)(2,1)S(1)}, bf16[64,2048]{1,0:T(8,128)(2,1)S(1)}, bf16[64,2048]{1,0:T(8,128)(2,1)S(1)}, bf16[64,2048]{1,0:T(8,128)(2,1)S(...) custom-call(s32[3]{0:T(128)S(1)} %copy-done.6, bf16[8,4,64,128]{3,2,1,0:T(8,128)(2,1)S(1)} %copy-done.3, ...), custom_call_target="tpu_custom_call" | custom-call | flops 1000 | bytes 1000 | tf_op jit(solution)/shard_map/attend/pallas_call | solution.py:253
  93.3 3.2 %collective-permute-start.18 = (bf16[64,2048]{1,0:T(8,128)(2,1)S(1)}, bf16[64,2048]{1,0:T(8,128)(2,1)S(1)}, u32[]{:S(2)}, u32[]{:S(2)}) collective-permute-start(bf16[64,2048]{1,0:T(8,128)(2,1)S(1)} %get-tuple-element.26), channel_id=1, source_target_pairs={{0,14},{2,0},{4,2},{6,4},{8,6},{10,8},{12,10},{14,12},{1,15},{3,1}... | collective-permute-start | bytes 786440 | tf_op jit(solution)/shard_map/ppermute | solution.py:404
  96.5 3.2 %collective-permute-start.24 = (bf16[64,2048]{1,0:T(8,128)(2,1)S(1)}, bf16[64,2048]{1,0:T(8,128)(2,1)S(1)}, u32[]{:S(2)}, u32[]{:S(2)}) collective-permute-start(bf16[64,2048]{1,0:T(8,128)(2,1)S(1)} %get-tuple-element.33), channel_id=1, source_target_pairs={{0,14},{2,0},{4,2},{6,4},{8,6},{10,8},{12,10},{14,12},{1,15},{3,1}... | collective-permute-start | bytes 786440 | tf_op jit(solution)/shard_map/ppermute | solution.py:398
  99.7 6.0 %attend.3 = (bf16[64,2048]{1,0:T(8,128)(2,1)S(1)}, bf16[64,2048]{1,0:T(8,128)(2,1)S(1)}, bf16[64,2048]{1,0:T(8,128)(2,1)S(1)}, bf16[64,2048]{1,0:T(8,128)(2,1)S(...) custom-call(s32[3]{0:T(128)S(1)} %copy-done.6, ...), custom_call_target="tpu_custom_call" | custom-call | flops 1000 | bytes 1000 | tf_op jit(solution)/shard_map/attend/pallas_call | solution.py:253
  106.0 3.5 %collective-permute-start.19 = (bf16[64,2048]{1,0:T(8,128)(2,1)S(1)}, bf16[64,2048]{1,0:T(8,128)(2,1)S(1)}, u32[]{:S(2)}, u32[]{:S(2)}) collective-permute-start(bf16[64,2048]{1,0:T(8,128)(2,1)S(1)} %add_convert_fusion.6), channel_id=1, source_target_pairs={{0,14},{2,0},{4,2},{6,4},{8,6},{10,8},{12,10},{14,12},{1,15},{3,1}... | collective-permute-start | bytes 786440 | tf_op jit(solution)/shard_map/ppermute | solution.py:404
  109.8 3.3 %collective-permute-start.25 = (bf16[64,2048]{1,0:T(8,128)(2,1)S(1)}, bf16[64,2048]{1,0:T(8,128)(2,1)S(1)}, u32[]{:S(2)}, u32[]{:S(2)}) collective-permute-start(bf16[64,2048]{1,0:T(8,128)(2,1)S(1)} %add_convert_fusion.2), channel_id=1, source_target_pairs={{0,14},{2,0},{4,2},{6,4},{8,6},{10,8},{12,10},{14,12},{1,15},{3,1}... | collective-permute-start | bytes 786440 | tf_op jit(solution)/shard_map/ppermute | solution.py:404
  113.1 3.3 %collective-permute-done.15 = bf16[64,2048]{1,0:T(8,128)(2,1)S(1)} collective-permute-done((bf16[64,2048]{1,0:T(8,128)(2,1)S(1)}, bf16[64,2048]{1,0:T(8,128)(2,1)S(1)}, u32[]{:S(2)}, u32[]{:S(2)}) %collective-permute-start.15) | collective-permute-done | bytes 262176 | tf_op jit(solution)/shard_map/ppermute | solution.py:403
  116.6 3.4 %collective-permute-start.20 = (bf16[64,2048]{1,0:T(8,128)(2,1)S(1)}, bf16[64,2048]{1,0:T(8,128)(2,1)S(1)}, u32[]{:S(2)}, u32[]{:S(2)}) collective-permute-start(bf16[64,2048]{1,0:T(8,128)(2,1)S(1)} %add_convert_fusion.5), channel_id=1, source_target_pairs={{0,14},{2,0},{4,2},{6,4},{8,6},{10,8},{12,10},{14,12},{1,15},{3,1}... | collective-permute-start | bytes 786440 | tf_op jit(solution)/shard_map/ppermute | solution.py:408
  120.1 2.0 %collective-permute-done.22 = bf16[64,2048]{1,0:T(8,128)(2,1)S(1)} collective-permute-done((bf16[64,2048]{1,0:T(8,128)(2,1)S(1)}, bf16[64,2048]{1,0:T(8,128)(2,1)S(1)}, u32[]{:S(2)}, u32[]{:S(2)}) %collective-permute-start.22) | collective-permute-done | bytes 262176 | tf_op jit(solution)/shard_map/ppermute | solution.py:403
  122.3 3.4 %collective-permute-start.26 = (bf16[64,2048]{1,0:T(8,128)(2,1)S(1)}, bf16[64,2048]{1,0:T(8,128)(2,1)S(1)}, u32[]{:S(2)}, u32[]{:S(2)}) collective-permute-start(bf16[64,2048]{1,0:T(8,128)(2,1)S(1)} %add_convert_fusion.1), channel_id=1, source_target_pairs={{0,14},{2,0},{4,2},{6,4},{8,6},{10,8},{12,10},{14,12},{1,15},{3,1}... | collective-permute-start | bytes 786440 | tf_op jit(solution)/shard_map/ppermute | solution.py:404
  125.7 2.0 %collective-permute-done.16 = bf16[64,2048]{1,0:T(8,128)(2,1)S(1)} collective-permute-done((bf16[64,2048]{1,0:T(8,128)(2,1)S(1)}, bf16[64,2048]{1,0:T(8,128)(2,1)S(1)}, u32[]{:S(2)}, u32[]{:S(2)}) %collective-permute-start.16) | collective-permute-done | bytes 262176 | tf_op jit(solution)/shard_map/ppermute | solution.py:403
  127.8 2.6 %collective-permute-done.26 = bf16[64,2048]{1,0:T(8,128)(2,1)S(1)} collective-permute-done((bf16[64,2048]{1,0:T(8,128)(2,1)S(1)}, bf16[64,2048]{1,0:T(8,128)(2,1)S(1)}, u32[]{:S(2)}, u32[]{:S(2)}) %collective-permute-start.26) | collective-permute-done | bytes 262176 | tf_op jit(solution)/shard_map/ppermute | solution.py:404
  130.5 3.8 %collective-permute-start.27 = (bf16[64,2048]{1,0:T(8,128)(2,1)S(1)}, bf16[64,2048]{1,0:T(8,128)(2,1)S(1)}, u32[]{:S(2)}, u32[]{:S(2)}) collective-permute-start(bf16[64,2048]{1,0:T(8,128)(2,1)S(1)} %add_convert_fusion), channel_id=1, source_target_pairs={{0,14},{2,0},{4,2},{6,4},{8,6},{10,8},{12,10},{14,12},{1,15},{3,1}... | collective-permute-start | bytes 786440 | tf_op jit(solution)/shard_map/ppermute | solution.py:408
  134.3 2.1 %collective-permute-done.17 = bf16[64,2048]{1,0:T(8,128)(2,1)S(1)} collective-permute-done((bf16[64,2048]{1,0:T(8,128)(2,1)S(1)}, bf16[64,2048]{1,0:T(8,128)(2,1)S(1)}, u32[]{:S(2)}, u32[]{:S(2)}) %collective-permute-start.17) | collective-permute-done | bytes 262176 | tf_op jit(solution)/shard_map/ppermute | solution.py:407
  136.4 0.1 convert_add_fusion.1
  136.5 1.6 %collective-permute-done.27 = bf16[64,2048]{1,0:T(8,128)(2,1)S(1)} collective-permute-done((bf16[64,2048]{1,0:T(8,128)(2,1)S(1)}, bf16[64,2048]{1,0:T(8,128)(2,1)S(1)}, u32[]{:S(2)}, u32[]{:S(2)}) %collective-permute-start.27) | collective-permute-done | bytes 262176 | tf_op jit(solution)/shard_map/ppermute | solution.py:408
  138.2 0.1 convert_add_fusion
  138.3 0.9 fusion
  (73 shorter events, 1.4 us)
Async XLA Ops:
  0.0 18.0 %collective-permute-start = (bf16[64,4096]{1,0:T(8,128)(2,1)}, bf16[64,4096]{1,0:T(8,128)(2,1)S(1)}, u32[]{:S(2)}, u32[]{:S(2)}) collective-permute-start(bf16[64,4096]{1,0:T(8,128)(2,1)} %refs_0_.5), channel_id=1, source_target_pairs={{0,2},{2,4},{4,6},{6,8},{8,10},{10,12},{12,14},{14,0},{1,3},{3,5},... | collective-permute-start | bytes 1572872 | tf_op jit(solution)/shard_map/ppermute | solution.py:348
  1.9 16.1 %collective-permute-start.1 = (bf16[64,4096]{1,0:T(8,128)(2,1)}, bf16[64,4096]{1,0:T(8,128)(2,1)S(1)}, u32[]{:S(2)}, u32[]{:S(2)}) collective-permute-start(bf16[64,4096]{1,0:T(8,128)(2,1)} %refs_0_.5), channel_id=1, source_target_pairs={{0,14},{2,0},{4,2},{6,4},{8,6},{10,8},{12,10},{14,12},{1,15},{3,1}... | collective-permute-start | bytes 1572872 | tf_op jit(solution)/shard_map/ppermute | solution.py:349
  9.7 37.4 %copy-start = (bf16[256,4096]{1,0:T(8,128)(2,1)S(1)}, bf16[256,4096]{1,0:T(8,128)(2,1)}, u32[]{:S(2)}) copy-start(bf16[256,4096]{1,0:T(8,128)(2,1)} %refs_0_.7) | copy-start | bytes 6291460
  9.7 37.4 %collective-permute-start.8 = (bf16[3072,256]{1,0:T(8,128)(2,1)}, bf16[3072,256]{1,0:T(8,128)(2,1)}, u32[]{:S(2)}, u32[]{:S(2)}) collective-permute-start(bf16[3072,256]{1,0:T(8,128)(2,1)} %pick.1), channel_id=1, source_target_pairs={{0,129},{1,128},{128,1},{129,0},{2,131},{3,130},{130,3},{131,2},{4... | collective-permute-start | bytes 4718600 | tf_op jit(solution)/shard_map/ppermute | solution.py:321
  18.0 3.2 %copy-start.11 = (bf16[64,4096]{1,0:T(8,128)(2,1)}, bf16[64,4096]{1,0:T(8,128)(2,1)S(1)}, u32[]{:S(2)}) copy-start(bf16[64,4096]{1,0:T(8,128)(2,1)S(1)} %collective-permute-done.refs_1_) | copy-start | bytes 1572868
  18.0 14.4 %collective-permute-start.2 = (bf16[64,4096]{1,0:T(8,128)(2,1)S(1)}, bf16[64,4096]{1,0:T(8,128)(2,1)S(1)}, u32[]{:S(2)}, u32[]{:S(2)}) collective-permute-start(bf16[64,4096]{1,0:T(8,128)(2,1)S(1)} %collective-permute-done.refs_1_), channel_id=1, source_target_pairs={{0,2},{2,4},{4,6},{6,8},{8,10},{10,12},{12,14},{14,0},{1,3},{3,5},... | collective-permute-start | bytes 1572872 | tf_op jit(solution)/shard_map/ppermute | solution.py:348
  18.0 14.4 %copy-start.12 = (bf16[64,4096]{1,0:T(8,128)(2,1)}, bf16[64,4096]{1,0:T(8,128)(2,1)S(1)}, u32[]{:S(2)}) copy-start(bf16[64,4096]{1,0:T(8,128)(2,1)S(1)} %collective-permute-done.1.refs_2_) | copy-start | bytes 1572868
  18.0 14.4 %collective-permute-start.3 = (bf16[64,4096]{1,0:T(8,128)(2,1)S(1)}, bf16[64,4096]{1,0:T(8,128)(2,1)S(1)}, u32[]{:S(2)}, u32[]{:S(2)}) collective-permute-start(bf16[64,4096]{1,0:T(8,128)(2,1)S(1)} %collective-permute-done.1.refs_2_), channel_id=1, source_target_pairs={{0,14},{2,0},{4,2},{6,4},{8,6},{10,8},{12,10},{14,12},{1,15},{3,1}... | collective-permute-start | bytes 1572872 | tf_op jit(solution)/shard_map/ppermute | solution.py:349
  32.4 13.6 %copy-start.9 = (bf16[64,4096]{1,0:T(8,128)(2,1)}, bf16[64,4096]{1,0:T(8,128)(2,1)S(1)}, u32[]{:S(2)}) copy-start(bf16[64,4096]{1,0:T(8,128)(2,1)S(1)} %collective-permute-done.2.refs_3_.refs_1_) | copy-start | bytes 1572868
  32.4 13.6 %collective-permute-start.4 = (bf16[64,4096]{1,0:T(8,128)(2,1)S(1)}, bf16[64,4096]{1,0:T(8,128)(2,1)S(1)}, u32[]{:S(2)}, u32[]{:S(2)}) collective-permute-start(bf16[64,4096]{1,0:T(8,128)(2,1)S(1)} %collective-permute-done.2.refs_3_.refs_1_), channel_id=1, source_target_pairs={{0,2},{2,4},{4,6},{6,8},{8,10},{10,12},{12,14},{14,0},{1,3},{3,5},... | collective-permute-start | bytes 1572872 | tf_op jit(solution)/shard_map/ppermute | solution.py:348
  32.4 13.6 %copy-start.13 = (bf16[64,4096]{1,0:T(8,128)(2,1)}, bf16[64,4096]{1,0:T(8,128)(2,1)S(1)}, u32[]{:S(2)}) copy-start(bf16[64,4096]{1,0:T(8,128)(2,1)S(1)} %collective-permute-done.3.refs_4_) | copy-start | bytes 1572868
  32.4 13.6 %collective-permute-start.5 = (bf16[64,4096]{1,0:T(8,128)(2,1)S(1)}, bf16[64,4096]{1,0:T(8,128)(2,1)S(1)}, u32[]{:S(2)}, u32[]{:S(2)}) collective-permute-start(bf16[64,4096]{1,0:T(8,128)(2,1)S(1)} %collective-permute-done.3.refs_4_), channel_id=1, source_target_pairs={{0,14},{2,0},{4,2},{6,4},{8,6},{10,8},{12,10},{14,12},{1,15},{3,1}... | collective-permute-start | bytes 1572872 | tf_op jit(solution)/shard_map/ppermute | solution.py:349
  46.0 1.1 copy-start.7
  46.0 1.1 copy-start.8
  47.1 6.9 %collective-permute-start.9 = (bf16[3072,256]{1,0:T(8,128)(2,1)}, bf16[3072,256]{1,0:T(8,128)(2,1)}, u32[]{:S(2)}, u32[]{:S(2)}) collective-permute-start(bf16[3072,256]{1,0:T(8,128)(2,1)} %gate.3.refs_10_.refs_5_.refs_11_), channel_id=1, source_target_pairs={{0,16},{16,0},{1,17},{17,1},{2,18},{18,2},{3,19},{19,3},{4,20},{20... | collective-permute-start | bytes 4718600 | tf_op jit(solution)/shard_map/ppermute | solution.py:325
  48.2 27.0 %collective-permute-start.12 = (bf16[128,4096]{1,0:T(8,128)(2,1)}, bf16[128,4096]{1,0:T(8,128)(2,1)S(1)}, u32[]{:S(2)}, u32[]{:S(2)}) collective-permute-start(bf16[128,4096]{1,0:T(8,128)(2,1)} %gate.4), channel_id=1, source_target_pairs={{0,129},{1,128},{128,1},{129,0},{2,131},{3,130},{130,3},{131,2},{4... | collective-permute-start | bytes 3145736 | tf_op jit(solution)/shard_map/ppermute | solution.py:321
  49.6 9.9 %collective-permute-start.6 = (bf16[32,4096]{1,0:T(8,128)(2,1)S(1)}, bf16[32,4096]{1,0:T(8,128)(2,1)S(1)}, u32[]{:S(2)}, u32[]{:S(2)}) collective-permute-start(bf16[32,4096]{1,0:T(8,128)(2,1)S(1)} %slice.8), channel_id=1, source_target_pairs={{0,2},{2,4},{4,6},{6,8},{8,10},{10,12},{12,14},{14,0},{1,3},{3,5},... | collective-permute-start | bytes 786440 | tf_op jit(solution)/shard_map/ppermute | solution.py:356
  50.7 9.0 %collective-permute-start.7 = (bf16[32,4096]{1,0:T(8,128)(2,1)S(1)}, bf16[32,4096]{1,0:T(8,128)(2,1)S(1)}, u32[]{:S(2)}, u32[]{:S(2)}) collective-permute-start(bf16[32,4096]{1,0:T(8,128)(2,1)S(1)} %slice.9), channel_id=1, source_target_pairs={{0,14},{2,0},{4,2},{6,4},{8,6},{10,8},{12,10},{14,12},{1,15},{3,1}... | collective-permute-start | bytes 786440 | tf_op jit(solution)/shard_map/ppermute | solution.py:356
  59.5 0.7 copy-start.14
  60.3 0.7 copy-start.15
  73.0 3.2 %copy-start.16 = (s32[2,16,16]{2,1,0:T(8,128)S(1)}, s32[2,16,16]{2,1,0:T(8,128)}, u32[]{:S(2)}) copy-start(s32[2,16,16]{2,1,0:T(8,128)} %param.19) | copy-start | bytes 6148
  73.0 3.3 %copy-start.4 = (bf16[2,448,128]{2,1,0:T(8,128)(2,1)S(1)}, bf16[2,448,128]{2,1,0:T(8,128)(2,1)}, u32[]{:S(2)}) copy-start(bf16[2,448,128]{2,1,0:T(8,128)(2,1)} %keys.2.refs_9_.kv_near) | copy-start | bytes 688132
  73.0 3.6 %copy-start.5 = (bf16[2,64,128]{2,1,0:T(8,128)(2,1)S(1)}, bf16[2,64,128]{2,1,0:T(8,128)(2,1)}, u32[]{:S(2)}) copy-start(bf16[2,64,128]{2,1,0:T(8,128)(2,1)} %keys.3.refs_15_.kv_far) | copy-start | bytes 98308
  73.0 13.9 %copy-start.6 = (s32[3]{0:T(128)S(1)}, s32[3]{0:T(128)}, u32[]{:S(2)}) copy-start(s32[3]{0:T(128)} %pad_add_fusion.meta) | copy-start | bytes 40
  75.2 1.0 copy-start.1
  76.2 10.7 %collective-permute-start.13 = (bf16[128,4096]{1,0:T(8,128)(2,1)}, bf16[128,4096]{1,0:T(8,128)(2,1)S(1)}, u32[]{:S(2)}, u32[]{:S(2)}) collective-permute-start(bf16[128,4096]{1,0:T(8,128)(2,1)} %gate.5.refs_1_), channel_id=1, source_target_pairs={{0,16},{16,0},{1,17},{17,1},{2,18},{18,2},{3,19},{19,3},{4,20},{20... | collective-permute-start | bytes 3145736 | tf_op jit(solution)/shard_map/ppermute | solution.py:325
  76.3 10.6 %collective-permute-start.10 = (bf16[912,128]{1,0:T(8,128)(2,1)S(1)}, bf16[912,128]{1,0:T(8,128)(2,1)S(1)}, u32[]{:S(2)}, u32[]{:S(2)}) collective-permute-start(bf16[912,128]{1,0:T(8,128)(2,1)S(1)} %pad_maximum_fusion), channel_id=1, source_target_pairs={{0,1},{1,0},{2,3},{3,2},{4,5},{5,4},{6,7},{7,6},{8,9},{9,8},{10,11... | collective-permute-start | bytes 700424 | tf_op jit(solution)/shard_map/ppermute | solution.py:329
  76.6 10.3 %collective-permute-start.11 = (bf16[2,64,128]{2,1,0:T(8,128)(2,1)S(1)}, bf16[2,64,128]{2,1,0:T(8,128)(2,1)S(1)}, u32[]{:S(2)}, u32[]{:S(2)}) collective-permute-start(bf16[2,64,128]{2,1,0:T(8,128)(2,1)S(1)} %copy-done.5), channel_id=1, source_target_pairs={{0,1},{1,0},{2,3},{3,2},{4,5},{5,4},{6,7},{7,6},{8,9},{9,8},{10,11... | collective-permute-start | bytes 98312 | tf_op jit(solution)/shard_map/ppermute | solution.py:329
  86.9 1.2 copy-start.2
  88.1 1.0 copy-start.3
  93.2 12.6 %collective-permute-start.14 = (bf16[64,2048]{1,0:T(8,128)(2,1)S(1)}, bf16[64,2048]{1,0:T(8,128)(2,1)S(1)}, u32[]{:S(2)}, u32[]{:S(2)}) collective-permute-start(bf16[64,2048]{1,0:T(8,128)(2,1)S(1)} %get-tuple-element.21.refs_3_), channel_id=1, source_target_pairs={{0,2},{2,4},{4,6},{6,8},{8,10},{10,12},{12,14},{14,0},{1,3},{3,5},... | collective-permute-start | bytes 786440 | tf_op jit(solution)/shard_map/ppermute | solution.py:397
  93.3 12.7 %collective-permute-start.18 = (bf16[64,2048]{1,0:T(8,128)(2,1)S(1)}, bf16[64,2048]{1,0:T(8,128)(2,1)S(1)}, u32[]{:S(2)}, u32[]{:S(2)}) collective-permute-start(bf16[64,2048]{1,0:T(8,128)(2,1)S(1)} %get-tuple-element.26), channel_id=1, source_target_pairs={{0,14},{2,0},{4,2},{6,4},{8,6},{10,8},{12,10},{14,12},{1,15},{3,1}... | collective-permute-start | bytes 786440 | tf_op jit(solution)/shard_map/ppermute | solution.py:404
  96.5 13.0 %collective-permute-start.21 = (bf16[64,2048]{1,0:T(8,128)(2,1)S(1)}, bf16[64,2048]{1,0:T(8,128)(2,1)S(1)}, u32[]{:S(2)}, u32[]{:S(2)}) collective-permute-start(bf16[64,2048]{1,0:T(8,128)(2,1)S(1)} %get-tuple-element.30), channel_id=1, source_target_pairs={{0,2},{2,4},{4,6},{6,8},{8,10},{10,12},{12,14},{14,0},{1,3},{3,5},... | collective-permute-start | bytes 786440 | tf_op jit(solution)/shard_map/ppermute | solution.py:403
  96.5 13.2 %collective-permute-start.24 = (bf16[64,2048]{1,0:T(8,128)(2,1)S(1)}, bf16[64,2048]{1,0:T(8,128)(2,1)S(1)}, u32[]{:S(2)}, u32[]{:S(2)}) collective-permute-start(bf16[64,2048]{1,0:T(8,128)(2,1)S(1)} %get-tuple-element.33), channel_id=1, source_target_pairs={{0,14},{2,0},{4,2},{6,4},{8,6},{10,8},{12,10},{14,12},{1,15},{3,1}... | collective-permute-start | bytes 786440 | tf_op jit(solution)/shard_map/ppermute | solution.py:398
  105.8 10.5 %collective-permute-start.15 = (bf16[64,2048]{1,0:T(8,128)(2,1)S(1)}, bf16[64,2048]{1,0:T(8,128)(2,1)S(1)}, u32[]{:S(2)}, u32[]{:S(2)}) collective-permute-start(bf16[64,2048]{1,0:T(8,128)(2,1)S(1)} %add_convert_fusion.9), channel_id=1, source_target_pairs={{0,2},{2,4},{4,6},{6,8},{8,10},{10,12},{12,14},{14,0},{1,3},{3,5},... | collective-permute-start | bytes 786440 | tf_op jit(solution)/shard_map/ppermute | solution.py:403
  106.0 10.5 %collective-permute-start.19 = (bf16[64,2048]{1,0:T(8,128)(2,1)S(1)}, bf16[64,2048]{1,0:T(8,128)(2,1)S(1)}, u32[]{:S(2)}, u32[]{:S(2)}) collective-permute-start(bf16[64,2048]{1,0:T(8,128)(2,1)S(1)} %add_convert_fusion.6), channel_id=1, source_target_pairs={{0,14},{2,0},{4,2},{6,4},{8,6},{10,8},{12,10},{14,12},{1,15},{3,1}... | collective-permute-start | bytes 786440 | tf_op jit(solution)/shard_map/ppermute | solution.py:404
  109.6 12.4 %collective-permute-start.22 = (bf16[64,2048]{1,0:T(8,128)(2,1)S(1)}, bf16[64,2048]{1,0:T(8,128)(2,1)S(1)}, u32[]{:S(2)}, u32[]{:S(2)}) collective-permute-start(bf16[64,2048]{1,0:T(8,128)(2,1)S(1)} %add_convert_fusion.4), channel_id=1, source_target_pairs={{0,2},{2,4},{4,6},{6,8},{8,10},{10,12},{12,14},{14,0},{1,3},{3,5},... | collective-permute-start | bytes 786440 | tf_op jit(solution)/shard_map/ppermute | solution.py:403
  109.8 12.4 %collective-permute-start.25 = (bf16[64,2048]{1,0:T(8,128)(2,1)S(1)}, bf16[64,2048]{1,0:T(8,128)(2,1)S(1)}, u32[]{:S(2)}, u32[]{:S(2)}) collective-permute-start(bf16[64,2048]{1,0:T(8,128)(2,1)S(1)} %add_convert_fusion.2), channel_id=1, source_target_pairs={{0,14},{2,0},{4,2},{6,4},{8,6},{10,8},{12,10},{14,12},{1,15},{3,1}... | collective-permute-start | bytes 786440 | tf_op jit(solution)/shard_map/ppermute | solution.py:404
  116.5 11.2 %collective-permute-start.16 = (bf16[64,2048]{1,0:T(8,128)(2,1)S(1)}, bf16[64,2048]{1,0:T(8,128)(2,1)S(1)}, u32[]{:S(2)}, u32[]{:S(2)}) collective-permute-start(bf16[64,2048]{1,0:T(8,128)(2,1)S(1)} %add_convert_fusion.8), channel_id=1, source_target_pairs={{0,2},{2,4},{4,6},{6,8},{8,10},{10,12},{12,14},{14,0},{1,3},{3,5},... | collective-permute-start | bytes 786440 | tf_op jit(solution)/shard_map/ppermute | solution.py:403
  116.6 17.6 %collective-permute-start.20 = (bf16[64,2048]{1,0:T(8,128)(2,1)S(1)}, bf16[64,2048]{1,0:T(8,128)(2,1)S(1)}, u32[]{:S(2)}, u32[]{:S(2)}) collective-permute-start(bf16[64,2048]{1,0:T(8,128)(2,1)S(1)} %add_convert_fusion.5), channel_id=1, source_target_pairs={{0,14},{2,0},{4,2},{6,4},{8,6},{10,8},{12,10},{14,12},{1,15},{3,1}... | collective-permute-start | bytes 786440 | tf_op jit(solution)/shard_map/ppermute | solution.py:408
  122.1 14.4 %collective-permute-start.23 = (bf16[64,2048]{1,0:T(8,128)(2,1)S(1)}, bf16[64,2048]{1,0:T(8,128)(2,1)S(1)}, u32[]{:S(2)}, u32[]{:S(2)}) collective-permute-start(bf16[64,2048]{1,0:T(8,128)(2,1)S(1)} %add_convert_fusion.3), channel_id=1, source_target_pairs={{0,2},{2,4},{4,6},{6,8},{8,10},{10,12},{12,14},{14,0},{1,3},{3,5},... | collective-permute-start | bytes 786440 | tf_op jit(solution)/shard_map/ppermute | solution.py:407
  122.3 8.2 %collective-permute-start.26 = (bf16[64,2048]{1,0:T(8,128)(2,1)S(1)}, bf16[64,2048]{1,0:T(8,128)(2,1)S(1)}, u32[]{:S(2)}, u32[]{:S(2)}) collective-permute-start(bf16[64,2048]{1,0:T(8,128)(2,1)S(1)} %add_convert_fusion.1), channel_id=1, source_target_pairs={{0,14},{2,0},{4,2},{6,4},{8,6},{10,8},{12,10},{14,12},{1,15},{3,1}... | collective-permute-start | bytes 786440 | tf_op jit(solution)/shard_map/ppermute | solution.py:404
  127.7 8.7 %collective-permute-start.17 = (bf16[64,2048]{1,0:T(8,128)(2,1)S(1)}, bf16[64,2048]{1,0:T(8,128)(2,1)S(1)}, u32[]{:S(2)}, u32[]{:S(2)}) collective-permute-start(bf16[64,2048]{1,0:T(8,128)(2,1)S(1)} %add_convert_fusion.7), channel_id=1, source_target_pairs={{0,2},{2,4},{4,6},{6,8},{8,10},{10,12},{12,14},{14,0},{1,3},{3,5},... | collective-permute-start | bytes 786440 | tf_op jit(solution)/shard_map/ppermute | solution.py:407
  130.4 7.8 %copy-start.10 = (bf16[64,4096]{1,0:T(8,128)(2,1)S(1)}, bf16[64,4096]{1,0:T(8,128)(2,1)}, u32[]{:S(2)}) copy-start(bf16[64,4096]{1,0:T(8,128)(2,1)} %refs_0_.5) | copy-start | bytes 1572868
  130.5 7.7 %collective-permute-start.27 = (bf16[64,2048]{1,0:T(8,128)(2,1)S(1)}, bf16[64,2048]{1,0:T(8,128)(2,1)S(1)}, u32[]{:S(2)}, u32[]{:S(2)}) collective-permute-start(bf16[64,2048]{1,0:T(8,128)(2,1)S(1)} %add_convert_fusion), channel_id=1, source_target_pairs={{0,14},{2,0},{4,2},{6,4},{8,6},{10,8},{12,10},{14,12},{1,15},{3,1}... | collective-permute-start | bytes 786440 | tf_op jit(solution)/shard_map/ppermute | solution.py:408

commit v2 on v1

--- a/solution.py
+++ b/solution.py
@@ -71,19 +71,26 @@
 def kv_kernel(places, slots, waits, meta, *refs):
     n = len(places)
     pieces = refs[:n]
-    gain, kt, vt, got, other, outer, inner = refs[n : n + 7]
-    kv, xs, kvs, acc, ss = refs[n + 7 + waits :]
+    gain, kt, vt = refs[n : n + 3]
+    theirs = refs[n + 3 : n + 7]
+    outer, inner = refs[n + 7 : n + 9]
+    kv, xs, kvs, acc, ss = refs[n + 9 + waits :]
     step = pl.program_id(0)
-    early = step < pl.num_programs(0) // 2
     load_tokens(places, pieces, gain, xs, ss, step)
     kvs[0:64] = kt[...]
     kvs[128:192] = vt[...]
-    for i in range(xs.shape[1] // 256):
-        at = slice(i * 256, (i + 1) * 256)
-        low = slice(i * 128, i * 128 + 64)
-        high = slice(i * 128 + 64, i * 128 + 128)
-        kvs[64:128, at] = jnp.where(early, got[low], other[low])
-        kvs[192:256, at] = jnp.where(early, got[high], other[high])
+    quarter = WIDTH // 4
+    for turn in range(2):
+
+        @pl.when(step == turn)
+        def _():
+            for t, base in ((0, meta[3] * quarter), (1, (1 - meta[3]) * quarter)):
+                part = theirs[2 * turn + t]
+                for i in range(quarter // 256):
+                    at = pl.ds(pl.multiple_of(base + i * 256, 256), 256)
+                    kvs[64:128, at] = part[i * 128 : i * 128 + 64]
+                    kvs[192:256, at] = part[i * 128 + 64 : i * 128 + 128]
+
     term = lax.dot_general(
         xs[...], kvs[...], (((1,), (1,)), ((), ())), preferred_element_type=F32
     )
@@ -109,14 +116,26 @@
 def q_kernel(places, slots, waits, meta, *refs):
     n = len(places)
     pieces = refs[:n]
-    gain, wq, got, other, outer, inner = refs[n : n + 6]
-    q, xs, acc, ss = refs[n + 6 + waits :]
+    gain, wq = refs[n : n + 2]
+    theirs = refs[n + 2 : n + 6]
+    outer, inner = refs[n + 6 : n + 8]
+    q, xs, acc, ss = refs[n + 8 + waits :]
     step = pl.program_id(0)
     load_tokens(places, pieces, gain, xs, ss, step)
     x = xs[...]
     gather_sum(acc.at[:, 0:256], jnp.dot(x, wq[...], preferred_element_type=F32), step)
-    w = jnp.where(step < pl.num_programs(0) // 2, got[...], other[...])
-    gather_sum(acc.at[:, 256:512], jnp.dot(x, w, preferred_element_type=F32), step)
+    for turn in range(4):
+
+        @pl.when(step == turn // 2)
+        def _():
+            place = meta[3] if turn % 2 == 0 else 1 - meta[3]
+            quarter = WIDTH // 4
+            columns = pl.ds(pl.multiple_of(place * quarter, quarter), quarter)
+            term = jnp.dot(xs[:, columns], theirs[turn][...], preferred_element_type=F32)
+            if turn == 0:
+                acc[:, 256:512] = term
+            else:
+                acc[:, 256:512] += term
 
     @pl.when(step == pl.num_programs(0) - 1)
     def _():
@@ -138,32 +157,26 @@
             q[i, 3] = jnp.where(core == 0, heads[3], heads[2])
 
 
-def project(queries, after, meta, pieces, places, slots, gain, own, got, other):
+def project(queries, after, meta, pieces, places, slots, gain, own, theirs):
     n = len(slots)
     rows = n * BLOCK
-    depth = 1024 if queries else 2048
+    depth = WIDTH // 2
     steps = WIDTH // depth
     outer, inner = tables()
-    turn = lambda i, m: lax.rem(steps // 2 * m[0] + i, steps)
+    turn = lambda i, m: lax.rem(m[0] + i, 2)
     across = lambda i, m: (0, turn(i, m))
-    soon = lambda i: jnp.minimum(i, steps // 2 - 1)
-    late = lambda i: jnp.maximum(i - steps // 2, 0)
     zero = lambda k: lambda i, m: (0,) * k
     if queries:
         weights = [
             pl.BlockSpec((depth, 256), lambda i, m: (turn(i, m), 0)),
-            pl.BlockSpec((depth, 256), lambda i, m: (soon(i), 0)),
-            pl.BlockSpec((depth, 256), lambda i, m: (late(i), 0)),
-        ]
+        ] + [pl.BlockSpec((depth // 2, 256), lambda i, m: (0, 0))] * 4
         shape = (n, 4, BLOCK, HEAD)
         scratch = [pltpu.VMEM((rows, depth), BF), pltpu.VMEM((rows, 512), F32)]
     else:
         weights = [
             pl.BlockSpec((64, depth), across),
             pl.BlockSpec((64, depth), across),
-            pl.BlockSpec((depth // 2, 256), lambda i, m: (steps + soon(i), 0)),
-            pl.BlockSpec((depth // 2, 256), lambda i, m: (steps + late(i), 0)),
-        ]
+        ] + [pl.BlockSpec((depth // 4, 256), lambda i, m: (2, 0))] * 4
         shape = (2, rows, HEAD)
         scratch = [
             pltpu.VMEM((rows, depth), BF),
@@ -185,14 +198,18 @@
         ),
         out_shape=jax.ShapeDtypeStruct(shape, BF),
         compiler_params=pltpu.CompilerParams(vmem_limit_bytes=56 << 20),
-        cost_estimate=TINY,
+        cost_estimate=pl.CostEstimate(
+            flops=2 * rows * WIDTH * 512, bytes_accessed=2 * WIDTH * (rows + 512), transcendentals=0
+        )
+        if queries
+        else TINY,
         name="queries" if queries else "keys",
-    )(meta, *pieces, gain, *own, got, other, outer, inner, *after)
+    )(meta, *pieces, gain, *own, *theirs, outer, inner, *after)
 
 
 def attend_kernel(slots, waits, meta, q, bits, kv_near, kv_far, their_near, their_far, *refs):
-    wo, wp_got, wp_other = refs[:3]
-    outs = refs[3 + waits : -3]
+    wo, *theirs_wo = refs[:5]
+    outs = refs[5 + waits : -3]
     heads, key, value = refs[-3:]
     nb = len(slots)
     for i, target in ((0, key), (1, value)):
@@ -238,7 +255,18 @@
     piece = 512
     for c in range(WIDTH // piece):
         cols = slice(c * piece, (c + 1) * piece)
-        w = jnp.concatenate([wo[:, cols], wp_got[:, cols], wp_other[:, cols]], axis=0)
+        low = meta[3] == 0
+        parts = [t[:, cols] for t in theirs_wo]
+        w = jnp.concatenate(
+            [
+                wo[:, cols],
+                jnp.where(low, parts[0], parts[1]),
+                jnp.where(low, parts[1], parts[0]),
+                jnp.where(low, parts[2], parts[3]),
+                jnp.where(low, parts[3], parts[2]),
+            ],
+            axis=0,
+        )
         t = jnp.dot(x, w, preferred_element_type=F32).astype(BF)
         half = c // (COLS // piece)
         at = slice(c * piece - half * COLS, (c + 1) * piece - half * COLS)
@@ -253,7 +281,7 @@
     return pl.pallas_call(
         functools.partial(attend_kernel, slots, len(after)),
         in_specs=[pl.BlockSpec(memory_space=pltpu.SMEM), vmem]
-        + [vmem] * 8
+        + [vmem] * 10
         + [pl.BlockSpec(memory_space=pl.ANY)] * len(after),
         out_specs=[vmem] * len(out_shape),
         out_shape=out_shape,
@@ -268,35 +296,38 @@
     )(meta, q, *rest, *after)
 
 
-def pick_kernel(meta, wq, kt, vt, out):
-    half = WIDTH // 2
-    out[0:half] = wq[...]
-    for i in range(half // 256):
+def pick_kernel(meta, wq, kt, vt, wo, out, wo_out):
+    quarter = WIDTH // 4
+    wo_out[...] = wo[...]
+    out[0:quarter] = wq[...]
+    for i in range(quarter // 256):
         at = slice(i * 256, (i + 1) * 256)
-        row = half + i * 128
+        row = quarter + i * 128
         out[row : row + 64] = kt[:, at]
         out[row + 64 : row + 128] = vt[:, at]
 
 
-def pick(meta, wq, kt, vt):
-    half = WIDTH // 2
+def pick(meta, wq, kt, vt, wo):
+    quarter = WIDTH // 4
+    shapes = [(quarter + quarter // 2, 256), (BLOCK, WIDTH)]
     return pl.pallas_call(
         pick_kernel,
         grid_spec=pltpu.PrefetchScalarGridSpec(
             num_scalar_prefetch=1,
             grid=(1,),
             in_specs=[
-                pl.BlockSpec((half, 256), lambda i, m: (m[0], 0)),
-                pl.BlockSpec((64, half), lambda i, m: (0, m[0])),
-                pl.BlockSpec((64, half), lambda i, m: (0, m[0])),
+                pl.BlockSpec((quarter, 256), lambda i, m: (2 * m[0] + m[3], 0)),
+                pl.BlockSpec((64, quarter), lambda i, m: (0, 2 * m[0] + m[3])),
+                pl.BlockSpec((64, quarter), lambda i, m: (0, 2 * m[0] + m[3])),
+                pl.BlockSpec((BLOCK, WIDTH), lambda i, m: (2 * m[0] + m[3], 0)),
             ],
-            out_specs=pl.BlockSpec((half + half // 2, 256), lambda i, m: (0, 0)),
+            out_specs=[pl.BlockSpec(shape, lambda i, m: (0, 0)) for shape in shapes],
         ),
-        out_shape=jax.ShapeDtypeStruct((half + half // 2, 256), BF),
+        out_shape=[jax.ShapeDtypeStruct(shape, BF) for shape in shapes],
         compiler_params=pltpu.CompilerParams(vmem_limit_bytes=56 << 20),
         cost_estimate=TINY,
         name="pick",
-    )(meta, wq, kt, vt)
+    )(meta, wq, kt, vt, wo)
 
 
 def gate_kernel(*refs):
@@ -321,6 +352,10 @@
     return lax.ppermute(array, ("xl", "xh"), [(i, 3 - i) for i in range(4)])
 
 
+def from_y(array):
+    return lax.ppermute(array, "y", [(i, i ^ 1) for i in range(4)])
+
+
 def from_core(array):
     return lax.ppermute(array, "c", [(0, 1), (1, 0)])
 
@@ -350,37 +385,42 @@
         pieces += [r, l]
         at = BLOCK * (1 + 2 * s)
         places += [(at, BLOCK), (at + BLOCK, BLOCK)]
+        if s == 0:
+            step_one = [r, l]
         if s == 1:
             step_two = [r, l]
     step_three = [r, l]
     last = [lax.ppermute(r[:HALF], "z", RIGHT), lax.ppermute(l[HALF:], "z", LEFT)]
     last_places = [(0, HALF), (HALF, HALF)]
 
-    meta = jnp.stack([core, z, xh]).astype(jnp.int32)
+    meta = jnp.stack([core, z, xh, lax.rem(lax.axis_index("y"), 2)]).astype(jnp.int32)
     kt = key_weight.T
     vt = value_matrix.T
-    got = from_x(pick(meta, query_weight, kt, vt))
-    (got,) = gate([got], step_three)
-    other = from_core(got)
-    wo_mine = lax.dynamic_slice_in_dim(output_weight, core * HEAD, HEAD, 0)
+    mine, wo_mine = pick(meta, query_weight, kt, vt, output_weight)
+    got = from_x(mine)
+    (got,) = gate([got], step_one)
+    near_got = from_y(got)
     (wo_mine,) = gate([wo_mine], [step_two[0]])
     wo_got = from_x(wo_mine)
+    (wo_got,) = gate([wo_got], step_three)
+    wo_near_got = from_y(wo_got)
+    (near_got,) = gate([near_got], step_three)
+    theirs = [got, near_got, from_core(got), from_core(near_got)]
 
     bits = keep_bits.astype(BF).transpose(1, 0, 2).reshape(16, 32)
     bits = jnp.pad(bits, ((0, 0), (0, HEAD - 32)))
 
     gain = norm_gain[None, :]
-    kv_near = project(False, [], meta, pieces, places, range(7), gain, (kt, vt), got, other)
+    kv_near = project(False, [], meta, pieces, places, range(7), gain, (kt, vt), theirs)
     their_near = pair(jnp.concatenate([kv_near.reshape(896, HEAD), bits]))
-    kv_far = project(False, [kv_near], meta, last, last_places, [7], gain, (kt, vt), got, other)
+    kv_far = project(False, [kv_near], meta, last, last_places, [7], gain, (kt, vt), theirs)
     their_far = pair(kv_far)
     everything = places + [(448 + start, count) for start, count in last_places]
     q = project(
-        True, [kv_far], meta, pieces + last, everything, range(8), gain, (query_weight,), got, other
+        True, [kv_far], meta, pieces + last, everything, range(8), gain, (query_weight,), theirs
     )
-    (wo_got,) = gate([wo_got], [q])
-    wo_other = from_core(wo_got)
-    shared = (bits, kv_near, kv_far, their_near, their_far, output_weight, wo_got, wo_other)
+    wo_got, wo_near_got = gate([wo_got, wo_near_got], [kv_far])
+    shared = (bits, kv_near, kv_far, their_near, their_far, output_weight, wo_got, wo_near_got, from_core(wo_got), from_core(wo_near_got))
 
     near = {}
 

time: 141 us -> 135 us (0.957)
  waiting for transfers between devices: 53 us -> 46.9 us
    ppermute x3, waiting for transfers between devices: 29.3 us -> 17.9 us  [on_device(): r = lax.ppermute(r, 'z', RIGHT)]
    ppermute x2, waiting for transfers between devices: 6.77 us -> 0.01 us  [pair(): return lax.ppermute(array, 'xh', [(0, 1), (1, 0)])]
    ppermute x2, waiting for transfers between devices: 3.15 us -> 8.81 us  [from_x(): return lax.ppermute(array, ('xl', 'xh'), [(i, 3 - i) for i in range(4)])]
    ppermute x4, waiting for transfers between devices: 7.24 us -> 2.82 us  [on_device(): r[c] = add(lax.ppermute(r[c], 'z', RIGHT), block(d, c))]
    ppermute x4, waiting for transfers between devices: 2.65 us -> 6.75 us  [on_device(): l[c] = add(lax.ppermute(l[c], 'z', LEFT), block(-d, c))]
    ppermute x0 -> x2, starting transfers between devices: none -> 3.15 us  [from_y(): return lax.ppermute(array, 'y', [(i, i ^ 1) for i in range(4)])]
    ppermute x0 -> x2, waiting for transfers between devices: none -> 3.1 us  [from_y(): return lax.ppermute(array, 'y', [(i, i ^ 1) for i in range(4)])]
    ppermute x2, waiting for transfers between devices: 2.15 us -> 4.76 us  [on_device(): right = lax.ppermute(r[c], 'z', RIGHT)]
  transfers between devices with their start and end apart: 28 -> 32, of which waited for: 13 -> 11; matrix products, arithmetic and copies ran while one was open for 3% -> 1% of each run, Pallas kernels for 19% -> 21%
where the time goes in v2:
time: 135 us
  waiting for transfers between devices  46.9 us (35%)
  starting transfers between devices  46.3 us (34%)
  Pallas kernels  31.7 us (23%)
  local copies, waits for them, and re-layouts  6.91 us (5%)
  other arithmetic  2.4 us (2%)
    pallas_call x3, Pallas kernels, project(): pl.pallas_call(functools.partial(q_kernel if queries else kv_kernel, plac...  18.5 us
    ppermute x3, waiting for transfers between devices, on_device(): r = lax.ppermute(r, 'z', RIGHT)  17.9 us
    ppermute x4, starting transfers between devices, on_device(): l[c] = add(lax.ppermute(l[c], 'z', LEFT), block(-d, c))  12.3 us
    ppermute x3, starting transfers between devices, on_device(): l = lax.ppermute(l, 'z', LEFT)  10.4 us
    pallas_call x2, Pallas kernels, attend(): pl.pallas_call(functools.partial(attend_kernel, slots, len(after)), in_sp...  10.1 us
    ppermute x2, waiting for transfers between devices, from_x(): return lax.ppermute(array, ('xl', 'xh'), [(i, 3 - i) for i in range(4)])  8.81 us
    ppermute x2, starting transfers between devices, on_device(): left = lax.ppermute(l[c], 'z', LEFT)  7.54 us
    unnamed x44, local copies, waits for them, and re-layouts  6.76 us
  transfers between devices with their start and end apart: 32, of which 11 were waited for; matrix products, arithmetic and copies ran while one was open for 1% of the time, Pallas kernels for 21%

profile of v2, /device:TPU:6, one launch (start us, length us, event | category | flops | bytes accessed | tf_op | source)
XLA Modules:
  0.0 134.5 jit_solution(4016606678373611637)
XLA Ops:
  0.0 1.9 %collective-permute-start = (bf16[64,4096]{1,0:T(8,128)(2,1)}, bf16[64,4096]{1,0:T(8,128)(2,1)S(1)}, u32[]{:S(2)}, u32[]{:S(2)}) collective-permute-start(bf16[64,4096]{1,0:T(8,128)(2,1)} %refs_0_.5), channel_id=1, source_target_pairs={{0,2},{2,4},{4,6},{6,8},{8,10},{10,12},{12,14},{14,0},{1,3},{3,5},... | collective-permute-start | bytes 1572872 | tf_op jit(solution)/shard_map/ppermute | solution.py:383
  1.9 3.9 %collective-permute-start.1 = (bf16[64,4096]{1,0:T(8,128)(2,1)}, bf16[64,4096]{1,0:T(8,128)(2,1)S(1)}, u32[]{:S(2)}, u32[]{:S(2)}) collective-permute-start(bf16[64,4096]{1,0:T(8,128)(2,1)} %refs_0_.5), channel_id=1, source_target_pairs={{0,14},{2,0},{4,2},{6,4},{8,6},{10,8},{12,10},{14,12},{1,15},{3,1}... | collective-permute-start | bytes 1572872 | tf_op jit(solution)/shard_map/ppermute | solution.py:384
  5.9 0.7 pad_add_fusion.meta
  6.5 3.1 %pick.1 = (bf16[1536,256]{1,0:T(8,128)(2,1)}, bf16[64,4096]{1,0:T(8,128)(2,1)}) custom-call(s32[4]{0:T(128)} %pad_add_fusion.meta, bf16[4096,256]{1,0:T(8,128)(2,1)} %refs_10_.2, bf16[64,4096]{1,0:T(8,128)(2,1)} %bitcast.11, bf16[64,4096]{1,0:T(8,128)(2,1)} %bitcast.14, bf16[256,4096]{1,0:T(8,128)(2,1)} %refs_0_.7), custom_call_target="tpu_custom_call" | custom-call | flops 1000 | bytes 1000 | tf_op jit(solution)/shard_map/pick/pallas_call | solution.py:313
  9.6 0.5 collective-permute-start.8
  10.1 7.9 %collective-permute-done.refs_1_ = bf16[64,4096]{1,0:T(8,128)(2,1)S(1)} collective-permute-done((bf16[64,4096]{1,0:T(8,128)(2,1)}, bf16[64,4096]{1,0:T(8,128)(2,1)S(1)}, u32[]{:S(2)}, u32[]{:S(2)}) %collective-permute-start) | collective-permute-done | bytes 524320 | tf_op jit(solution)/shard_map/ppermute | solution.py:383
  18.0 3.2 %collective-permute-start.3 = (bf16[64,4096]{1,0:T(8,128)(2,1)S(1)}, bf16[64,4096]{1,0:T(8,128)(2,1)}, u32[]{:S(2)}, u32[]{:S(2)}) collective-permute-start(bf16[64,4096]{1,0:T(8,128)(2,1)S(1)} %collective-permute-done.1.refs_2_), channel_id=1, source_target_pairs={{0,14},{2,0},{4,2},{6,4},{8,6},{10,8},{12,10},{14,12},{1,15},{3,1}... | collective-permute-start | bytes 1572872 | tf_op jit(solution)/shard_map/ppermute | solution.py:384
  21.2 8.8 %collective-permute-done.8.refs_0_ = bf16[1536,256]{1,0:T(8,128)(2,1)S(1)} collective-permute-done((bf16[1536,256]{1,0:T(8,128)(2,1)}, bf16[1536,256]{1,0:T(8,128)(2,1)S(1)}, u32[]{:S(2)}, u32[]{:S(2)}) %collective-permute-start.8) | collective-permute-done | bytes 786464 | tf_op jit(solution)/shard_map/ppermute | solution.py:352
  30.0 0.9 copy-done.10
  30.9 1.6 %collective-permute-start.9 = (bf16[1536,256]{1,0:T(8,128)(2,1)}, bf16[1536,256]{1,0:T(8,128)(2,1)S(1)}, u32[]{:S(2)}, u32[]{:S(2)}) collective-permute-start(bf16[1536,256]{1,0:T(8,128)(2,1)} %gate.5.refs_10_.refs_5_.refs_11_), channel_id=1, source_target_pairs={{0,32},{32,0},{64,96},{96,64},{1,33},{33,1},{65,97},{97,65},{2,34}... | collective-permute-start | bytes 2359304 | tf_op jit(solution)/shard_map/ppermute | solution.py:356
  32.5 3.2 %collective-permute-start.5 = (bf16[64,4096]{1,0:T(8,128)(2,1)}, bf16[64,4096]{1,0:T(8,128)(2,1)S(1)}, u32[]{:S(2)}, u32[]{:S(2)}) collective-permute-start(bf16[64,4096]{1,0:T(8,128)(2,1)} %collective-permute-done.3.refs_4_), channel_id=1, source_target_pairs={{0,14},{2,0},{4,2},{6,4},{8,6},{10,8},{12,10},{14,12},{1,15},{3,1}... | collective-permute-start | bytes 1572872 | tf_op jit(solution)/shard_map/ppermute | solution.py:384
  35.7 0.5 collective-permute-start.14
  36.2 10.0 %collective-permute-done.4.refs_1_.refs_5_ = bf16[64,4096]{1,0:T(8,128)(2,1)S(1)} collective-permute-done((bf16[64,4096]{1,0:T(8,128)(2,1)}, bf16[64,4096]{1,0:T(8,128)(2,1)S(1)}, u32[]{:S(2)}, u32[]{:S(2)}) %collective-permute-start.4) | collective-permute-done | bytes 524320 | tf_op jit(solution)/shard_map/ppermute | solution.py:383
  46.2 3.1 %collective-permute-done.9.refs_0_ = bf16[1536,256]{1,0:T(8,128)(2,1)S(1)} collective-permute-done((bf16[1536,256]{1,0:T(8,128)(2,1)}, bf16[1536,256]{1,0:T(8,128)(2,1)S(1)}, u32[]{:S(2)}, u32[]{:S(2)}) %collective-permute-start.9) | collective-permute-done | bytes 786464 | tf_op jit(solution)/shard_map/ppermute | solution.py:356
  49.3 0.9 copy-done.9
  50.3 0.8 copy-done.1
  51.0 1.6 %collective-permute-start.15 = (bf16[64,4096]{1,0:T(8,128)(2,1)}, bf16[64,4096]{1,0:T(8,128)(2,1)S(1)}, u32[]{:S(2)}, u32[]{:S(2)}) collective-permute-start(bf16[64,4096]{1,0:T(8,128)(2,1)} %gate.8.refs_0_), channel_id=1, source_target_pairs={{0,32},{32,0},{64,96},{96,64},{1,33},{33,1},{65,97},{97,65},{2,34}... | collective-permute-start | bytes 1572872 | tf_op jit(solution)/shard_map/ppermute | solution.py:356
  52.8 3.3 %collective-permute-start.7 = (bf16[32,4096]{1,0:T(8,128)(2,1)S(1)}, bf16[32,4096]{1,0:T(8,128)(2,1)S(1)}, u32[]{:S(2)}, u32[]{:S(2)}) collective-permute-start(bf16[32,4096]{1,0:T(8,128)(2,1)S(1)} %slice.9), channel_id=1, source_target_pairs={{0,14},{2,0},{4,2},{6,4},{8,6},{10,8},{12,10},{14,12},{1,15},{3,1}... | collective-permute-start | bytes 786440 | tf_op jit(solution)/shard_map/ppermute | solution.py:393
  56.1 0.9 copy-done.15
  56.9 6.5 %keys.2.refs_11_.kv_near = bf16[2,448,128]{2,1,0:T(8,128)(2,1)} custom-call(s32[4]{0:T(128)} %pad_add_fusion.meta, bf16[64,4096]{1,0:T(8,128)(2,1)} %refs_0_.5, bf16[64,4096]{1,0:T(8,128)(2,1)} %copy-done.16, bf16[64,4096]{1,0:T(8,128)(2,1)} %copy-done.17, bf16[64,4096]{1,0:T(8,128)(2,1)} %collective-permute-done.2.refs_3_.refs_1_, ...), custom_call_target="tpu_custom_call" | custom-call | flops 1000 | bytes 1000 | tf_op jit(solution)/shard_map/keys/pallas_call | solution.py:186
  63.5 0.7 copy-done.19
  64.2 0.7 copy-done.20
  65.0 4.4 %keys.3.refs_17_.refs_2_.kv_far = bf16[2,64,128]{2,1,0:T(8,128)(2,1)} custom-call(s32[4]{0:T(128)} %pad_add_fusion.meta, bf16[32,4096]{1,0:T(8,128)(2,1)} %copy-done.19, bf16[32,4096]{1,0:T(8,128)(2,1)} %copy-done.20, f32[1,4096]{1,0:T(1,128)} %bitcast.18, bf16[64,4096]{1,0:T(8,128)(2,1)} %bitcast.13, bf16[64,4096]{1,0:T(8,128)(2,1)} %bitcast.16, ...), custom_call_target="tpu_custom_call" | custom-call | flops 1000 | bytes 1000 | tf_op jit(solution)/shard_map/keys/pallas_call | solution.py:186
  69.4 0.8 copy-done.5
  70.2 0.5 collective-permute-start.17
  70.9 0.3 collective-permute-start.12
  71.2 3.3 %collective-permute-start.13 = (bf16[2,64,128]{2,1,0:T(8,128)(2,1)}, bf16[2,64,128]{2,1,0:T(8,128)(2,1)S(1)}, u32[]{:S(2)}, u32[]{:S(2)}) collective-permute-start(bf16[2,64,128]{2,1,0:T(8,128)(2,1)} %keys.3.refs_17_.refs_2_.kv_far), channel_id=1, source_target_pairs={{0,1},{1,0},{2,3},{3,2},{4,5},{5,4},{6,7},{7,6},{8,9},{9,8},{10,11... | collective-permute-start | bytes 98312 | tf_op jit(solution)/shard_map/ppermute | solution.py:364
  74.5 7.5 %queries.1.q = bf16[8,4,64,128]{3,2,1,0:T(8,128)(2,1)} custom-call(s32[4]{0:T(128)} %pad_add_fusion.meta, bf16[64,4096]{1,0:T(8,128)(2,1)} %refs_0_.5, bf16[64,4096]{1,0:T(8,128)(2,1)} %copy-done.16, bf16[64,4096]{1,0:T(8,128)(2,1)} %copy-done.17, bf16[64,4096]{1,0:T(8,128)(2,1)} %collective-permute-done.2.refs_3_.refs_1_, ...), custom_call_target="tpu_custom_call" | custom-call | flops 2147483648 | bytes 8388608 | tf_op jit(solution)/shard_map/queries/pallas_call | solution.py:186
  82.2 1.0 copy-done.4
  83.2 4.0 %attend.2 = (bf16[64,2048]{1,0:T(8,128)(2,1)S(1)}, bf16[64,2048]{1,0:T(8,128)(2,1)S(1)}, bf16[64,2048]{1,0:T(8,128)(2,1)S(1)}, bf16[64,2048]{1,0:T(8,128)(2,1)S(...) custom-call(s32[4]{0:T(128)S(1)} %copy-done.8, bf16[8,4,64,128]{3,2,1,0:T(8,128)(2,1)S(1)} %copy-done.4, ...), custom_call_target="tpu_custom_call" | custom-call | flops 1000 | bytes 1000 | tf_op jit(solution)/shard_map/attend/pallas_call | solution.py:281
  87.2 1.3 collective-permute-start.28
  88.5 0.8 collective-permute-start.25
  89.3 2.4 %collective-permute-start.22 = (bf16[64,2048]{1,0:T(8,128)(2,1)S(1)}, bf16[64,2048]{1,0:T(8,128)(2,1)S(1)}, u32[]{:S(2)}, u32[]{:S(2)}) collective-permute-start(bf16[64,2048]{1,0:T(8,128)(2,1)S(1)} %get-tuple-element.34), channel_id=1, source_target_pairs={{0,14},{2,0},{4,2},{6,4},{8,6},{10,8},{12,10},{14,12},{1,15},{3,1}... | collective-permute-start | bytes 786440 | tf_op jit(solution)/shard_map/ppermute | solution.py:444
  91.7 6.1 %attend.3 = (bf16[64,2048]{1,0:T(8,128)(2,1)S(1)}, bf16[64,2048]{1,0:T(8,128)(2,1)S(1)}, bf16[64,2048]{1,0:T(8,128)(2,1)S(1)}, bf16[64,2048]{1,0:T(8,128)(2,1)S(...) custom-call(s32[4]{0:T(128)S(1)} %copy-done.8, ...), custom_call_target="tpu_custom_call" | custom-call | flops 1000 | bytes 1000 | tf_op jit(solution)/shard_map/attend/pallas_call | solution.py:281
  97.9 3.3 %collective-permute-start.29 = (bf16[64,2048]{1,0:T(8,128)(2,1)S(1)}, bf16[64,2048]{1,0:T(8,128)(2,1)S(1)}, u32[]{:S(2)}, u32[]{:S(2)}) collective-permute-start(bf16[64,2048]{1,0:T(8,128)(2,1)S(1)} %add_convert_fusion.2), channel_id=1, source_target_pairs={{0,14},{2,0},{4,2},{6,4},{8,6},{10,8},{12,10},{14,12},{1,15},{3,1}... | collective-permute-start | bytes 786440 | tf_op jit(solution)/shard_map/ppermute | solution.py:444
  101.4 0.5 collective-permute-done.22
  102.0 2.8 %collective-permute-start.23 = (bf16[64,2048]{1,0:T(8,128)(2,1)S(1)}, bf16[64,2048]{1,0:T(8,128)(2,1)S(1)}, u32[]{:S(2)}, u32[]{:S(2)}) collective-permute-start(bf16[64,2048]{1,0:T(8,128)(2,1)S(1)} %add_convert_fusion.6), channel_id=1, source_target_pairs={{0,14},{2,0},{4,2},{6,4},{8,6},{10,8},{12,10},{14,12},{1,15},{3,1}... | collective-permute-start | bytes 786440 | tf_op jit(solution)/shard_map/ppermute | solution.py:444
  104.9 3.0 %collective-permute-done.29 = bf16[64,2048]{1,0:T(8,128)(2,1)S(1)} collective-permute-done((bf16[64,2048]{1,0:T(8,128)(2,1)S(1)}, bf16[64,2048]{1,0:T(8,128)(2,1)S(1)}, u32[]{:S(2)}, u32[]{:S(2)}) %collective-permute-start.29) | collective-permute-done | bytes 262176 | tf_op jit(solution)/shard_map/ppermute | solution.py:444
  108.0 3.8 %collective-permute-start.30 = (bf16[64,2048]{1,0:T(8,128)(2,1)S(1)}, bf16[64,2048]{1,0:T(8,128)(2,1)S(1)}, u32[]{:S(2)}, u32[]{:S(2)}) collective-permute-start(bf16[64,2048]{1,0:T(8,128)(2,1)S(1)} %add_convert_fusion.1), channel_id=1, source_target_pairs={{0,14},{2,0},{4,2},{6,4},{8,6},{10,8},{12,10},{14,12},{1,15},{3,1}... | collective-permute-start | bytes 786440 | tf_op jit(solution)/shard_map/ppermute | solution.py:444
  111.9 1.6 %collective-permute-done.23 = bf16[64,2048]{1,0:T(8,128)(2,1)S(1)} collective-permute-done((bf16[64,2048]{1,0:T(8,128)(2,1)S(1)}, bf16[64,2048]{1,0:T(8,128)(2,1)S(1)}, u32[]{:S(2)}, u32[]{:S(2)}) %collective-permute-start.23) | collective-permute-done | bytes 262176 | tf_op jit(solution)/shard_map/ppermute | solution.py:444
  113.6 3.8 %collective-permute-start.24 = (bf16[64,2048]{1,0:T(8,128)(2,1)S(1)}, bf16[64,2048]{1,0:T(8,128)(2,1)S(1)}, u32[]{:S(2)}, u32[]{:S(2)}) collective-permute-start(bf16[64,2048]{1,0:T(8,128)(2,1)S(1)} %add_convert_fusion.5), channel_id=1, source_target_pairs={{0,14},{2,0},{4,2},{6,4},{8,6},{10,8},{12,10},{14,12},{1,15},{3,1}... | collective-permute-start | bytes 786440 | tf_op jit(solution)/shard_map/ppermute | solution.py:448
  117.5 1.6 %collective-permute-done.30 = bf16[64,2048]{1,0:T(8,128)(2,1)S(1)} collective-permute-done((bf16[64,2048]{1,0:T(8,128)(2,1)S(1)}, bf16[64,2048]{1,0:T(8,128)(2,1)S(1)}, u32[]{:S(2)}, u32[]{:S(2)}) %collective-permute-start.30) | collective-permute-done | bytes 262176 | tf_op jit(solution)/shard_map/ppermute | solution.py:444
  119.2 3.8 %collective-permute-start.31 = (bf16[64,2048]{1,0:T(8,128)(2,1)S(1)}, bf16[64,2048]{1,0:T(8,128)(2,1)S(1)}, u32[]{:S(2)}, u32[]{:S(2)}) collective-permute-start(bf16[64,2048]{1,0:T(8,128)(2,1)S(1)} %add_convert_fusion), channel_id=1, source_target_pairs={{0,14},{2,0},{4,2},{6,4},{8,6},{10,8},{12,10},{14,12},{1,15},{3,1}... | collective-permute-start | bytes 786440 | tf_op jit(solution)/shard_map/ppermute | solution.py:448
  123.0 2.8 %collective-permute-done.20 = bf16[64,2048]{1,0:T(8,128)(2,1)S(1)} collective-permute-done((bf16[64,2048]{1,0:T(8,128)(2,1)S(1)}, bf16[64,2048]{1,0:T(8,128)(2,1)S(1)}, u32[]{:S(2)}, u32[]{:S(2)}) %collective-permute-start.20) | collective-permute-done | bytes 262176 | tf_op jit(solution)/shard_map/ppermute | solution.py:443
  126.0 2.7 %collective-permute-done.31 = bf16[64,2048]{1,0:T(8,128)(2,1)S(1)} collective-permute-done((bf16[64,2048]{1,0:T(8,128)(2,1)S(1)}, bf16[64,2048]{1,0:T(8,128)(2,1)S(1)}, u32[]{:S(2)}, u32[]{:S(2)}) %collective-permute-start.31) | collective-permute-done | bytes 262176 | tf_op jit(solution)/shard_map/ppermute | solution.py:448
  128.8 4.8 %collective-permute-done.21 = bf16[64,2048]{1,0:T(8,128)(2,1)S(1)} collective-permute-done((bf16[64,2048]{1,0:T(8,128)(2,1)S(1)}, bf16[64,2048]{1,0:T(8,128)(2,1)S(1)}, u32[]{:S(2)}, u32[]{:S(2)}) %collective-permute-start.21) | collective-permute-done | bytes 262176 | tf_op jit(solution)/shard_map/ppermute | solution.py:447
  133.5 0.1 convert_add_fusion.1
  133.6 0.9 fusion
  (92 shorter events, 1.6 us)
Async XLA Ops:
  0.0 18.0 %collective-permute-start = (bf16[64,4096]{1,0:T(8,128)(2,1)}, bf16[64,4096]{1,0:T(8,128)(2,1)S(1)}, u32[]{:S(2)}, u32[]{:S(2)}) collective-permute-start(bf16[64,4096]{1,0:T(8,128)(2,1)} %refs_0_.5), channel_id=1, source_target_pairs={{0,2},{2,4},{4,6},{6,8},{8,10},{10,12},{12,14},{14,0},{1,3},{3,5},... | collective-permute-start | bytes 1572872 | tf_op jit(solution)/shard_map/ppermute | solution.py:383
  1.9 16.1 %collective-permute-start.1 = (bf16[64,4096]{1,0:T(8,128)(2,1)}, bf16[64,4096]{1,0:T(8,128)(2,1)S(1)}, u32[]{:S(2)}, u32[]{:S(2)}) collective-permute-start(bf16[64,4096]{1,0:T(8,128)(2,1)} %refs_0_.5), channel_id=1, source_target_pairs={{0,14},{2,0},{4,2},{6,4},{8,6},{10,8},{12,10},{14,12},{1,15},{3,1}... | collective-permute-start | bytes 1572872 | tf_op jit(solution)/shard_map/ppermute | solution.py:384
  9.6 20.4 %collective-permute-start.8 = (bf16[1536,256]{1,0:T(8,128)(2,1)}, bf16[1536,256]{1,0:T(8,128)(2,1)S(1)}, u32[]{:S(2)}, u32[]{:S(2)}) collective-permute-start(bf16[1536,256]{1,0:T(8,128)(2,1)} %get-tuple-element.25), channel_id=1, source_target_pairs={{0,129},{1,128},{128,1},{129,0},{2,131},{3,130},{130,3},{131,2},{4... | collective-permute-start | bytes 2359304 | tf_op jit(solution)/shard_map/ppermute | solution.py:352
  18.0 12.1 %copy-start.16 = (bf16[64,4096]{1,0:T(8,128)(2,1)}, bf16[64,4096]{1,0:T(8,128)(2,1)S(1)}, u32[]{:S(2)}) copy-start(bf16[64,4096]{1,0:T(8,128)(2,1)S(1)} %collective-permute-done.refs_1_) | copy-start | bytes 1572868
  18.0 14.5 %collective-permute-start.2 = (bf16[64,4096]{1,0:T(8,128)(2,1)S(1)}, bf16[64,4096]{1,0:T(8,128)(2,1)}, u32[]{:S(2)}, u32[]{:S(2)}) collective-permute-start(bf16[64,4096]{1,0:T(8,128)(2,1)S(1)} %collective-permute-done.refs_1_), channel_id=1, source_target_pairs={{0,2},{2,4},{4,6},{6,8},{8,10},{10,12},{12,14},{14,0},{1,3},{3,5},... | collective-permute-start | bytes 1572872 | tf_op jit(solution)/shard_map/ppermute | solution.py:383
  18.0 12.0 %copy-start.17 = (bf16[64,4096]{1,0:T(8,128)(2,1)}, bf16[64,4096]{1,0:T(8,128)(2,1)S(1)}, u32[]{:S(2)}) copy-start(bf16[64,4096]{1,0:T(8,128)(2,1)S(1)} %collective-permute-done.1.refs_2_) | copy-start | bytes 1572868
  18.0 14.5 %collective-permute-start.3 = (bf16[64,4096]{1,0:T(8,128)(2,1)S(1)}, bf16[64,4096]{1,0:T(8,128)(2,1)}, u32[]{:S(2)}, u32[]{:S(2)}) collective-permute-start(bf16[64,4096]{1,0:T(8,128)(2,1)S(1)} %collective-permute-done.1.refs_2_), channel_id=1, source_target_pairs={{0,14},{2,0},{4,2},{6,4},{8,6},{10,8},{12,10},{14,12},{1,15},{3,1}... | collective-permute-start | bytes 1572872 | tf_op jit(solution)/shard_map/ppermute | solution.py:384
  30.9 18.4 %collective-permute-start.9 = (bf16[1536,256]{1,0:T(8,128)(2,1)}, bf16[1536,256]{1,0:T(8,128)(2,1)S(1)}, u32[]{:S(2)}, u32[]{:S(2)}) collective-permute-start(bf16[1536,256]{1,0:T(8,128)(2,1)} %gate.5.refs_10_.refs_5_.refs_11_), channel_id=1, source_target_pairs={{0,32},{32,0},{64,96},{96,64},{1,33},{33,1},{65,97},{97,65},{2,34}... | collective-permute-start | bytes 2359304 | tf_op jit(solution)/shard_map/ppermute | solution.py:356
  32.5 13.7 %collective-permute-start.4 = (bf16[64,4096]{1,0:T(8,128)(2,1)}, bf16[64,4096]{1,0:T(8,128)(2,1)S(1)}, u32[]{:S(2)}, u32[]{:S(2)}) collective-permute-start(bf16[64,4096]{1,0:T(8,128)(2,1)} %collective-permute-done.2.refs_3_.refs_1_), channel_id=1, source_target_pairs={{0,2},{2,4},{4,6},{6,8},{8,10},{10,12},{12,14},{14,0},{1,3},{3,5},... | collective-permute-start | bytes 1572872 | tf_op jit(solution)/shard_map/ppermute | solution.py:383
  32.5 13.7 %collective-permute-start.5 = (bf16[64,4096]{1,0:T(8,128)(2,1)}, bf16[64,4096]{1,0:T(8,128)(2,1)S(1)}, u32[]{:S(2)}, u32[]{:S(2)}) collective-permute-start(bf16[64,4096]{1,0:T(8,128)(2,1)} %collective-permute-done.3.refs_4_), channel_id=1, source_target_pairs={{0,14},{2,0},{4,2},{6,4},{8,6},{10,8},{12,10},{14,12},{1,15},{3,1}... | collective-permute-start | bytes 1572872 | tf_op jit(solution)/shard_map/ppermute | solution.py:384
  35.7 14.5 %collective-permute-start.14 = (bf16[64,4096]{1,0:T(8,128)(2,1)}, bf16[64,4096]{1,0:T(8,128)(2,1)S(1)}, u32[]{:S(2)}, u32[]{:S(2)}) collective-permute-start(bf16[64,4096]{1,0:T(8,128)(2,1)} %gate.7), channel_id=1, source_target_pairs={{0,129},{1,128},{128,1},{129,0},{2,131},{3,130},{130,3},{131,2},{4... | collective-permute-start | bytes 1572872 | tf_op jit(solution)/shard_map/ppermute | solution.py:352
  36.2 19.8 %collective-permute-start.10 = (bf16[1536,256]{1,0:T(8,128)(2,1)}, bf16[1536,256]{1,0:T(8,128)(2,1)S(1)}, u32[]{:S(2)}, u32[]{:S(2)}) collective-permute-start(bf16[1536,256]{1,0:T(8,128)(2,1)} %gate.5.refs_10_.refs_5_.refs_11_), channel_id=1, source_target_pairs={{0,16},{16,0},{1,17},{17,1},{2,18},{18,2},{3,19},{19,3},{4,20},{20... | collective-permute-start | bytes 2359304 | tf_op jit(solution)/shard_map/ppermute | solution.py:360
  46.2 3.1 %copy-start.11 = (bf16[64,4096]{1,0:T(8,128)(2,1)}, bf16[64,4096]{1,0:T(8,128)(2,1)S(1)}, u32[]{:S(2)}) copy-start(bf16[64,4096]{1,0:T(8,128)(2,1)S(1)} %collective-permute-done.4.refs_1_.refs_5_) | copy-start | bytes 1572868
  46.2 3.1 %copy-start.13 = (bf16[64,4096]{1,0:T(8,128)(2,1)}, bf16[64,4096]{1,0:T(8,128)(2,1)S(1)}, u32[]{:S(2)}) copy-start(bf16[64,4096]{1,0:T(8,128)(2,1)S(1)} %collective-permute-done.5.refs_2_.refs_6_) | copy-start | bytes 1572868
  49.3 0.9 copy-start.9
  50.2 2.4 %copy-start.12 = (bf16[64,4096]{1,0:T(8,128)(2,1)S(1)}, bf16[64,4096]{1,0:T(8,128)(2,1)}, u32[]{:S(2)}) copy-start(bf16[64,4096]{1,0:T(8,128)(2,1)} %copy-done.11) | copy-start | bytes 1572868
  50.2 2.5 %copy-start.14 = (bf16[64,4096]{1,0:T(8,128)(2,1)S(1)}, bf16[64,4096]{1,0:T(8,128)(2,1)}, u32[]{:S(2)}) copy-start(bf16[64,4096]{1,0:T(8,128)(2,1)} %copy-done.13) | copy-start | bytes 1572868
  50.2 5.8 %collective-permute-start.11 = (bf16[1536,256]{1,0:T(8,128)(2,1)}, bf16[1536,256]{1,0:T(8,128)(2,1)}, u32[]{:S(2)}, u32[]{:S(2)}) collective-permute-start(bf16[1536,256]{1,0:T(8,128)(2,1)} %gate.6.refs_11_.refs_6_.refs_12_), channel_id=1, source_target_pairs={{0,16},{16,0},{1,17},{17,1},{2,18},{18,2},{3,19},{19,3},{4,20},{20... | collective-permute-start | bytes 2359304 | tf_op jit(solution)/shard_map/ppermute | solution.py:360
  51.0 18.4 %collective-permute-start.15 = (bf16[64,4096]{1,0:T(8,128)(2,1)}, bf16[64,4096]{1,0:T(8,128)(2,1)S(1)}, u32[]{:S(2)}, u32[]{:S(2)}) collective-permute-start(bf16[64,4096]{1,0:T(8,128)(2,1)} %gate.8.refs_0_), channel_id=1, source_target_pairs={{0,32},{32,0},{64,96},{96,64},{1,33},{33,1},{65,97},{97,65},{2,34}... | collective-permute-start | bytes 1572872 | tf_op jit(solution)/shard_map/ppermute | solution.py:356
  52.6 10.8 %collective-permute-start.6 = (bf16[32,4096]{1,0:T(8,128)(2,1)S(1)}, bf16[32,4096]{1,0:T(8,128)(2,1)S(1)}, u32[]{:S(2)}, u32[]{:S(2)}) collective-permute-start(bf16[32,4096]{1,0:T(8,128)(2,1)S(1)} %slice.8), channel_id=1, source_target_pairs={{0,2},{2,4},{4,6},{6,8},{8,10},{10,12},{12,14},{14,0},{1,3},{3,5},... | collective-permute-start | bytes 786440 | tf_op jit(solution)/shard_map/ppermute | solution.py:393
  52.8 10.7 %collective-permute-start.7 = (bf16[32,4096]{1,0:T(8,128)(2,1)S(1)}, bf16[32,4096]{1,0:T(8,128)(2,1)S(1)}, u32[]{:S(2)}, u32[]{:S(2)}) collective-permute-start(bf16[32,4096]{1,0:T(8,128)(2,1)S(1)} %slice.9), channel_id=1, source_target_pairs={{0,14},{2,0},{4,2},{6,4},{8,6},{10,8},{12,10},{14,12},{1,15},{3,1}... | collective-permute-start | bytes 786440 | tf_op jit(solution)/shard_map/ppermute | solution.py:393
  63.4 7.3 %copy-start.21 = (s32[2,16,16]{2,1,0:T(8,128)S(1)}, s32[2,16,16]{2,1,0:T(8,128)}, u32[]{:S(2)}) copy-start(s32[2,16,16]{2,1,0:T(8,128)} %param.19) | copy-start | bytes 6148
  63.5 7.4 %copy-start.3 = (bf16[2,448,128]{2,1,0:T(8,128)(2,1)S(1)}, bf16[2,448,128]{2,1,0:T(8,128)(2,1)}, u32[]{:S(2)}) copy-start(bf16[2,448,128]{2,1,0:T(8,128)(2,1)} %keys.2.refs_11_.kv_near) | copy-start | bytes 688132
  70.2 11.9 %collective-permute-start.16 = (bf16[64,4096]{1,0:T(8,128)(2,1)}, bf16[64,4096]{1,0:T(8,128)(2,1)S(1)}, u32[]{:S(2)}, u32[]{:S(2)}) collective-permute-start(bf16[64,4096]{1,0:T(8,128)(2,1)} %get-tuple-element.27.refs_1_), channel_id=1, source_target_pairs={{0,16},{16,0},{1,17},{17,1},{2,18},{18,2},{3,19},{19,3},{4,20},{20... | collective-permute-start | bytes 1572872 | tf_op jit(solution)/shard_map/ppermute | solution.py:360
  70.2 11.9 %collective-permute-start.17 = (bf16[64,4096]{1,0:T(8,128)(2,1)}, bf16[64,4096]{1,0:T(8,128)(2,1)S(1)}, u32[]{:S(2)}, u32[]{:S(2)}) collective-permute-start(bf16[64,4096]{1,0:T(8,128)(2,1)} %get-tuple-element.28.refs_2_), channel_id=1, source_target_pairs={{0,16},{16,0},{1,17},{17,1},{2,18},{18,2},{3,19},{19,3},{4,20},{20... | collective-permute-start | bytes 1572872 | tf_op jit(solution)/shard_map/ppermute | solution.py:360
  70.9 11.2 %copy-start = (bf16[256,4096]{1,0:T(8,128)(2,1)S(1)}, bf16[256,4096]{1,0:T(8,128)(2,1)}, u32[]{:S(2)}) copy-start(bf16[256,4096]{1,0:T(8,128)(2,1)} %refs_0_.7) | copy-start | bytes 6291460
  70.9 11.2 %copy-start.2 = (bf16[64,4096]{1,0:T(8,128)(2,1)S(1)}, bf16[64,4096]{1,0:T(8,128)(2,1)}, u32[]{:S(2)}) copy-start(bf16[64,4096]{1,0:T(8,128)(2,1)} %get-tuple-element.27.refs_1_) | copy-start | bytes 1572868
  70.9 11.2 %copy-start.6 = (bf16[64,4096]{1,0:T(8,128)(2,1)S(1)}, bf16[64,4096]{1,0:T(8,128)(2,1)}, u32[]{:S(2)}) copy-start(bf16[64,4096]{1,0:T(8,128)(2,1)} %get-tuple-element.28.refs_2_) | copy-start | bytes 1572868
  70.9 11.2 %copy-start.7 = (bf16[2,64,128]{2,1,0:T(8,128)(2,1)S(1)}, bf16[2,64,128]{2,1,0:T(8,128)(2,1)}, u32[]{:S(2)}) copy-start(bf16[2,64,128]{2,1,0:T(8,128)(2,1)} %keys.3.refs_17_.refs_2_.kv_far) | copy-start | bytes 98308
  70.9 11.2 %copy-start.8 = (s32[4]{0:T(128)S(1)}, s32[4]{0:T(128)}, u32[]{:S(2)}) copy-start(s32[4]{0:T(128)} %pad_add_fusion.meta) | copy-start | bytes 52
  70.9 11.2 %collective-permute-start.12 = (bf16[912,128]{1,0:T(8,128)(2,1)S(1)}, bf16[912,128]{1,0:T(8,128)(2,1)S(1)}, u32[]{:S(2)}, u32[]{:S(2)}) collective-permute-start(bf16[912,128]{1,0:T(8,128)(2,1)S(1)} %pad_maximum_fusion), channel_id=1, source_target_pairs={{0,1},{1,0},{2,3},{3,2},{4,5},{5,4},{6,7},{7,6},{8,9},{9,8},{10,11... | collective-permute-start | bytes 700424 | tf_op jit(solution)/shard_map/ppermute | solution.py:364
  71.2 10.9 %collective-permute-start.13 = (bf16[2,64,128]{2,1,0:T(8,128)(2,1)}, bf16[2,64,128]{2,1,0:T(8,128)(2,1)S(1)}, u32[]{:S(2)}, u32[]{:S(2)}) collective-permute-start(bf16[2,64,128]{2,1,0:T(8,128)(2,1)} %keys.3.refs_17_.refs_2_.kv_far), channel_id=1, source_target_pairs={{0,1},{1,0},{2,3},{3,2},{4,5},{5,4},{6,7},{7,6},{8,9},{9,8},{10,11... | collective-permute-start | bytes 98312 | tf_op jit(solution)/shard_map/ppermute | solution.py:364
  82.1 1.0 copy-start.4
  87.2 10.6 %collective-permute-start.28 = (bf16[64,2048]{1,0:T(8,128)(2,1)S(1)}, bf16[64,2048]{1,0:T(8,128)(2,1)S(1)}, u32[]{:S(2)}, u32[]{:S(2)}) collective-permute-start(bf16[64,2048]{1,0:T(8,128)(2,1)S(1)} %get-tuple-element.41), channel_id=1, source_target_pairs={{0,14},{2,0},{4,2},{6,4},{8,6},{10,8},{12,10},{14,12},{1,15},{3,1}... | collective-permute-start | bytes 786440 | tf_op jit(solution)/shard_map/ppermute | solution.py:438
  88.5 12.7 %collective-permute-start.25 = (bf16[64,2048]{1,0:T(8,128)(2,1)S(1)}, bf16[64,2048]{1,0:T(8,128)(2,1)S(1)}, u32[]{:S(2)}, u32[]{:S(2)}) collective-permute-start(bf16[64,2048]{1,0:T(8,128)(2,1)S(1)} %get-tuple-element.38), channel_id=1, source_target_pairs={{0,2},{2,4},{4,6},{6,8},{8,10},{10,12},{12,14},{14,0},{1,3},{3,5},... | collective-permute-start | bytes 786440 | tf_op jit(solution)/shard_map/ppermute | solution.py:443
  89.3 12.6 %collective-permute-start.22 = (bf16[64,2048]{1,0:T(8,128)(2,1)S(1)}, bf16[64,2048]{1,0:T(8,128)(2,1)S(1)}, u32[]{:S(2)}, u32[]{:S(2)}) collective-permute-start(bf16[64,2048]{1,0:T(8,128)(2,1)S(1)} %get-tuple-element.34), channel_id=1, source_target_pairs={{0,14},{2,0},{4,2},{6,4},{8,6},{10,8},{12,10},{14,12},{1,15},{3,1}... | collective-permute-start | bytes 786440 | tf_op jit(solution)/shard_map/ppermute | solution.py:444
  91.7 13.0 %collective-permute-start.18 = (bf16[64,2048]{1,0:T(8,128)(2,1)S(1)}, bf16[64,2048]{1,0:T(8,128)(2,1)S(1)}, u32[]{:S(2)}, u32[]{:S(2)}) collective-permute-start(bf16[64,2048]{1,0:T(8,128)(2,1)S(1)} %get-tuple-element.29.refs_5_), channel_id=1, source_target_pairs={{0,2},{2,4},{4,6},{6,8},{8,10},{10,12},{12,14},{14,0},{1,3},{3,5},... | collective-permute-start | bytes 786440 | tf_op jit(solution)/shard_map/ppermute | solution.py:437
  97.9 10.0 %collective-permute-start.29 = (bf16[64,2048]{1,0:T(8,128)(2,1)S(1)}, bf16[64,2048]{1,0:T(8,128)(2,1)S(1)}, u32[]{:S(2)}, u32[]{:S(2)}) collective-permute-start(bf16[64,2048]{1,0:T(8,128)(2,1)S(1)} %add_convert_fusion.2), channel_id=1, source_target_pairs={{0,14},{2,0},{4,2},{6,4},{8,6},{10,8},{12,10},{14,12},{1,15},{3,1}... | collective-permute-start | bytes 786440 | tf_op jit(solution)/shard_map/ppermute | solution.py:444
  101.3 10.5 %collective-permute-start.26 = (bf16[64,2048]{1,0:T(8,128)(2,1)S(1)}, bf16[64,2048]{1,0:T(8,128)(2,1)S(1)}, u32[]{:S(2)}, u32[]{:S(2)}) collective-permute-start(bf16[64,2048]{1,0:T(8,128)(2,1)S(1)} %add_convert_fusion.4), channel_id=1, source_target_pairs={{0,2},{2,4},{4,6},{6,8},{8,10},{10,12},{12,14},{14,0},{1,3},{3,5},... | collective-permute-start | bytes 786440 | tf_op jit(solution)/shard_map/ppermute | solution.py:443
  102.0 11.6 %collective-permute-start.23 = (bf16[64,2048]{1,0:T(8,128)(2,1)S(1)}, bf16[64,2048]{1,0:T(8,128)(2,1)S(1)}, u32[]{:S(2)}, u32[]{:S(2)}) collective-permute-start(bf16[64,2048]{1,0:T(8,128)(2,1)S(1)} %add_convert_fusion.6), channel_id=1, source_target_pairs={{0,14},{2,0},{4,2},{6,4},{8,6},{10,8},{12,10},{14,12},{1,15},{3,1}... | collective-permute-start | bytes 786440 | tf_op jit(solution)/shard_map/ppermute | solution.py:444
  104.8 12.5 %collective-permute-start.19 = (bf16[64,2048]{1,0:T(8,128)(2,1)S(1)}, bf16[64,2048]{1,0:T(8,128)(2,1)S(1)}, u32[]{:S(2)}, u32[]{:S(2)}) collective-permute-start(bf16[64,2048]{1,0:T(8,128)(2,1)S(1)} %add_convert_fusion.9), channel_id=1, source_target_pairs={{0,2},{2,4},{4,6},{6,8},{8,10},{10,12},{12,14},{14,0},{1,3},{3,5},... | collective-permute-start | bytes 786440 | tf_op jit(solution)/shard_map/ppermute | solution.py:443
  108.0 11.2 %collective-permute-start.30 = (bf16[64,2048]{1,0:T(8,128)(2,1)S(1)}, bf16[64,2048]{1,0:T(8,128)(2,1)S(1)}, u32[]{:S(2)}, u32[]{:S(2)}) collective-permute-start(bf16[64,2048]{1,0:T(8,128)(2,1)S(1)} %add_convert_fusion.1), channel_id=1, source_target_pairs={{0,14},{2,0},{4,2},{6,4},{8,6},{10,8},{12,10},{14,12},{1,15},{3,1}... | collective-permute-start | bytes 786440 | tf_op jit(solution)/shard_map/ppermute | solution.py:444
  111.8 14.1 %collective-permute-start.27 = (bf16[64,2048]{1,0:T(8,128)(2,1)S(1)}, bf16[64,2048]{1,0:T(8,128)(2,1)S(1)}, u32[]{:S(2)}, u32[]{:S(2)}) collective-permute-start(bf16[64,2048]{1,0:T(8,128)(2,1)S(1)} %add_convert_fusion.3), channel_id=1, source_target_pairs={{0,2},{2,4},{4,6},{6,8},{8,10},{10,12},{12,14},{14,0},{1,3},{3,5},... | collective-permute-start | bytes 786440 | tf_op jit(solution)/shard_map/ppermute | solution.py:447
  113.6 15.2 %collective-permute-start.24 = (bf16[64,2048]{1,0:T(8,128)(2,1)S(1)}, bf16[64,2048]{1,0:T(8,128)(2,1)S(1)}, u32[]{:S(2)}, u32[]{:S(2)}) collective-permute-start(bf16[64,2048]{1,0:T(8,128)(2,1)S(1)} %add_convert_fusion.5), channel_id=1, source_target_pairs={{0,14},{2,0},{4,2},{6,4},{8,6},{10,8},{12,10},{14,12},{1,15},{3,1}... | collective-permute-start | bytes 786440 | tf_op jit(solution)/shard_map/ppermute | solution.py:448
  117.4 8.4 %collective-permute-start.20 = (bf16[64,2048]{1,0:T(8,128)(2,1)S(1)}, bf16[64,2048]{1,0:T(8,128)(2,1)S(1)}, u32[]{:S(2)}, u32[]{:S(2)}) collective-permute-start(bf16[64,2048]{1,0:T(8,128)(2,1)S(1)} %add_convert_fusion.8), channel_id=1, source_target_pairs={{0,2},{2,4},{4,6},{6,8},{8,10},{10,12},{12,14},{14,0},{1,3},{3,5},... | collective-permute-start | bytes 786440 | tf_op jit(solution)/shard_map/ppermute | solution.py:443
  119.1 14.5 %copy-start.18 = (bf16[64,4096]{1,0:T(8,128)(2,1)S(1)}, bf16[64,4096]{1,0:T(8,128)(2,1)}, u32[]{:S(2)}) copy-start(bf16[64,4096]{1,0:T(8,128)(2,1)} %refs_0_.5) | copy-start | bytes 1572868
  119.2 9.4 %collective-permute-start.31 = (bf16[64,2048]{1,0:T(8,128)(2,1)S(1)}, bf16[64,2048]{1,0:T(8,128)(2,1)S(1)}, u32[]{:S(2)}, u32[]{:S(2)}) collective-permute-start(bf16[64,2048]{1,0:T(8,128)(2,1)S(1)} %add_convert_fusion), channel_id=1, source_target_pairs={{0,14},{2,0},{4,2},{6,4},{8,6},{10,8},{12,10},{14,12},{1,15},{3,1}... | collective-permute-start | bytes 786440 | tf_op jit(solution)/shard_map/ppermute | solution.py:448
  125.9 7.7 %collective-permute-start.21 = (bf16[64,2048]{1,0:T(8,128)(2,1)S(1)}, bf16[64,2048]{1,0:T(8,128)(2,1)S(1)}, u32[]{:S(2)}, u32[]{:S(2)}) collective-permute-start(bf16[64,2048]{1,0:T(8,128)(2,1)S(1)} %add_convert_fusion.7), channel_id=1, source_target_pairs={{0,2},{2,4},{4,6},{6,8},{8,10},{10,12},{12,14},{14,0},{1,3},{3,5},... | collective-permute-start | bytes 786440 | tf_op jit(solution)/shard_map/ppermute | solution.py:447
  (6 other events, 4.8 us)

commit v3 on v2

--- a/solution.py
+++ b/solution.py
@@ -197,7 +197,7 @@
             scratch_shapes=scratch + [pltpu.VMEM((rows, HEAD), F32)],
         ),
         out_shape=jax.ShapeDtypeStruct(shape, BF),
-        compiler_params=pltpu.CompilerParams(vmem_limit_bytes=56 << 20),
+        compiler_params=pltpu.CompilerParams(vmem_limit_bytes=(56 if queries else 40) << 20),
         cost_estimate=pl.CostEstimate(
             flops=2 * rows * WIDTH * 512, bytes_accessed=2 * WIDTH * (rows + 512), transcendentals=0
         )
@@ -343,6 +343,7 @@
         out_specs=[anywhere] * n,
         out_shape=[jax.ShapeDtypeStruct(a.shape, a.dtype) for a in arrays],
         input_output_aliases={i: i for i in range(n)},
+        compiler_params=pltpu.CompilerParams(vmem_limit_bytes=1 << 20),
         cost_estimate=TINY,
         name="gate",
     )(*arrays, *after)

time: 135 us -> 130 us (0.963)
  local copies, waits for them, and re-layouts: 6.91 us -> 2.06 us
  Pallas kernels: 31.7 us -> 28.1 us
  starting transfers between devices: 46.3 us -> 48.4 us
  waiting for transfers between devices: 46.9 us -> 48.5 us
    unnamed x44 -> x58, local copies, waits for them, and re-layouts: 6.76 us -> 1.91 us
    pallas_call x3, Pallas kernels: 18.5 us -> 13.9 us  [project(): pl.pallas_call(functools.partial(q_kernel if queries else kv_kernel, plac...]
    ppermute x1, waiting for transfers between devices: 0.01 us -> 1.6 us  [on_device(): lax.ppermute(r[:HALF], 'z', RIGHT)]
    ppermute x1, starting transfers between devices: 1.26 us -> 2.62 us  [on_device(): l = [None, lax.ppermute(far[1], 'z', LEFT)]]
  transfers between devices with their start and end apart: 32 -> 32, of which waited for: 11 -> 14; matrix products, arithmetic and copies ran while one was open for 1% -> 1% of each run, Pallas kernels for 21% -> 18%
where the time goes in v3:
time: 130 us
  waiting for transfers between devices  48.5 us (37%)
  starting transfers between devices  48.4 us (37%)
  Pallas kernels  28.1 us (22%)
  other arithmetic  2.34 us (2%)
  local copies, waits for them, and re-layouts  2.06 us (2%)
    ppermute x3, waiting for transfers between devices, on_device(): r = lax.ppermute(r, 'z', RIGHT)  18.3 us
    pallas_call x3, Pallas kernels, project(): pl.pallas_call(functools.partial(q_kernel if queries else kv_kernel, plac...  13.9 us
    ppermute x4, starting transfers between devices, on_device(): l[c] = add(lax.ppermute(l[c], 'z', LEFT), block(-d, c))  13.6 us
    pallas_call x2, Pallas kernels, attend(): pl.pallas_call(functools.partial(attend_kernel, slots, len(after)), in_sp...  11.1 us
    ppermute x3, starting transfers between devices, on_device(): l = lax.ppermute(l, 'z', LEFT)  10.5 us
    ppermute x2, waiting for transfers between devices, from_x(): return lax.ppermute(array, ('xl', 'xh'), [(i, 3 - i) for i in range(4)])  8.96 us
    ppermute x2, starting transfers between devices, on_device(): left = lax.ppermute(l[c], 'z', LEFT)  7.54 us
    ppermute x4, waiting for transfers between devices, on_device(): l[c] = add(lax.ppermute(l[c], 'z', LEFT), block(-d, c))  6.3 us
  transfers between devices with their start and end apart: 32, of which 14 were waited for; matrix products, arithmetic and copies ran while one was open for 1% of the time, Pallas kernels for 18%

profile of v3, /device:TPU:6, one launch (start us, length us, event | category | flops | bytes accessed | tf_op | source)
XLA Modules:
  0.0 130.0 jit_solution(3622431291975389226)
XLA Ops:
  0.0 1.9 %collective-permute-start = (bf16[64,4096]{1,0:T(8,128)(2,1)}, bf16[64,4096]{1,0:T(8,128)(2,1)S(1)}, u32[]{:S(2)}, u32[]{:S(2)}) collective-permute-start(bf16[64,4096]{1,0:T(8,128)(2,1)} %refs_0_.5), channel_id=1, source_target_pairs={{0,2},{2,4},{4,6},{6,8},{8,10},{10,12},{12,14},{14,0},{1,3},{3,5},... | collective-permute-start | bytes 1572872 | tf_op jit(solution)/shard_map/ppermute | solution.py:384
  1.9 3.9 %collective-permute-start.1 = (bf16[64,4096]{1,0:T(8,128)(2,1)}, bf16[64,4096]{1,0:T(8,128)(2,1)S(1)}, u32[]{:S(2)}, u32[]{:S(2)}) collective-permute-start(bf16[64,4096]{1,0:T(8,128)(2,1)} %refs_0_.5), channel_id=1, source_target_pairs={{0,14},{2,0},{4,2},{6,4},{8,6},{10,8},{12,10},{14,12},{1,15},{3,1}... | collective-permute-start | bytes 1572872 | tf_op jit(solution)/shard_map/ppermute | solution.py:385
  5.9 0.6 pad_add_fusion.meta
  6.5 3.1 %pick.1 = (bf16[1536,256]{1,0:T(8,128)(2,1)}, bf16[64,4096]{1,0:T(8,128)(2,1)}) custom-call(s32[4]{0:T(128)} %pad_add_fusion.meta, bf16[4096,256]{1,0:T(8,128)(2,1)} %refs_10_.2, bf16[64,4096]{1,0:T(8,128)(2,1)} %bitcast.11, bf16[64,4096]{1,0:T(8,128)(2,1)} %bitcast.14, bf16[256,4096]{1,0:T(8,128)(2,1)} %refs_0_.7), custom_call_target="tpu_custom_call" | custom-call | flops 1000 | bytes 1000 | tf_op jit(solution)/shard_map/pick/pallas_call | solution.py:313
  9.6 0.5 collective-permute-start.8
  10.0 7.9 %collective-permute-done.refs_1_ = bf16[64,4096]{1,0:T(8,128)(2,1)S(1)} collective-permute-done((bf16[64,4096]{1,0:T(8,128)(2,1)}, bf16[64,4096]{1,0:T(8,128)(2,1)S(1)}, u32[]{:S(2)}, u32[]{:S(2)}) %collective-permute-start) | collective-permute-done | bytes 524320 | tf_op jit(solution)/shard_map/ppermute | solution.py:384
  18.0 3.2 %collective-permute-start.3 = (bf16[64,4096]{1,0:T(8,128)(2,1)S(1)}, bf16[64,4096]{1,0:T(8,128)(2,1)S(1)}, u32[]{:S(2)}, u32[]{:S(2)}) collective-permute-start(bf16[64,4096]{1,0:T(8,128)(2,1)S(1)} %collective-permute-done.1.refs_2_), channel_id=1, source_target_pairs={{0,14},{2,0},{4,2},{6,4},{8,6},{10,8},{12,10},{14,12},{1,15},{3,1}... | collective-permute-start | bytes 1572872 | tf_op jit(solution)/shard_map/ppermute | solution.py:385
  21.2 8.8 %collective-permute-done.8.refs_0_ = bf16[1536,256]{1,0:T(8,128)(2,1)S(1)} collective-permute-done((bf16[1536,256]{1,0:T(8,128)(2,1)}, bf16[1536,256]{1,0:T(8,128)(2,1)S(1)}, u32[]{:S(2)}, u32[]{:S(2)}) %collective-permute-start.8) | collective-permute-done | bytes 786464 | tf_op jit(solution)/shard_map/ppermute | solution.py:353
  30.0 1.6 %collective-permute-start.9 = (bf16[1536,256]{1,0:T(8,128)(2,1)S(1)}, bf16[1536,256]{1,0:T(8,128)(2,1)S(1)}, u32[]{:S(2)}, u32[]{:S(2)}) collective-permute-start(bf16[1536,256]{1,0:T(8,128)(2,1)S(1)} %gate.5.refs_10_.refs_5_.refs_11_), channel_id=1, source_target_pairs={{0,32},{32,0},{64,96},{96,64},{1,33},{33,1},{65,97},{97,65},{2,34}... | collective-permute-start | bytes 2359304 | tf_op jit(solution)/shard_map/ppermute | solution.py:357
  31.6 0.7 collective-permute-done.2.refs_3_.refs_1_
  32.3 3.3 %collective-permute-start.5 = (bf16[64,4096]{1,0:T(8,128)(2,1)S(1)}, bf16[64,4096]{1,0:T(8,128)(2,1)S(1)}, u32[]{:S(2)}, u32[]{:S(2)}) collective-permute-start(bf16[64,4096]{1,0:T(8,128)(2,1)S(1)} %collective-permute-done.3.refs_4_), channel_id=1, source_target_pairs={{0,14},{2,0},{4,2},{6,4},{8,6},{10,8},{12,10},{14,12},{1,15},{3,1}... | collective-permute-start | bytes 1572872 | tf_op jit(solution)/shard_map/ppermute | solution.py:385
  35.6 0.5 collective-permute-start.14
  36.1 9.6 %collective-permute-done.4.refs_1_.refs_5_ = bf16[64,4096]{1,0:T(8,128)(2,1)S(1)} collective-permute-done((bf16[64,4096]{1,0:T(8,128)(2,1)S(1)}, bf16[64,4096]{1,0:T(8,128)(2,1)S(1)}, u32[]{:S(2)}, u32[]{:S(2)}) %collective-permute-start.4) | collective-permute-done | bytes 524320 | tf_op jit(solution)/shard_map/ppermute | solution.py:384
  45.7 2.4 %collective-permute-done.9.refs_0_ = bf16[1536,256]{1,0:T(8,128)(2,1)S(1)} collective-permute-done((bf16[1536,256]{1,0:T(8,128)(2,1)S(1)}, bf16[1536,256]{1,0:T(8,128)(2,1)S(1)}, u32[]{:S(2)}, u32[]{:S(2)}) %collective-permute-start.9) | collective-permute-done | bytes 786464 | tf_op jit(solution)/shard_map/ppermute | solution.py:357
  48.2 0.1 collective-permute-start.11
  48.3 0.2 collective-permute-done.14.refs_0_
  48.5 1.6 %collective-permute-start.15 = (bf16[64,4096]{1,0:T(8,128)(2,1)S(1)}, bf16[64,4096]{1,0:T(8,128)(2,1)}, u32[]{:S(2)}, u32[]{:S(2)}) collective-permute-start(bf16[64,4096]{1,0:T(8,128)(2,1)S(1)} %gate.8.refs_0_), channel_id=1, source_target_pairs={{0,32},{32,0},{64,96},{96,64},{1,33},{33,1},{65,97},{97,65},{2,34}... | collective-permute-start | bytes 1572872 | tf_op jit(solution)/shard_map/ppermute | solution.py:357
  50.1 0.1 collective-permute-start.6
  50.2 3.5 %collective-permute-start.7 = (bf16[32,4096]{1,0:T(8,128)(2,1)S(1)}, bf16[32,4096]{1,0:T(8,128)(2,1)S(1)}, u32[]{:S(2)}, u32[]{:S(2)}) collective-permute-start(bf16[32,4096]{1,0:T(8,128)(2,1)S(1)} %slice.9), channel_id=1, source_target_pairs={{0,14},{2,0},{4,2},{6,4},{8,6},{10,8},{12,10},{14,12},{1,15},{3,1}... | collective-permute-start | bytes 786440 | tf_op jit(solution)/shard_map/ppermute | solution.py:394
  53.8 4.2 %keys.2.refs_11_.kv_near = bf16[2,448,128]{2,1,0:T(8,128)(2,1)S(1)} custom-call(s32[4]{0:T(128)S(1)} %copy-done.26, bf16[64,4096]{1,0:T(8,128)(2,1)S(1)} %copy-done.12, bf16[64,4096]{1,0:T(8,128)(2,1)S(1)} %copy-done.8, bf16[64,4096]{1,0:T(8,128)(2,1)S(1)} %copy-done.10, bf16[64,4096]{1,0:T(8,128)(2,1)S(1)} %collective-permute-done.2.refs_3_.refs_1_, ...), custom_call_target="tpu_custom_call" | custom-call | flops 1000 | bytes 1000 | tf_op jit(solution)/shard_map/keys/pallas_call | solution.py:186
  58.0 1.6 %collective-permute-done.6.refs_0_.refs_7_ = bf16[32,4096]{1,0:T(8,128)(2,1)S(1)} collective-permute-done((bf16[32,4096]{1,0:T(8,128)(2,1)S(1)}, bf16[32,4096]{1,0:T(8,128)(2,1)S(1)}, u32[]{:S(2)}, u32[]{:S(2)}) %collective-permute-start.6) | collective-permute-done | bytes 262176 | tf_op jit(solution)/shard_map/ppermute | solution.py:394
  59.6 2.2 %keys.3.refs_17_.refs_2_.kv_far = bf16[2,64,128]{2,1,0:T(8,128)(2,1)S(1)} custom-call(s32[4]{0:T(128)S(1)} %copy-done.26, bf16[32,4096]{1,0:T(8,128)(2,1)S(1)} %collective-permute-done.6.refs_0_.refs_7_, bf16[32,4096]{1,0:T(8,128)(2,1)S(1)} %collective-permute-done.7.refs_1_.refs_8_, f32[1,4096]{1,0:T(1,128)S(1)} %bitcast.19, bf16[64,4096]{1,0:T(8,128)(2,1)S(1)} %bitcast.13, ...), custom_call_target="tpu_custom_call" | custom-call | flops 1000 | bytes 1000 | tf_op jit(solution)/shard_map/keys/pallas_call | solution.py:186
  61.9 0.8 collective-permute-done.15.refs_1_
  62.7 0.5 collective-permute-start.17
  63.2 0.1 reshape.6
  63.4 0.3 collective-permute-start.12
  63.7 3.3 %collective-permute-start.13 = (bf16[2,64,128]{2,1,0:T(8,128)(2,1)S(1)}, bf16[2,64,128]{2,1,0:T(8,128)(2,1)S(1)}, u32[]{:S(2)}, u32[]{:S(2)}) collective-permute-start(bf16[2,64,128]{2,1,0:T(8,128)(2,1)S(1)} %keys.3.refs_17_.refs_2_.kv_far), channel_id=1, source_target_pairs={{0,1},{1,0},{2,3},{3,2},{4,5},{5,4},{6,7},{7,6},{8,9},{9,8},{10,11... | collective-permute-start | bytes 98312 | tf_op jit(solution)/shard_map/ppermute | solution.py:365
  67.0 7.5 %queries.1.q = bf16[8,4,64,128]{3,2,1,0:T(8,128)(2,1)} custom-call(s32[4]{0:T(128)} %pad_add_fusion.meta, bf16[64,4096]{1,0:T(8,128)(2,1)} %refs_0_.5, bf16[64,4096]{1,0:T(8,128)(2,1)} %copy-done.7, bf16[64,4096]{1,0:T(8,128)(2,1)} %copy-done.9, bf16[64,4096]{1,0:T(8,128)(2,1)} %copy-done.11, bf16[64,4096]{1,0:T(8,128)(2,1)} %copy-done.17, ...), custom_call_target="tpu_custom_call" | custom-call | flops 2147483648 | bytes 8388608 | tf_op jit(solution)/shard_map/queries/pallas_call | solution.py:186
  74.6 1.0 copy-done.16
  75.6 0.8 copy-done.21
  76.4 4.5 %attend.2 = (bf16[64,2048]{1,0:T(8,128)(2,1)S(1)}, bf16[64,2048]{1,0:T(8,128)(2,1)S(1)}, bf16[64,2048]{1,0:T(8,128)(2,1)S(1)}, bf16[64,2048]{1,0:T(8,128)(2,1)S(...) custom-call(s32[4]{0:T(128)S(1)} %copy-done.27, bf16[8,4,64,128]{3,2,1,0:T(8,128)(2,1)S(1)} %copy-done.16, ...), custom_call_target="tpu_custom_call" | custom-call | flops 1000 | bytes 1000 | tf_op jit(solution)/shard_map/attend/pallas_call | solution.py:281
  80.9 2.6 %collective-permute-start.28 = (bf16[64,2048]{1,0:T(8,128)(2,1)S(1)}, bf16[64,2048]{1,0:T(8,128)(2,1)S(1)}, u32[]{:S(2)}, u32[]{:S(2)}) collective-permute-start(bf16[64,2048]{1,0:T(8,128)(2,1)S(1)} %get-tuple-element.41), channel_id=1, source_target_pairs={{0,14},{2,0},{4,2},{6,4},{8,6},{10,8},{12,10},{14,12},{1,15},{3,1}... | collective-permute-start | bytes 786440 | tf_op jit(solution)/shard_map/ppermute | solution.py:439
  83.5 3.2 %collective-permute-start.22 = (bf16[64,2048]{1,0:T(8,128)(2,1)S(1)}, bf16[64,2048]{1,0:T(8,128)(2,1)S(1)}, u32[]{:S(2)}, u32[]{:S(2)}) collective-permute-start(bf16[64,2048]{1,0:T(8,128)(2,1)S(1)} %get-tuple-element.34), channel_id=1, source_target_pairs={{0,14},{2,0},{4,2},{6,4},{8,6},{10,8},{12,10},{14,12},{1,15},{3,1}... | collective-permute-start | bytes 786440 | tf_op jit(solution)/shard_map/ppermute | solution.py:445
  86.8 6.5 %attend.3 = (bf16[64,2048]{1,0:T(8,128)(2,1)S(1)}, bf16[64,2048]{1,0:T(8,128)(2,1)S(1)}, bf16[64,2048]{1,0:T(8,128)(2,1)S(1)}, bf16[64,2048]{1,0:T(8,128)(2,1)S(...) custom-call(s32[4]{0:T(128)S(1)} %copy-done.27, ...), custom_call_target="tpu_custom_call" | custom-call | flops 1000 | bytes 1000 | tf_op jit(solution)/shard_map/attend/pallas_call | solution.py:281
  93.4 3.3 %collective-permute-start.29 = (bf16[64,2048]{1,0:T(8,128)(2,1)S(1)}, bf16[64,2048]{1,0:T(8,128)(2,1)S(1)}, u32[]{:S(2)}, u32[]{:S(2)}) collective-permute-start(bf16[64,2048]{1,0:T(8,128)(2,1)S(1)} %add_convert_fusion.2), channel_id=1, source_target_pairs={{0,14},{2,0},{4,2},{6,4},{8,6},{10,8},{12,10},{14,12},{1,15},{3,1}... | collective-permute-start | bytes 786440 | tf_op jit(solution)/shard_map/ppermute | solution.py:445
  97.0 3.3 %collective-permute-start.23 = (bf16[64,2048]{1,0:T(8,128)(2,1)S(1)}, bf16[64,2048]{1,0:T(8,128)(2,1)S(1)}, u32[]{:S(2)}, u32[]{:S(2)}) collective-permute-start(bf16[64,2048]{1,0:T(8,128)(2,1)S(1)} %add_convert_fusion.6), channel_id=1, source_target_pairs={{0,14},{2,0},{4,2},{6,4},{8,6},{10,8},{12,10},{14,12},{1,15},{3,1}... | collective-permute-start | bytes 786440 | tf_op jit(solution)/shard_map/ppermute | solution.py:445
  100.4 3.1 %collective-permute-done.29 = bf16[64,2048]{1,0:T(8,128)(2,1)S(1)} collective-permute-done((bf16[64,2048]{1,0:T(8,128)(2,1)S(1)}, bf16[64,2048]{1,0:T(8,128)(2,1)S(1)}, u32[]{:S(2)}, u32[]{:S(2)}) %collective-permute-start.29) | collective-permute-done | bytes 262176 | tf_op jit(solution)/shard_map/ppermute | solution.py:445
  103.6 3.8 %collective-permute-start.30 = (bf16[64,2048]{1,0:T(8,128)(2,1)S(1)}, bf16[64,2048]{1,0:T(8,128)(2,1)S(1)}, u32[]{:S(2)}, u32[]{:S(2)}) collective-permute-start(bf16[64,2048]{1,0:T(8,128)(2,1)S(1)} %add_convert_fusion.1), channel_id=1, source_target_pairs={{0,14},{2,0},{4,2},{6,4},{8,6},{10,8},{12,10},{14,12},{1,15},{3,1}... | collective-permute-start | bytes 786440 | tf_op jit(solution)/shard_map/ppermute | solution.py:445
  107.5 1.6 %collective-permute-done.23 = bf16[64,2048]{1,0:T(8,128)(2,1)S(1)} collective-permute-done((bf16[64,2048]{1,0:T(8,128)(2,1)S(1)}, bf16[64,2048]{1,0:T(8,128)(2,1)S(1)}, u32[]{:S(2)}, u32[]{:S(2)}) %collective-permute-start.23) | collective-permute-done | bytes 262176 | tf_op jit(solution)/shard_map/ppermute | solution.py:445
  109.2 3.8 %collective-permute-start.24 = (bf16[64,2048]{1,0:T(8,128)(2,1)S(1)}, bf16[64,2048]{1,0:T(8,128)(2,1)S(1)}, u32[]{:S(2)}, u32[]{:S(2)}) collective-permute-start(bf16[64,2048]{1,0:T(8,128)(2,1)S(1)} %add_convert_fusion.5), channel_id=1, source_target_pairs={{0,14},{2,0},{4,2},{6,4},{8,6},{10,8},{12,10},{14,12},{1,15},{3,1}... | collective-permute-start | bytes 786440 | tf_op jit(solution)/shard_map/ppermute | solution.py:449
  113.1 1.6 %collective-permute-done.30 = bf16[64,2048]{1,0:T(8,128)(2,1)S(1)} collective-permute-done((bf16[64,2048]{1,0:T(8,128)(2,1)S(1)}, bf16[64,2048]{1,0:T(8,128)(2,1)S(1)}, u32[]{:S(2)}, u32[]{:S(2)}) %collective-permute-start.30) | collective-permute-done | bytes 262176 | tf_op jit(solution)/shard_map/ppermute | solution.py:445
  114.8 3.8 %collective-permute-start.31 = (bf16[64,2048]{1,0:T(8,128)(2,1)S(1)}, bf16[64,2048]{1,0:T(8,128)(2,1)S(1)}, u32[]{:S(2)}, u32[]{:S(2)}) collective-permute-start(bf16[64,2048]{1,0:T(8,128)(2,1)S(1)} %add_convert_fusion), channel_id=1, source_target_pairs={{0,14},{2,0},{4,2},{6,4},{8,6},{10,8},{12,10},{14,12},{1,15},{3,1}... | collective-permute-start | bytes 786440 | tf_op jit(solution)/shard_map/ppermute | solution.py:449
  118.6 2.7 %collective-permute-done.20 = bf16[64,2048]{1,0:T(8,128)(2,1)S(1)} collective-permute-done((bf16[64,2048]{1,0:T(8,128)(2,1)S(1)}, bf16[64,2048]{1,0:T(8,128)(2,1)S(1)}, u32[]{:S(2)}, u32[]{:S(2)}) %collective-permute-start.20) | collective-permute-done | bytes 262176 | tf_op jit(solution)/shard_map/ppermute | solution.py:444
  121.5 1.9 %collective-permute-done.31 = bf16[64,2048]{1,0:T(8,128)(2,1)S(1)} collective-permute-done((bf16[64,2048]{1,0:T(8,128)(2,1)S(1)}, bf16[64,2048]{1,0:T(8,128)(2,1)S(1)}, u32[]{:S(2)}, u32[]{:S(2)}) %collective-permute-start.31) | collective-permute-done | bytes 262176 | tf_op jit(solution)/shard_map/ppermute | solution.py:449
  123.3 0.1 convert_add_fusion
  123.4 5.6 %collective-permute-done.21 = bf16[64,2048]{1,0:T(8,128)(2,1)S(1)} collective-permute-done((bf16[64,2048]{1,0:T(8,128)(2,1)S(1)}, bf16[64,2048]{1,0:T(8,128)(2,1)S(1)}, u32[]{:S(2)}, u32[]{:S(2)}) %collective-permute-start.21) | collective-permute-done | bytes 262176 | tf_op jit(solution)/shard_map/ppermute | solution.py:448
  129.0 0.1 convert_add_fusion.1
  129.1 0.9 fusion
  (106 shorter events, 1.3 us)
Async XLA Ops:
  0.0 18.0 %collective-permute-start = (bf16[64,4096]{1,0:T(8,128)(2,1)}, bf16[64,4096]{1,0:T(8,128)(2,1)S(1)}, u32[]{:S(2)}, u32[]{:S(2)}) collective-permute-start(bf16[64,4096]{1,0:T(8,128)(2,1)} %refs_0_.5), channel_id=1, source_target_pairs={{0,2},{2,4},{4,6},{6,8},{8,10},{10,12},{12,14},{14,0},{1,3},{3,5},... | collective-permute-start | bytes 1572872 | tf_op jit(solution)/shard_map/ppermute | solution.py:384
  1.9 16.1 %collective-permute-start.1 = (bf16[64,4096]{1,0:T(8,128)(2,1)}, bf16[64,4096]{1,0:T(8,128)(2,1)S(1)}, u32[]{:S(2)}, u32[]{:S(2)}) collective-permute-start(bf16[64,4096]{1,0:T(8,128)(2,1)} %refs_0_.5), channel_id=1, source_target_pairs={{0,14},{2,0},{4,2},{6,4},{8,6},{10,8},{12,10},{14,12},{1,15},{3,1}... | collective-permute-start | bytes 1572872 | tf_op jit(solution)/shard_map/ppermute | solution.py:385
  9.6 26.1 %copy-start.23 = (bf16[64,4096]{1,0:T(8,128)(2,1)S(1)}, bf16[64,4096]{1,0:T(8,128)(2,1)}, u32[]{:S(2)}) copy-start(bf16[64,4096]{1,0:T(8,128)(2,1)} %get-tuple-element.26.refs_0_) | copy-start | bytes 1572868
  9.6 20.4 %collective-permute-start.8 = (bf16[1536,256]{1,0:T(8,128)(2,1)}, bf16[1536,256]{1,0:T(8,128)(2,1)S(1)}, u32[]{:S(2)}, u32[]{:S(2)}) collective-permute-start(bf16[1536,256]{1,0:T(8,128)(2,1)} %get-tuple-element.25), channel_id=1, source_target_pairs={{0,129},{1,128},{128,1},{129,0},{2,131},{3,130},{130,3},{131,2},{4... | collective-permute-start | bytes 2359304 | tf_op jit(solution)/shard_map/ppermute | solution.py:353
  18.0 13.6 %copy-start.7 = (bf16[64,4096]{1,0:T(8,128)(2,1)}, bf16[64,4096]{1,0:T(8,128)(2,1)S(1)}, u32[]{:S(2)}) copy-start(bf16[64,4096]{1,0:T(8,128)(2,1)S(1)} %collective-permute-done.refs_1_) | copy-start | bytes 1572868
  18.0 14.3 %collective-permute-start.2 = (bf16[64,4096]{1,0:T(8,128)(2,1)S(1)}, bf16[64,4096]{1,0:T(8,128)(2,1)S(1)}, u32[]{:S(2)}, u32[]{:S(2)}) collective-permute-start(bf16[64,4096]{1,0:T(8,128)(2,1)S(1)} %collective-permute-done.refs_1_), channel_id=1, source_target_pairs={{0,2},{2,4},{4,6},{6,8},{8,10},{10,12},{12,14},{14,0},{1,3},{3,5},... | collective-permute-start | bytes 1572872 | tf_op jit(solution)/shard_map/ppermute | solution.py:384
  18.0 14.3 %copy-start.9 = (bf16[64,4096]{1,0:T(8,128)(2,1)}, bf16[64,4096]{1,0:T(8,128)(2,1)S(1)}, u32[]{:S(2)}) copy-start(bf16[64,4096]{1,0:T(8,128)(2,1)S(1)} %collective-permute-done.1.refs_2_) | copy-start | bytes 1572868
  18.0 14.3 %collective-permute-start.3 = (bf16[64,4096]{1,0:T(8,128)(2,1)S(1)}, bf16[64,4096]{1,0:T(8,128)(2,1)S(1)}, u32[]{:S(2)}, u32[]{:S(2)}) collective-permute-start(bf16[64,4096]{1,0:T(8,128)(2,1)S(1)} %collective-permute-done.1.refs_2_), channel_id=1, source_target_pairs={{0,14},{2,0},{4,2},{6,4},{8,6},{10,8},{12,10},{14,12},{1,15},{3,1}... | collective-permute-start | bytes 1572872 | tf_op jit(solution)/shard_map/ppermute | solution.py:385
  30.0 29.6 %copy-start.2 = (bf16[1536,256]{1,0:T(8,128)(2,1)}, bf16[1536,256]{1,0:T(8,128)(2,1)S(1)}, u32[]{:S(2)}) copy-start(bf16[1536,256]{1,0:T(8,128)(2,1)S(1)} %gate.5.refs_10_.refs_5_.refs_11_) | copy-start | bytes 2359300
  30.0 18.1 %collective-permute-start.9 = (bf16[1536,256]{1,0:T(8,128)(2,1)S(1)}, bf16[1536,256]{1,0:T(8,128)(2,1)S(1)}, u32[]{:S(2)}, u32[]{:S(2)}) collective-permute-start(bf16[1536,256]{1,0:T(8,128)(2,1)S(1)} %gate.5.refs_10_.refs_5_.refs_11_), channel_id=1, source_target_pairs={{0,32},{32,0},{64,96},{96,64},{1,33},{33,1},{65,97},{97,65},{2,34}... | collective-permute-start | bytes 2359304 | tf_op jit(solution)/shard_map/ppermute | solution.py:357
  32.3 21.4 %copy-start.11 = (bf16[64,4096]{1,0:T(8,128)(2,1)}, bf16[64,4096]{1,0:T(8,128)(2,1)S(1)}, u32[]{:S(2)}) copy-start(bf16[64,4096]{1,0:T(8,128)(2,1)S(1)} %collective-permute-done.2.refs_3_.refs_1_) | copy-start | bytes 1572868
  32.3 13.4 %collective-permute-start.4 = (bf16[64,4096]{1,0:T(8,128)(2,1)S(1)}, bf16[64,4096]{1,0:T(8,128)(2,1)S(1)}, u32[]{:S(2)}, u32[]{:S(2)}) collective-permute-start(bf16[64,4096]{1,0:T(8,128)(2,1)S(1)} %collective-permute-done.2.refs_3_.refs_1_), channel_id=1, source_target_pairs={{0,2},{2,4},{4,6},{6,8},{8,10},{10,12},{12,14},{14,0},{1,3},{3,5},... | collective-permute-start | bytes 1572872 | tf_op jit(solution)/shard_map/ppermute | solution.py:384
  32.3 21.4 %copy-start.17 = (bf16[64,4096]{1,0:T(8,128)(2,1)}, bf16[64,4096]{1,0:T(8,128)(2,1)S(1)}, u32[]{:S(2)}) copy-start(bf16[64,4096]{1,0:T(8,128)(2,1)S(1)} %collective-permute-done.3.refs_4_) | copy-start | bytes 1572868
  32.3 13.4 %collective-permute-start.5 = (bf16[64,4096]{1,0:T(8,128)(2,1)S(1)}, bf16[64,4096]{1,0:T(8,128)(2,1)S(1)}, u32[]{:S(2)}, u32[]{:S(2)}) collective-permute-start(bf16[64,4096]{1,0:T(8,128)(2,1)S(1)} %collective-permute-done.3.refs_4_), channel_id=1, source_target_pairs={{0,14},{2,0},{4,2},{6,4},{8,6},{10,8},{12,10},{14,12},{1,15},{3,1}... | collective-permute-start | bytes 1572872 | tf_op jit(solution)/shard_map/ppermute | solution.py:385
  35.6 12.8 %collective-permute-start.14 = (bf16[64,4096]{1,0:T(8,128)(2,1)S(1)}, bf16[64,4096]{1,0:T(8,128)(2,1)S(1)}, u32[]{:S(2)}, u32[]{:S(2)}) collective-permute-start(bf16[64,4096]{1,0:T(8,128)(2,1)S(1)} %gate.7), channel_id=1, source_target_pairs={{0,129},{1,128},{128,1},{129,0},{2,131},{3,130},{130,3},{131,2},{4... | collective-permute-start | bytes 1572872 | tf_op jit(solution)/shard_map/ppermute | solution.py:353
  36.1 17.6 %collective-permute-start.10 = (bf16[1536,256]{1,0:T(8,128)(2,1)S(1)}, bf16[1536,256]{1,0:T(8,128)(2,1)S(1)}, u32[]{:S(2)}, u32[]{:S(2)}) collective-permute-start(bf16[1536,256]{1,0:T(8,128)(2,1)S(1)} %gate.5.refs_10_.refs_5_.refs_11_), channel_id=1, source_target_pairs={{0,16},{16,0},{1,17},{17,1},{2,18},{18,2},{3,19},{19,3},{4,20},{20... | collective-permute-start | bytes 2359304 | tf_op jit(solution)/shard_map/ppermute | solution.py:361
  45.7 8.0 %copy-start.3 = (bf16[64,4096]{1,0:T(8,128)(2,1)}, bf16[64,4096]{1,0:T(8,128)(2,1)S(1)}, u32[]{:S(2)}) copy-start(bf16[64,4096]{1,0:T(8,128)(2,1)S(1)} %collective-permute-done.4.refs_1_.refs_5_) | copy-start | bytes 1572868
  45.7 8.0 %copy-start.4 = (bf16[64,4096]{1,0:T(8,128)(2,1)}, bf16[64,4096]{1,0:T(8,128)(2,1)S(1)}, u32[]{:S(2)}) copy-start(bf16[64,4096]{1,0:T(8,128)(2,1)S(1)} %collective-permute-done.5.refs_2_.refs_6_) | copy-start | bytes 1572868
  48.1 11.5 %copy-start.1 = (bf16[1536,256]{1,0:T(8,128)(2,1)}, bf16[1536,256]{1,0:T(8,128)(2,1)S(1)}, u32[]{:S(2)}) copy-start(bf16[1536,256]{1,0:T(8,128)(2,1)S(1)} %gate.6.refs_11_.refs_6_.refs_12_) | copy-start | bytes 2359300
  48.1 5.7 %copy-start.14 = (bf16[4096,64]{0,1:T(8,128)(2,1)S(1)}, bf16[4096,64]{0,1:T(8,128)(2,1)}, u32[]{:S(2)}) copy-start(bf16[4096,64]{0,1:T(8,128)(2,1)} %param.16) | copy-start | bytes 1572868
  48.1 5.7 %copy-start.15 = (bf16[4096,64]{0,1:T(8,128)(2,1)S(1)}, bf16[4096,64]{0,1:T(8,128)(2,1)}, u32[]{:S(2)}) copy-start(bf16[4096,64]{0,1:T(8,128)(2,1)} %param.17) | copy-start | bytes 1572868
  48.2 5.5 %collective-permute-start.11 = (bf16[1536,256]{1,0:T(8,128)(2,1)S(1)}, bf16[1536,256]{1,0:T(8,128)(2,1)S(1)}, u32[]{:S(2)}, u32[]{:S(2)}) collective-permute-start(bf16[1536,256]{1,0:T(8,128)(2,1)S(1)} %gate.6.refs_11_.refs_6_.refs_12_), channel_id=1, source_target_pairs={{0,16},{16,0},{1,17},{17,1},{2,18},{18,2},{3,19},{19,3},{4,20},{20... | collective-permute-start | bytes 2359304 | tf_op jit(solution)/shard_map/ppermute | solution.py:361
  48.5 14.2 %collective-permute-start.15 = (bf16[64,4096]{1,0:T(8,128)(2,1)S(1)}, bf16[64,4096]{1,0:T(8,128)(2,1)}, u32[]{:S(2)}, u32[]{:S(2)}) collective-permute-start(bf16[64,4096]{1,0:T(8,128)(2,1)S(1)} %gate.8.refs_0_), channel_id=1, source_target_pairs={{0,32},{32,0},{64,96},{96,64},{1,33},{33,1},{65,97},{97,65},{2,34}... | collective-permute-start | bytes 1572872 | tf_op jit(solution)/shard_map/ppermute | solution.py:357
  50.1 9.5 %collective-permute-start.6 = (bf16[32,4096]{1,0:T(8,128)(2,1)S(1)}, bf16[32,4096]{1,0:T(8,128)(2,1)S(1)}, u32[]{:S(2)}, u32[]{:S(2)}) collective-permute-start(bf16[32,4096]{1,0:T(8,128)(2,1)S(1)} %slice.8), channel_id=1, source_target_pairs={{0,2},{2,4},{4,6},{6,8},{8,10},{10,12},{12,14},{14,0},{1,3},{3,5},... | collective-permute-start | bytes 786440 | tf_op jit(solution)/shard_map/ppermute | solution.py:394
  50.2 9.4 %collective-permute-start.7 = (bf16[32,4096]{1,0:T(8,128)(2,1)S(1)}, bf16[32,4096]{1,0:T(8,128)(2,1)S(1)}, u32[]{:S(2)}, u32[]{:S(2)}) collective-permute-start(bf16[32,4096]{1,0:T(8,128)(2,1)S(1)} %slice.9), channel_id=1, source_target_pairs={{0,14},{2,0},{4,2},{6,4},{8,6},{10,8},{12,10},{14,12},{1,15},{3,1}... | collective-permute-start | bytes 786440 | tf_op jit(solution)/shard_map/ppermute | solution.py:394
  53.7 5.9 %copy-start.5 = (bf16[1536,256]{1,0:T(8,128)(2,1)}, bf16[1536,256]{1,0:T(8,128)(2,1)S(1)}, u32[]{:S(2)}) copy-start(bf16[1536,256]{1,0:T(8,128)(2,1)S(1)} %collective-permute-done.10.refs_12_.refs_7_.refs_13_) | copy-start | bytes 2359300
  53.7 5.9 %copy-start.6 = (bf16[1536,256]{1,0:T(8,128)(2,1)}, bf16[1536,256]{1,0:T(8,128)(2,1)S(1)}, u32[]{:S(2)}) copy-start(bf16[1536,256]{1,0:T(8,128)(2,1)S(1)} %collective-permute-done.11.refs_13_.refs_8_.refs_14_) | copy-start | bytes 2359300
  62.7 11.9 %collective-permute-start.16 = (bf16[64,4096]{1,0:T(8,128)(2,1)S(1)}, bf16[64,4096]{1,0:T(8,128)(2,1)S(1)}, u32[]{:S(2)}, u32[]{:S(2)}) collective-permute-start(bf16[64,4096]{1,0:T(8,128)(2,1)S(1)} %get-tuple-element.27.refs_1_), channel_id=1, source_target_pairs={{0,16},{16,0},{1,17},{17,1},{2,18},{18,2},{3,19},{19,3},{4,20},{20... | collective-permute-start | bytes 1572872 | tf_op jit(solution)/shard_map/ppermute | solution.py:361
  62.7 11.9 %collective-permute-start.17 = (bf16[64,4096]{1,0:T(8,128)(2,1)}, bf16[64,4096]{1,0:T(8,128)(2,1)S(1)}, u32[]{:S(2)}, u32[]{:S(2)}) collective-permute-start(bf16[64,4096]{1,0:T(8,128)(2,1)} %get-tuple-element.28.refs_2_), channel_id=1, source_target_pairs={{0,16},{16,0},{1,17},{17,1},{2,18},{18,2},{3,19},{19,3},{4,20},{20... | collective-permute-start | bytes 1572872 | tf_op jit(solution)/shard_map/ppermute | solution.py:361
  63.4 11.2 %copy-start = (bf16[256,4096]{1,0:T(8,128)(2,1)S(1)}, bf16[256,4096]{1,0:T(8,128)(2,1)}, u32[]{:S(2)}) copy-start(bf16[256,4096]{1,0:T(8,128)(2,1)} %refs_0_.7) | copy-start | bytes 6291460
  63.4 11.2 %copy-start.27 = (s32[4]{0:T(128)S(1)}, s32[4]{0:T(128)}, u32[]{:S(2)}) copy-start(s32[4]{0:T(128)} %pad_add_fusion.meta) | copy-start | bytes 52
  63.4 11.2 %collective-permute-start.12 = (bf16[912,128]{1,0:T(8,128)(2,1)S(1)}, bf16[912,128]{1,0:T(8,128)(2,1)S(1)}, u32[]{:S(2)}, u32[]{:S(2)}) collective-permute-start(bf16[912,128]{1,0:T(8,128)(2,1)S(1)} %pad_maximum_fusion), channel_id=1, source_target_pairs={{0,1},{1,0},{2,3},{3,2},{4,5},{5,4},{6,7},{7,6},{8,9},{9,8},{10,11... | collective-permute-start | bytes 700424 | tf_op jit(solution)/shard_map/ppermute | solution.py:365
  63.7 10.9 %collective-permute-start.13 = (bf16[2,64,128]{2,1,0:T(8,128)(2,1)S(1)}, bf16[2,64,128]{2,1,0:T(8,128)(2,1)S(1)}, u32[]{:S(2)}, u32[]{:S(2)}) collective-permute-start(bf16[2,64,128]{2,1,0:T(8,128)(2,1)S(1)} %keys.3.refs_17_.refs_2_.kv_far), channel_id=1, source_target_pairs={{0,1},{1,0},{2,3},{3,2},{4,5},{5,4},{6,7},{7,6},{8,9},{9,8},{10,11... | collective-permute-start | bytes 98312 | tf_op jit(solution)/shard_map/ppermute | solution.py:365
  80.9 12.4 %collective-permute-start.28 = (bf16[64,2048]{1,0:T(8,128)(2,1)S(1)}, bf16[64,2048]{1,0:T(8,128)(2,1)S(1)}, u32[]{:S(2)}, u32[]{:S(2)}) collective-permute-start(bf16[64,2048]{1,0:T(8,128)(2,1)S(1)} %get-tuple-element.41), channel_id=1, source_target_pairs={{0,14},{2,0},{4,2},{6,4},{8,6},{10,8},{12,10},{14,12},{1,15},{3,1}... | collective-permute-start | bytes 786440 | tf_op jit(solution)/shard_map/ppermute | solution.py:439
  83.5 13.2 %collective-permute-start.25 = (bf16[64,2048]{1,0:T(8,128)(2,1)S(1)}, bf16[64,2048]{1,0:T(8,128)(2,1)S(1)}, u32[]{:S(2)}, u32[]{:S(2)}) collective-permute-start(bf16[64,2048]{1,0:T(8,128)(2,1)S(1)} %get-tuple-element.38), channel_id=1, source_target_pairs={{0,2},{2,4},{4,6},{6,8},{8,10},{10,12},{12,14},{14,0},{1,3},{3,5},... | collective-permute-start | bytes 786440 | tf_op jit(solution)/shard_map/ppermute | solution.py:444
  83.5 13.3 %collective-permute-start.22 = (bf16[64,2048]{1,0:T(8,128)(2,1)S(1)}, bf16[64,2048]{1,0:T(8,128)(2,1)S(1)}, u32[]{:S(2)}, u32[]{:S(2)}) collective-permute-start(bf16[64,2048]{1,0:T(8,128)(2,1)S(1)} %get-tuple-element.34), channel_id=1, source_target_pairs={{0,14},{2,0},{4,2},{6,4},{8,6},{10,8},{12,10},{14,12},{1,15},{3,1}... | collective-permute-start | bytes 786440 | tf_op jit(solution)/shard_map/ppermute | solution.py:445
  86.8 13.5 %collective-permute-start.18 = (bf16[64,2048]{1,0:T(8,128)(2,1)S(1)}, bf16[64,2048]{1,0:T(8,128)(2,1)S(1)}, u32[]{:S(2)}, u32[]{:S(2)}) collective-permute-start(bf16[64,2048]{1,0:T(8,128)(2,1)S(1)} %get-tuple-element.29.refs_5_), channel_id=1, source_target_pairs={{0,2},{2,4},{4,6},{6,8},{8,10},{10,12},{12,14},{14,0},{1,3},{3,5},... | collective-permute-start | bytes 786440 | tf_op jit(solution)/shard_map/ppermute | solution.py:438
  93.4 10.1 %collective-permute-start.29 = (bf16[64,2048]{1,0:T(8,128)(2,1)S(1)}, bf16[64,2048]{1,0:T(8,128)(2,1)S(1)}, u32[]{:S(2)}, u32[]{:S(2)}) collective-permute-start(bf16[64,2048]{1,0:T(8,128)(2,1)S(1)} %add_convert_fusion.2), channel_id=1, source_target_pairs={{0,14},{2,0},{4,2},{6,4},{8,6},{10,8},{12,10},{14,12},{1,15},{3,1}... | collective-permute-start | bytes 786440 | tf_op jit(solution)/shard_map/ppermute | solution.py:445
  96.8 10.5 %collective-permute-start.26 = (bf16[64,2048]{1,0:T(8,128)(2,1)S(1)}, bf16[64,2048]{1,0:T(8,128)(2,1)S(1)}, u32[]{:S(2)}, u32[]{:S(2)}) collective-permute-start(bf16[64,2048]{1,0:T(8,128)(2,1)S(1)} %add_convert_fusion.4), channel_id=1, source_target_pairs={{0,2},{2,4},{4,6},{6,8},{8,10},{10,12},{12,14},{14,0},{1,3},{3,5},... | collective-permute-start | bytes 786440 | tf_op jit(solution)/shard_map/ppermute | solution.py:444
  97.0 12.1 %collective-permute-start.23 = (bf16[64,2048]{1,0:T(8,128)(2,1)S(1)}, bf16[64,2048]{1,0:T(8,128)(2,1)S(1)}, u32[]{:S(2)}, u32[]{:S(2)}) collective-permute-start(bf16[64,2048]{1,0:T(8,128)(2,1)S(1)} %add_convert_fusion.6), channel_id=1, source_target_pairs={{0,14},{2,0},{4,2},{6,4},{8,6},{10,8},{12,10},{14,12},{1,15},{3,1}... | collective-permute-start | bytes 786440 | tf_op jit(solution)/shard_map/ppermute | solution.py:445
  100.3 12.6 %collective-permute-start.19 = (bf16[64,2048]{1,0:T(8,128)(2,1)S(1)}, bf16[64,2048]{1,0:T(8,128)(2,1)S(1)}, u32[]{:S(2)}, u32[]{:S(2)}) collective-permute-start(bf16[64,2048]{1,0:T(8,128)(2,1)S(1)} %add_convert_fusion.9), channel_id=1, source_target_pairs={{0,2},{2,4},{4,6},{6,8},{8,10},{10,12},{12,14},{14,0},{1,3},{3,5},... | collective-permute-start | bytes 786440 | tf_op jit(solution)/shard_map/ppermute | solution.py:444
  103.6 11.2 %collective-permute-start.30 = (bf16[64,2048]{1,0:T(8,128)(2,1)S(1)}, bf16[64,2048]{1,0:T(8,128)(2,1)S(1)}, u32[]{:S(2)}, u32[]{:S(2)}) collective-permute-start(bf16[64,2048]{1,0:T(8,128)(2,1)S(1)} %add_convert_fusion.1), channel_id=1, source_target_pairs={{0,14},{2,0},{4,2},{6,4},{8,6},{10,8},{12,10},{14,12},{1,15},{3,1}... | collective-permute-start | bytes 786440 | tf_op jit(solution)/shard_map/ppermute | solution.py:445
  107.4 14.1 %collective-permute-start.27 = (bf16[64,2048]{1,0:T(8,128)(2,1)S(1)}, bf16[64,2048]{1,0:T(8,128)(2,1)S(1)}, u32[]{:S(2)}, u32[]{:S(2)}) collective-permute-start(bf16[64,2048]{1,0:T(8,128)(2,1)S(1)} %add_convert_fusion.3), channel_id=1, source_target_pairs={{0,2},{2,4},{4,6},{6,8},{8,10},{10,12},{12,14},{14,0},{1,3},{3,5},... | collective-permute-start | bytes 786440 | tf_op jit(solution)/shard_map/ppermute | solution.py:448
  109.2 14.3 %collective-permute-start.24 = (bf16[64,2048]{1,0:T(8,128)(2,1)S(1)}, bf16[64,2048]{1,0:T(8,128)(2,1)S(1)}, u32[]{:S(2)}, u32[]{:S(2)}) collective-permute-start(bf16[64,2048]{1,0:T(8,128)(2,1)S(1)} %add_convert_fusion.5), channel_id=1, source_target_pairs={{0,14},{2,0},{4,2},{6,4},{8,6},{10,8},{12,10},{14,12},{1,15},{3,1}... | collective-permute-start | bytes 786440 | tf_op jit(solution)/shard_map/ppermute | solution.py:449
  113.0 8.3 %collective-permute-start.20 = (bf16[64,2048]{1,0:T(8,128)(2,1)S(1)}, bf16[64,2048]{1,0:T(8,128)(2,1)S(1)}, u32[]{:S(2)}, u32[]{:S(2)}) collective-permute-start(bf16[64,2048]{1,0:T(8,128)(2,1)S(1)} %add_convert_fusion.8), channel_id=1, source_target_pairs={{0,2},{2,4},{4,6},{6,8},{8,10},{10,12},{12,14},{14,0},{1,3},{3,5},... | collective-permute-start | bytes 786440 | tf_op jit(solution)/shard_map/ppermute | solution.py:444
  114.7 14.4 %copy-start.13 = (bf16[64,4096]{1,0:T(8,128)(2,1)S(1)}, bf16[64,4096]{1,0:T(8,128)(2,1)}, u32[]{:S(2)}) copy-start(bf16[64,4096]{1,0:T(8,128)(2,1)} %refs_0_.5) | copy-start | bytes 1572868
  114.8 8.6 %collective-permute-start.31 = (bf16[64,2048]{1,0:T(8,128)(2,1)S(1)}, bf16[64,2048]{1,0:T(8,128)(2,1)S(1)}, u32[]{:S(2)}, u32[]{:S(2)}) collective-permute-start(bf16[64,2048]{1,0:T(8,128)(2,1)S(1)} %add_convert_fusion), channel_id=1, source_target_pairs={{0,14},{2,0},{4,2},{6,4},{8,6},{10,8},{12,10},{14,12},{1,15},{3,1}... | collective-permute-start | bytes 786440 | tf_op jit(solution)/shard_map/ppermute | solution.py:449
  121.4 7.7 %collective-permute-start.21 = (bf16[64,2048]{1,0:T(8,128)(2,1)S(1)}, bf16[64,2048]{1,0:T(8,128)(2,1)S(1)}, u32[]{:S(2)}, u32[]{:S(2)}) collective-permute-start(bf16[64,2048]{1,0:T(8,128)(2,1)S(1)} %add_convert_fusion.7), channel_id=1, source_target_pairs={{0,2},{2,4},{4,6},{6,8},{8,10},{10,12},{12,14},{14,0},{1,3},{3,5},... | collective-permute-start | bytes 786440 | tf_op jit(solution)/shard_map/ppermute | solution.py:448
  (13 other events, 56.3 us)

commit v4 on v3

--- a/solution.py
+++ b/solution.py
@@ -197,7 +197,7 @@
             scratch_shapes=scratch + [pltpu.VMEM((rows, HEAD), F32)],
         ),
         out_shape=jax.ShapeDtypeStruct(shape, BF),
-        compiler_params=pltpu.CompilerParams(vmem_limit_bytes=(56 if queries else 40) << 20),
+        compiler_params=pltpu.CompilerParams(vmem_limit_bytes=(60 if queries else 40) << 20),
         cost_estimate=pl.CostEstimate(
             flops=2 * rows * WIDTH * 512, bytes_accessed=2 * WIDTH * (rows + 512), transcendentals=0
         )

time: 130 us -> 131 us (level)
  no operation moved by 1% of the time
where the time goes in v4:
time: 131 us; the launch traced here: 130 us
  waiting for transfers between devices  48.8 us (37%)
  starting transfers between devices  48.2 us (37%)
  Pallas kernels  28.4 us (22%)
  other arithmetic  2.4 us (2%)
  local copies, waits for them, and re-layouts  2.05 us (2%)
    ppermute x3, waiting for transfers between devices, on_device(): r = lax.ppermute(r, 'z', RIGHT)  18.3 us
    pallas_call x3, Pallas kernels, project(): pl.pallas_call(functools.partial(q_kernel if queries else kv_kernel, plac...  13.9 us
    ppermute x4, starting transfers between devices, on_device(): l[c] = add(lax.ppermute(l[c], 'z', LEFT), block(-d, c))  13.6 us
    pallas_call x2, Pallas kernels, attend(): pl.pallas_call(functools.partial(attend_kernel, slots, len(after)), in_sp...  11.4 us
    ppermute x3, starting transfers between devices, on_device(): l = lax.ppermute(l, 'z', LEFT)  10.4 us
    ppermute x2, waiting for transfers between devices, from_x(): return lax.ppermute(array, ('xl', 'xh'), [(i, 3 - i) for i in range(4)])  9.01 us
    ppermute x2, starting transfers between devices, on_device(): left = lax.ppermute(l[c], 'z', LEFT)  7.54 us
    ppermute x4, waiting for transfers between devices, on_device(): l[c] = add(lax.ppermute(l[c], 'z', LEFT), block(-d, c))  6.29 us
  transfers between devices with their start and end apart: 32, of which 14 were waited for; matrix products, arithmetic and copies ran while one was open for 1% of the time, Pallas kernels for 18%

profile of v4, /device:TPU:6, one launch (start us, length us, event | category | flops | bytes accessed | tf_op | source)
XLA Modules:
  0.0 130.4 jit_solution(9537971482921929149)
XLA Ops:
  0.0 1.9 %collective-permute-start = (bf16[64,4096]{1,0:T(8,128)(2,1)}, bf16[64,4096]{1,0:T(8,128)(2,1)S(1)}, u32[]{:S(2)}, u32[]{:S(2)}) collective-permute-start(bf16[64,4096]{1,0:T(8,128)(2,1)} %refs_0_.5), channel_id=1, source_target_pairs={{0,2},{2,4},{4,6},{6,8},{8,10},{10,12},{12,14},{14,0},{1,3},{3,5},... | collective-permute-start | bytes 1572872 | tf_op jit(solution)/shard_map/ppermute | solution.py:384
  1.9 3.9 %collective-permute-start.1 = (bf16[64,4096]{1,0:T(8,128)(2,1)}, bf16[64,4096]{1,0:T(8,128)(2,1)S(1)}, u32[]{:S(2)}, u32[]{:S(2)}) collective-permute-start(bf16[64,4096]{1,0:T(8,128)(2,1)} %refs_0_.5), channel_id=1, source_target_pairs={{0,14},{2,0},{4,2},{6,4},{8,6},{10,8},{12,10},{14,12},{1,15},{3,1}... | collective-permute-start | bytes 1572872 | tf_op jit(solution)/shard_map/ppermute | solution.py:385
  5.9 0.6 pad_add_fusion.meta
  6.5 3.1 %pick.1 = (bf16[1536,256]{1,0:T(8,128)(2,1)}, bf16[64,4096]{1,0:T(8,128)(2,1)}) custom-call(s32[4]{0:T(128)} %pad_add_fusion.meta, bf16[4096,256]{1,0:T(8,128)(2,1)} %refs_10_.2, bf16[64,4096]{1,0:T(8,128)(2,1)} %bitcast.11, bf16[64,4096]{1,0:T(8,128)(2,1)} %bitcast.14, bf16[256,4096]{1,0:T(8,128)(2,1)} %refs_0_.7), custom_call_target="tpu_custom_call" | custom-call | flops 1000 | bytes 1000 | tf_op jit(solution)/shard_map/pick/pallas_call | solution.py:313
  9.6 0.5 collective-permute-start.8
  10.1 7.9 %collective-permute-done.refs_1_ = bf16[64,4096]{1,0:T(8,128)(2,1)S(1)} collective-permute-done((bf16[64,4096]{1,0:T(8,128)(2,1)}, bf16[64,4096]{1,0:T(8,128)(2,1)S(1)}, u32[]{:S(2)}, u32[]{:S(2)}) %collective-permute-start) | collective-permute-done | bytes 524320 | tf_op jit(solution)/shard_map/ppermute | solution.py:384
  18.0 3.2 %collective-permute-start.3 = (bf16[64,4096]{1,0:T(8,128)(2,1)S(1)}, bf16[64,4096]{1,0:T(8,128)(2,1)S(1)}, u32[]{:S(2)}, u32[]{:S(2)}) collective-permute-start(bf16[64,4096]{1,0:T(8,128)(2,1)S(1)} %collective-permute-done.1.refs_2_), channel_id=1, source_target_pairs={{0,14},{2,0},{4,2},{6,4},{8,6},{10,8},{12,10},{14,12},{1,15},{3,1}... | collective-permute-start | bytes 1572872 | tf_op jit(solution)/shard_map/ppermute | solution.py:385
  21.2 8.8 %collective-permute-done.8.refs_0_ = bf16[1536,256]{1,0:T(8,128)(2,1)S(1)} collective-permute-done((bf16[1536,256]{1,0:T(8,128)(2,1)}, bf16[1536,256]{1,0:T(8,128)(2,1)S(1)}, u32[]{:S(2)}, u32[]{:S(2)}) %collective-permute-start.8) | collective-permute-done | bytes 786464 | tf_op jit(solution)/shard_map/ppermute | solution.py:353
  30.0 1.6 %collective-permute-start.9 = (bf16[1536,256]{1,0:T(8,128)(2,1)S(1)}, bf16[1536,256]{1,0:T(8,128)(2,1)S(1)}, u32[]{:S(2)}, u32[]{:S(2)}) collective-permute-start(bf16[1536,256]{1,0:T(8,128)(2,1)S(1)} %gate.5.refs_10_.refs_5_.refs_11_), channel_id=1, source_target_pairs={{0,32},{32,0},{64,96},{96,64},{1,33},{33,1},{65,97},{97,65},{2,34}... | collective-permute-start | bytes 2359304 | tf_op jit(solution)/shard_map/ppermute | solution.py:357
  31.6 0.7 collective-permute-done.2.refs_3_.refs_1_
  32.3 3.2 %collective-permute-start.5 = (bf16[64,4096]{1,0:T(8,128)(2,1)S(1)}, bf16[64,4096]{1,0:T(8,128)(2,1)S(1)}, u32[]{:S(2)}, u32[]{:S(2)}) collective-permute-start(bf16[64,4096]{1,0:T(8,128)(2,1)S(1)} %collective-permute-done.3.refs_4_), channel_id=1, source_target_pairs={{0,14},{2,0},{4,2},{6,4},{8,6},{10,8},{12,10},{14,12},{1,15},{3,1}... | collective-permute-start | bytes 1572872 | tf_op jit(solution)/shard_map/ppermute | solution.py:385
  35.6 0.5 collective-permute-start.14
  36.0 9.7 %collective-permute-done.4.refs_1_.refs_5_ = bf16[64,4096]{1,0:T(8,128)(2,1)S(1)} collective-permute-done((bf16[64,4096]{1,0:T(8,128)(2,1)S(1)}, bf16[64,4096]{1,0:T(8,128)(2,1)S(1)}, u32[]{:S(2)}, u32[]{:S(2)}) %collective-permute-start.4) | collective-permute-done | bytes 524320 | tf_op jit(solution)/shard_map/ppermute | solution.py:384
  45.7 2.4 %collective-permute-done.9.refs_0_ = bf16[1536,256]{1,0:T(8,128)(2,1)S(1)} collective-permute-done((bf16[1536,256]{1,0:T(8,128)(2,1)S(1)}, bf16[1536,256]{1,0:T(8,128)(2,1)S(1)}, u32[]{:S(2)}, u32[]{:S(2)}) %collective-permute-start.9) | collective-permute-done | bytes 786464 | tf_op jit(solution)/shard_map/ppermute | solution.py:357
  48.2 0.1 collective-permute-start.11
  48.3 0.2 collective-permute-done.14.refs_0_
  48.5 1.6 %collective-permute-start.15 = (bf16[64,4096]{1,0:T(8,128)(2,1)}, bf16[64,4096]{1,0:T(8,128)(2,1)}, u32[]{:S(2)}, u32[]{:S(2)}) collective-permute-start(bf16[64,4096]{1,0:T(8,128)(2,1)} %gate.8.refs_0_), channel_id=1, source_target_pairs={{0,32},{32,0},{64,96},{96,64},{1,33},{33,1},{65,97},{97,65},{2,34}... | collective-permute-start | bytes 1572872 | tf_op jit(solution)/shard_map/ppermute | solution.py:357
  50.2 3.5 %collective-permute-start.7 = (bf16[32,4096]{1,0:T(8,128)(2,1)S(1)}, bf16[32,4096]{1,0:T(8,128)(2,1)S(1)}, u32[]{:S(2)}, u32[]{:S(2)}) collective-permute-start(bf16[32,4096]{1,0:T(8,128)(2,1)S(1)} %slice.9), channel_id=1, source_target_pairs={{0,14},{2,0},{4,2},{6,4},{8,6},{10,8},{12,10},{14,12},{1,15},{3,1}... | collective-permute-start | bytes 786440 | tf_op jit(solution)/shard_map/ppermute | solution.py:394
  53.8 4.2 %keys.2.refs_11_.kv_near = bf16[2,448,128]{2,1,0:T(8,128)(2,1)S(1)} custom-call(s32[4]{0:T(128)S(1)} %copy-done.24, bf16[64,4096]{1,0:T(8,128)(2,1)S(1)} %copy-done.10, bf16[64,4096]{1,0:T(8,128)(2,1)S(1)} %collective-permute-done.refs_1_, bf16[64,4096]{1,0:T(8,128)(2,1)S(1)} %collective-permute-done.1.refs_2_, ...), custom_call_target="tpu_custom_call" | custom-call | flops 1000 | bytes 1000 | tf_op jit(solution)/shard_map/keys/pallas_call | solution.py:186
  58.0 1.6 %collective-permute-done.6.refs_0_.refs_7_ = bf16[32,4096]{1,0:T(8,128)(2,1)S(1)} collective-permute-done((bf16[32,4096]{1,0:T(8,128)(2,1)S(1)}, bf16[32,4096]{1,0:T(8,128)(2,1)S(1)}, u32[]{:S(2)}, u32[]{:S(2)}) %collective-permute-start.6) | collective-permute-done | bytes 262176 | tf_op jit(solution)/shard_map/ppermute | solution.py:394
  59.7 2.2 %keys.3.refs_17_.refs_2_.kv_far = bf16[2,64,128]{2,1,0:T(8,128)(2,1)S(1)} custom-call(s32[4]{0:T(128)S(1)} %copy-done.24, bf16[32,4096]{1,0:T(8,128)(2,1)S(1)} %collective-permute-done.6.refs_0_.refs_7_, bf16[32,4096]{1,0:T(8,128)(2,1)S(1)} %collective-permute-done.7.refs_1_.refs_8_, f32[1,4096]{1,0:T(1,128)S(1)} %bitcast.19, bf16[64,4096]{1,0:T(8,128)(2,1)S(1)} %bitcast.13, ...), custom_call_target="tpu_custom_call" | custom-call | flops 1000 | bytes 1000 | tf_op jit(solution)/shard_map/keys/pallas_call | solution.py:186
  62.0 1.0 collective-permute-done.15.refs_1_
  62.9 0.5 collective-permute-start.17
  63.5 0.1 reshape.6
  63.6 0.3 collective-permute-start.12
  63.9 3.3 %collective-permute-start.13 = (bf16[2,64,128]{2,1,0:T(8,128)(2,1)S(1)}, bf16[2,64,128]{2,1,0:T(8,128)(2,1)S(1)}, u32[]{:S(2)}, u32[]{:S(2)}) collective-permute-start(bf16[2,64,128]{2,1,0:T(8,128)(2,1)S(1)} %keys.3.refs_17_.refs_2_.kv_far), channel_id=1, source_target_pairs={{0,1},{1,0},{2,3},{3,2},{4,5},{5,4},{6,7},{7,6},{8,9},{9,8},{10,11... | collective-permute-start | bytes 98312 | tf_op jit(solution)/shard_map/ppermute | solution.py:365
  67.2 7.5 %queries.1.q = bf16[8,4,64,128]{3,2,1,0:T(8,128)(2,1)} custom-call(s32[4]{0:T(128)} %pad_add_fusion.meta, bf16[64,4096]{1,0:T(8,128)(2,1)} %refs_0_.5, bf16[64,4096]{1,0:T(8,128)(2,1)} %copy-done.7, bf16[64,4096]{1,0:T(8,128)(2,1)} %copy-done.8, bf16[64,4096]{1,0:T(8,128)(2,1)} %copy-done.9, bf16[64,4096]{1,0:T(8,128)(2,1)} %copy-done.15, ...), custom_call_target="tpu_custom_call" | custom-call | flops 2147483648 | bytes 8388608 | tf_op jit(solution)/shard_map/queries/pallas_call | solution.py:186
  74.8 1.0 copy-done.14
  75.9 0.8 copy-done.19
  76.6 4.7 %attend.2 = (bf16[64,2048]{1,0:T(8,128)(2,1)S(1)}, bf16[64,2048]{1,0:T(8,128)(2,1)S(1)}, bf16[64,2048]{1,0:T(8,128)(2,1)S(1)}, bf16[64,2048]{1,0:T(8,128)(2,1)S(...) custom-call(s32[4]{0:T(128)S(1)} %copy-done.25, bf16[8,4,64,128]{3,2,1,0:T(8,128)(2,1)S(1)} %copy-done.14, ...), custom_call_target="tpu_custom_call" | custom-call | flops 1000 | bytes 1000 | tf_op jit(solution)/shard_map/attend/pallas_call | solution.py:281
  81.3 2.4 %collective-permute-start.28 = (bf16[64,2048]{1,0:T(8,128)(2,1)S(1)}, bf16[64,2048]{1,0:T(8,128)(2,1)S(1)}, u32[]{:S(2)}, u32[]{:S(2)}) collective-permute-start(bf16[64,2048]{1,0:T(8,128)(2,1)S(1)} %get-tuple-element.41), channel_id=1, source_target_pairs={{0,14},{2,0},{4,2},{6,4},{8,6},{10,8},{12,10},{14,12},{1,15},{3,1}... | collective-permute-start | bytes 786440 | tf_op jit(solution)/shard_map/ppermute | solution.py:439
  83.7 3.2 %collective-permute-start.22 = (bf16[64,2048]{1,0:T(8,128)(2,1)S(1)}, bf16[64,2048]{1,0:T(8,128)(2,1)S(1)}, u32[]{:S(2)}, u32[]{:S(2)}) collective-permute-start(bf16[64,2048]{1,0:T(8,128)(2,1)S(1)} %get-tuple-element.34), channel_id=1, source_target_pairs={{0,14},{2,0},{4,2},{6,4},{8,6},{10,8},{12,10},{14,12},{1,15},{3,1}... | collective-permute-start | bytes 786440 | tf_op jit(solution)/shard_map/ppermute | solution.py:445
  87.0 6.7 %attend.3 = (bf16[64,2048]{1,0:T(8,128)(2,1)S(1)}, bf16[64,2048]{1,0:T(8,128)(2,1)S(1)}, bf16[64,2048]{1,0:T(8,128)(2,1)S(1)}, bf16[64,2048]{1,0:T(8,128)(2,1)S(...) custom-call(s32[4]{0:T(128)S(1)} %copy-done.25, ...), custom_call_target="tpu_custom_call" | custom-call | flops 1000 | bytes 1000 | tf_op jit(solution)/shard_map/attend/pallas_call | solution.py:281
  93.7 3.3 %collective-permute-start.29 = (bf16[64,2048]{1,0:T(8,128)(2,1)S(1)}, bf16[64,2048]{1,0:T(8,128)(2,1)S(1)}, u32[]{:S(2)}, u32[]{:S(2)}) collective-permute-start(bf16[64,2048]{1,0:T(8,128)(2,1)S(1)} %add_convert_fusion.2), channel_id=1, source_target_pairs={{0,14},{2,0},{4,2},{6,4},{8,6},{10,8},{12,10},{14,12},{1,15},{3,1}... | collective-permute-start | bytes 786440 | tf_op jit(solution)/shard_map/ppermute | solution.py:445
  97.3 3.3 %collective-permute-start.23 = (bf16[64,2048]{1,0:T(8,128)(2,1)S(1)}, bf16[64,2048]{1,0:T(8,128)(2,1)S(1)}, u32[]{:S(2)}, u32[]{:S(2)}) collective-permute-start(bf16[64,2048]{1,0:T(8,128)(2,1)S(1)} %add_convert_fusion.6), channel_id=1, source_target_pairs={{0,14},{2,0},{4,2},{6,4},{8,6},{10,8},{12,10},{14,12},{1,15},{3,1}... | collective-permute-start | bytes 786440 | tf_op jit(solution)/shard_map/ppermute | solution.py:445
  100.8 3.1 %collective-permute-done.29 = bf16[64,2048]{1,0:T(8,128)(2,1)S(1)} collective-permute-done((bf16[64,2048]{1,0:T(8,128)(2,1)S(1)}, bf16[64,2048]{1,0:T(8,128)(2,1)S(1)}, u32[]{:S(2)}, u32[]{:S(2)}) %collective-permute-start.29) | collective-permute-done | bytes 262176 | tf_op jit(solution)/shard_map/ppermute | solution.py:445
  103.9 3.8 %collective-permute-start.30 = (bf16[64,2048]{1,0:T(8,128)(2,1)S(1)}, bf16[64,2048]{1,0:T(8,128)(2,1)S(1)}, u32[]{:S(2)}, u32[]{:S(2)}) collective-permute-start(bf16[64,2048]{1,0:T(8,128)(2,1)S(1)} %add_convert_fusion.1), channel_id=1, source_target_pairs={{0,14},{2,0},{4,2},{6,4},{8,6},{10,8},{12,10},{14,12},{1,15},{3,1}... | collective-permute-start | bytes 786440 | tf_op jit(solution)/shard_map/ppermute | solution.py:445
  107.7 0.1 collective-permute-start.27
  107.8 1.6 %collective-permute-done.23 = bf16[64,2048]{1,0:T(8,128)(2,1)S(1)} collective-permute-done((bf16[64,2048]{1,0:T(8,128)(2,1)S(1)}, bf16[64,2048]{1,0:T(8,128)(2,1)S(1)}, u32[]{:S(2)}, u32[]{:S(2)}) %collective-permute-start.23) | collective-permute-done | bytes 262176 | tf_op jit(solution)/shard_map/ppermute | solution.py:445
  109.5 3.8 %collective-permute-start.24 = (bf16[64,2048]{1,0:T(8,128)(2,1)S(1)}, bf16[64,2048]{1,0:T(8,128)(2,1)S(1)}, u32[]{:S(2)}, u32[]{:S(2)}) collective-permute-start(bf16[64,2048]{1,0:T(8,128)(2,1)S(1)} %add_convert_fusion.5), channel_id=1, source_target_pairs={{0,14},{2,0},{4,2},{6,4},{8,6},{10,8},{12,10},{14,12},{1,15},{3,1}... | collective-permute-start | bytes 786440 | tf_op jit(solution)/shard_map/ppermute | solution.py:449
  113.4 1.6 %collective-permute-done.30 = bf16[64,2048]{1,0:T(8,128)(2,1)S(1)} collective-permute-done((bf16[64,2048]{1,0:T(8,128)(2,1)S(1)}, bf16[64,2048]{1,0:T(8,128)(2,1)S(1)}, u32[]{:S(2)}, u32[]{:S(2)}) %collective-permute-start.30) | collective-permute-done | bytes 262176 | tf_op jit(solution)/shard_map/ppermute | solution.py:445
  115.1 3.8 %collective-permute-start.31 = (bf16[64,2048]{1,0:T(8,128)(2,1)S(1)}, bf16[64,2048]{1,0:T(8,128)(2,1)S(1)}, u32[]{:S(2)}, u32[]{:S(2)}) collective-permute-start(bf16[64,2048]{1,0:T(8,128)(2,1)S(1)} %add_convert_fusion), channel_id=1, source_target_pairs={{0,14},{2,0},{4,2},{6,4},{8,6},{10,8},{12,10},{14,12},{1,15},{3,1}... | collective-permute-start | bytes 786440 | tf_op jit(solution)/shard_map/ppermute | solution.py:449
  118.9 2.8 %collective-permute-done.20 = bf16[64,2048]{1,0:T(8,128)(2,1)S(1)} collective-permute-done((bf16[64,2048]{1,0:T(8,128)(2,1)S(1)}, bf16[64,2048]{1,0:T(8,128)(2,1)S(1)}, u32[]{:S(2)}, u32[]{:S(2)}) %collective-permute-start.20) | collective-permute-done | bytes 262176 | tf_op jit(solution)/shard_map/ppermute | solution.py:444
  121.8 1.9 %collective-permute-done.31 = bf16[64,2048]{1,0:T(8,128)(2,1)S(1)} collective-permute-done((bf16[64,2048]{1,0:T(8,128)(2,1)S(1)}, bf16[64,2048]{1,0:T(8,128)(2,1)S(1)}, u32[]{:S(2)}, u32[]{:S(2)}) %collective-permute-start.31) | collective-permute-done | bytes 262176 | tf_op jit(solution)/shard_map/ppermute | solution.py:449
  123.7 0.1 convert_add_fusion
  123.8 5.6 %collective-permute-done.21 = bf16[64,2048]{1,0:T(8,128)(2,1)S(1)} collective-permute-done((bf16[64,2048]{1,0:T(8,128)(2,1)S(1)}, bf16[64,2048]{1,0:T(8,128)(2,1)S(1)}, u32[]{:S(2)}, u32[]{:S(2)}) %collective-permute-start.21) | collective-permute-done | bytes 262176 | tf_op jit(solution)/shard_map/ppermute | solution.py:448
  129.4 0.1 convert_add_fusion.1
  129.5 0.9 fusion
  (102 shorter events, 1.3 us)
Async XLA Ops:
  0.0 18.0 %collective-permute-start = (bf16[64,4096]{1,0:T(8,128)(2,1)}, bf16[64,4096]{1,0:T(8,128)(2,1)S(1)}, u32[]{:S(2)}, u32[]{:S(2)}) collective-permute-start(bf16[64,4096]{1,0:T(8,128)(2,1)} %refs_0_.5), channel_id=1, source_target_pairs={{0,2},{2,4},{4,6},{6,8},{8,10},{10,12},{12,14},{14,0},{1,3},{3,5},... | collective-permute-start | bytes 1572872 | tf_op jit(solution)/shard_map/ppermute | solution.py:384
  1.9 16.1 %collective-permute-start.1 = (bf16[64,4096]{1,0:T(8,128)(2,1)}, bf16[64,4096]{1,0:T(8,128)(2,1)S(1)}, u32[]{:S(2)}, u32[]{:S(2)}) collective-permute-start(bf16[64,4096]{1,0:T(8,128)(2,1)} %refs_0_.5), channel_id=1, source_target_pairs={{0,14},{2,0},{4,2},{6,4},{8,6},{10,8},{12,10},{14,12},{1,15},{3,1}... | collective-permute-start | bytes 1572872 | tf_op jit(solution)/shard_map/ppermute | solution.py:385
  9.6 25.9 %copy-start.21 = (bf16[64,4096]{1,0:T(8,128)(2,1)S(1)}, bf16[64,4096]{1,0:T(8,128)(2,1)}, u32[]{:S(2)}) copy-start(bf16[64,4096]{1,0:T(8,128)(2,1)} %get-tuple-element.26.refs_0_) | copy-start | bytes 1572868
  9.6 20.4 %collective-permute-start.8 = (bf16[1536,256]{1,0:T(8,128)(2,1)}, bf16[1536,256]{1,0:T(8,128)(2,1)S(1)}, u32[]{:S(2)}, u32[]{:S(2)}) collective-permute-start(bf16[1536,256]{1,0:T(8,128)(2,1)} %get-tuple-element.25), channel_id=1, source_target_pairs={{0,129},{1,128},{128,1},{129,0},{2,131},{3,130},{130,3},{131,2},{4... | collective-permute-start | bytes 2359304 | tf_op jit(solution)/shard_map/ppermute | solution.py:353
  18.0 35.7 %copy-start.7 = (bf16[64,4096]{1,0:T(8,128)(2,1)}, bf16[64,4096]{1,0:T(8,128)(2,1)S(1)}, u32[]{:S(2)}) copy-start(bf16[64,4096]{1,0:T(8,128)(2,1)S(1)} %collective-permute-done.refs_1_) | copy-start | bytes 1572868
  18.0 14.3 %collective-permute-start.2 = (bf16[64,4096]{1,0:T(8,128)(2,1)S(1)}, bf16[64,4096]{1,0:T(8,128)(2,1)S(1)}, u32[]{:S(2)}, u32[]{:S(2)}) collective-permute-start(bf16[64,4096]{1,0:T(8,128)(2,1)S(1)} %collective-permute-done.refs_1_), channel_id=1, source_target_pairs={{0,2},{2,4},{4,6},{6,8},{8,10},{10,12},{12,14},{14,0},{1,3},{3,5},... | collective-permute-start | bytes 1572872 | tf_op jit(solution)/shard_map/ppermute | solution.py:384
  18.0 35.7 %copy-start.8 = (bf16[64,4096]{1,0:T(8,128)(2,1)}, bf16[64,4096]{1,0:T(8,128)(2,1)S(1)}, u32[]{:S(2)}) copy-start(bf16[64,4096]{1,0:T(8,128)(2,1)S(1)} %collective-permute-done.1.refs_2_) | copy-start | bytes 1572868
  18.0 14.3 %collective-permute-start.3 = (bf16[64,4096]{1,0:T(8,128)(2,1)S(1)}, bf16[64,4096]{1,0:T(8,128)(2,1)S(1)}, u32[]{:S(2)}, u32[]{:S(2)}) collective-permute-start(bf16[64,4096]{1,0:T(8,128)(2,1)S(1)} %collective-permute-done.1.refs_2_), channel_id=1, source_target_pairs={{0,14},{2,0},{4,2},{6,4},{8,6},{10,8},{12,10},{14,12},{1,15},{3,1}... | collective-permute-start | bytes 1572872 | tf_op jit(solution)/shard_map/ppermute | solution.py:385
  30.0 29.6 %copy-start.2 = (bf16[1536,256]{1,0:T(8,128)(2,1)}, bf16[1536,256]{1,0:T(8,128)(2,1)S(1)}, u32[]{:S(2)}) copy-start(bf16[1536,256]{1,0:T(8,128)(2,1)S(1)} %gate.5.refs_10_.refs_5_.refs_11_) | copy-start | bytes 2359300
  30.0 18.1 %collective-permute-start.9 = (bf16[1536,256]{1,0:T(8,128)(2,1)S(1)}, bf16[1536,256]{1,0:T(8,128)(2,1)S(1)}, u32[]{:S(2)}, u32[]{:S(2)}) collective-permute-start(bf16[1536,256]{1,0:T(8,128)(2,1)S(1)} %gate.5.refs_10_.refs_5_.refs_11_), channel_id=1, source_target_pairs={{0,32},{32,0},{64,96},{96,64},{1,33},{33,1},{65,97},{97,65},{2,34}... | collective-permute-start | bytes 2359304 | tf_op jit(solution)/shard_map/ppermute | solution.py:357
  32.3 21.4 %copy-start.9 = (bf16[64,4096]{1,0:T(8,128)(2,1)}, bf16[64,4096]{1,0:T(8,128)(2,1)S(1)}, u32[]{:S(2)}) copy-start(bf16[64,4096]{1,0:T(8,128)(2,1)S(1)} %collective-permute-done.2.refs_3_.refs_1_) | copy-start | bytes 1572868
  32.3 13.4 %collective-permute-start.4 = (bf16[64,4096]{1,0:T(8,128)(2,1)S(1)}, bf16[64,4096]{1,0:T(8,128)(2,1)S(1)}, u32[]{:S(2)}, u32[]{:S(2)}) collective-permute-start(bf16[64,4096]{1,0:T(8,128)(2,1)S(1)} %collective-permute-done.2.refs_3_.refs_1_), channel_id=1, source_target_pairs={{0,2},{2,4},{4,6},{6,8},{8,10},{10,12},{12,14},{14,0},{1,3},{3,5},... | collective-permute-start | bytes 1572872 | tf_op jit(solution)/shard_map/ppermute | solution.py:384
  32.3 21.4 %copy-start.15 = (bf16[64,4096]{1,0:T(8,128)(2,1)}, bf16[64,4096]{1,0:T(8,128)(2,1)S(1)}, u32[]{:S(2)}) copy-start(bf16[64,4096]{1,0:T(8,128)(2,1)S(1)} %collective-permute-done.3.refs_4_) | copy-start | bytes 1572868
  32.3 13.4 %collective-permute-start.5 = (bf16[64,4096]{1,0:T(8,128)(2,1)S(1)}, bf16[64,4096]{1,0:T(8,128)(2,1)S(1)}, u32[]{:S(2)}, u32[]{:S(2)}) collective-permute-start(bf16[64,4096]{1,0:T(8,128)(2,1)S(1)} %collective-permute-done.3.refs_4_), channel_id=1, source_target_pairs={{0,14},{2,0},{4,2},{6,4},{8,6},{10,8},{12,10},{14,12},{1,15},{3,1}... | collective-permute-start | bytes 1572872 | tf_op jit(solution)/shard_map/ppermute | solution.py:385
  35.6 12.9 %collective-permute-start.14 = (bf16[64,4096]{1,0:T(8,128)(2,1)S(1)}, bf16[64,4096]{1,0:T(8,128)(2,1)}, u32[]{:S(2)}, u32[]{:S(2)}) collective-permute-start(bf16[64,4096]{1,0:T(8,128)(2,1)S(1)} %gate.7), channel_id=1, source_target_pairs={{0,129},{1,128},{128,1},{129,0},{2,131},{3,130},{130,3},{131,2},{4... | collective-permute-start | bytes 1572872 | tf_op jit(solution)/shard_map/ppermute | solution.py:353
  36.0 17.7 %collective-permute-start.10 = (bf16[1536,256]{1,0:T(8,128)(2,1)S(1)}, bf16[1536,256]{1,0:T(8,128)(2,1)S(1)}, u32[]{:S(2)}, u32[]{:S(2)}) collective-permute-start(bf16[1536,256]{1,0:T(8,128)(2,1)S(1)} %gate.5.refs_10_.refs_5_.refs_11_), channel_id=1, source_target_pairs={{0,16},{16,0},{1,17},{17,1},{2,18},{18,2},{3,19},{19,3},{4,20},{20... | collective-permute-start | bytes 2359304 | tf_op jit(solution)/shard_map/ppermute | solution.py:361
  45.7 8.0 %copy-start.3 = (bf16[64,4096]{1,0:T(8,128)(2,1)}, bf16[64,4096]{1,0:T(8,128)(2,1)S(1)}, u32[]{:S(2)}) copy-start(bf16[64,4096]{1,0:T(8,128)(2,1)S(1)} %collective-permute-done.4.refs_1_.refs_5_) | copy-start | bytes 1572868
  45.7 8.1 %copy-start.4 = (bf16[64,4096]{1,0:T(8,128)(2,1)}, bf16[64,4096]{1,0:T(8,128)(2,1)S(1)}, u32[]{:S(2)}) copy-start(bf16[64,4096]{1,0:T(8,128)(2,1)S(1)} %collective-permute-done.5.refs_2_.refs_6_) | copy-start | bytes 1572868
  48.1 11.5 %copy-start.1 = (bf16[1536,256]{1,0:T(8,128)(2,1)}, bf16[1536,256]{1,0:T(8,128)(2,1)S(1)}, u32[]{:S(2)}) copy-start(bf16[1536,256]{1,0:T(8,128)(2,1)S(1)} %gate.6.refs_11_.refs_6_.refs_12_) | copy-start | bytes 2359300
  48.1 5.7 %copy-start.13 = (bf16[4096,64]{0,1:T(8,128)(2,1)S(1)}, bf16[4096,64]{0,1:T(8,128)(2,1)}, u32[]{:S(2)}) copy-start(bf16[4096,64]{0,1:T(8,128)(2,1)} %param.17) | copy-start | bytes 1572868
  48.1 5.7 %copy-start.20 = (f32[2,64,128]{2,1,0:T(8,128)S(1)}, f32[2,64,128]{2,1,0:T(8,128)}, u32[]{:S(2)}) copy-start(f32[2,64,128]{2,1,0:T(8,128)} %constant.31.clone.refs_15_.refs_10_.refs_16_) | copy-start | bytes 196612
  48.2 5.5 %collective-permute-start.11 = (bf16[1536,256]{1,0:T(8,128)(2,1)S(1)}, bf16[1536,256]{1,0:T(8,128)(2,1)S(1)}, u32[]{:S(2)}, u32[]{:S(2)}) collective-permute-start(bf16[1536,256]{1,0:T(8,128)(2,1)S(1)} %gate.6.refs_11_.refs_6_.refs_12_), channel_id=1, source_target_pairs={{0,16},{16,0},{1,17},{17,1},{2,18},{18,2},{3,19},{19,3},{4,20},{20... | collective-permute-start | bytes 2359304 | tf_op jit(solution)/shard_map/ppermute | solution.py:361
  48.5 14.4 %collective-permute-start.15 = (bf16[64,4096]{1,0:T(8,128)(2,1)}, bf16[64,4096]{1,0:T(8,128)(2,1)}, u32[]{:S(2)}, u32[]{:S(2)}) collective-permute-start(bf16[64,4096]{1,0:T(8,128)(2,1)} %gate.8.refs_0_), channel_id=1, source_target_pairs={{0,32},{32,0},{64,96},{96,64},{1,33},{33,1},{65,97},{97,65},{2,34}... | collective-permute-start | bytes 1572872 | tf_op jit(solution)/shard_map/ppermute | solution.py:357
  50.1 9.5 %collective-permute-start.6 = (bf16[32,4096]{1,0:T(8,128)(2,1)S(1)}, bf16[32,4096]{1,0:T(8,128)(2,1)S(1)}, u32[]{:S(2)}, u32[]{:S(2)}) collective-permute-start(bf16[32,4096]{1,0:T(8,128)(2,1)S(1)} %slice.8), channel_id=1, source_target_pairs={{0,2},{2,4},{4,6},{6,8},{8,10},{10,12},{12,14},{14,0},{1,3},{3,5},... | collective-permute-start | bytes 786440 | tf_op jit(solution)/shard_map/ppermute | solution.py:394
  50.2 9.4 %collective-permute-start.7 = (bf16[32,4096]{1,0:T(8,128)(2,1)S(1)}, bf16[32,4096]{1,0:T(8,128)(2,1)S(1)}, u32[]{:S(2)}, u32[]{:S(2)}) collective-permute-start(bf16[32,4096]{1,0:T(8,128)(2,1)S(1)} %slice.9), channel_id=1, source_target_pairs={{0,14},{2,0},{4,2},{6,4},{8,6},{10,8},{12,10},{14,12},{1,15},{3,1}... | collective-permute-start | bytes 786440 | tf_op jit(solution)/shard_map/ppermute | solution.py:394
  53.7 5.9 %copy-start.5 = (bf16[1536,256]{1,0:T(8,128)(2,1)}, bf16[1536,256]{1,0:T(8,128)(2,1)S(1)}, u32[]{:S(2)}) copy-start(bf16[1536,256]{1,0:T(8,128)(2,1)S(1)} %collective-permute-done.10.refs_12_.refs_7_.refs_13_) | copy-start | bytes 2359300
  53.7 5.9 %copy-start.6 = (bf16[1536,256]{1,0:T(8,128)(2,1)}, bf16[1536,256]{1,0:T(8,128)(2,1)S(1)}, u32[]{:S(2)}) copy-start(bf16[1536,256]{1,0:T(8,128)(2,1)S(1)} %collective-permute-done.11.refs_13_.refs_8_.refs_14_) | copy-start | bytes 2359300
  62.9 11.8 %collective-permute-start.16 = (bf16[64,4096]{1,0:T(8,128)(2,1)}, bf16[64,4096]{1,0:T(8,128)(2,1)S(1)}, u32[]{:S(2)}, u32[]{:S(2)}) collective-permute-start(bf16[64,4096]{1,0:T(8,128)(2,1)} %get-tuple-element.27.refs_1_), channel_id=1, source_target_pairs={{0,16},{16,0},{1,17},{17,1},{2,18},{18,2},{3,19},{19,3},{4,20},{20... | collective-permute-start | bytes 1572872 | tf_op jit(solution)/shard_map/ppermute | solution.py:361
  62.9 11.9 %collective-permute-start.17 = (bf16[64,4096]{1,0:T(8,128)(2,1)}, bf16[64,4096]{1,0:T(8,128)(2,1)S(1)}, u32[]{:S(2)}, u32[]{:S(2)}) collective-permute-start(bf16[64,4096]{1,0:T(8,128)(2,1)} %get-tuple-element.28.refs_2_), channel_id=1, source_target_pairs={{0,16},{16,0},{1,17},{17,1},{2,18},{18,2},{3,19},{19,3},{4,20},{20... | collective-permute-start | bytes 1572872 | tf_op jit(solution)/shard_map/ppermute | solution.py:361
  63.6 11.2 %copy-start = (bf16[256,4096]{1,0:T(8,128)(2,1)S(1)}, bf16[256,4096]{1,0:T(8,128)(2,1)}, u32[]{:S(2)}) copy-start(bf16[256,4096]{1,0:T(8,128)(2,1)} %refs_0_.7) | copy-start | bytes 6291460
  63.6 11.2 %copy-start.25 = (s32[4]{0:T(128)S(1)}, s32[4]{0:T(128)}, u32[]{:S(2)}) copy-start(s32[4]{0:T(128)} %pad_add_fusion.meta) | copy-start | bytes 52
  63.6 11.2 %collective-permute-start.12 = (bf16[912,128]{1,0:T(8,128)(2,1)S(1)}, bf16[912,128]{1,0:T(8,128)(2,1)S(1)}, u32[]{:S(2)}, u32[]{:S(2)}) collective-permute-start(bf16[912,128]{1,0:T(8,128)(2,1)S(1)} %pad_maximum_fusion), channel_id=1, source_target_pairs={{0,1},{1,0},{2,3},{3,2},{4,5},{5,4},{6,7},{7,6},{8,9},{9,8},{10,11... | collective-permute-start | bytes 700424 | tf_op jit(solution)/shard_map/ppermute | solution.py:365
  63.9 10.9 %collective-permute-start.13 = (bf16[2,64,128]{2,1,0:T(8,128)(2,1)S(1)}, bf16[2,64,128]{2,1,0:T(8,128)(2,1)S(1)}, u32[]{:S(2)}, u32[]{:S(2)}) collective-permute-start(bf16[2,64,128]{2,1,0:T(8,128)(2,1)S(1)} %keys.3.refs_17_.refs_2_.kv_far), channel_id=1, source_target_pairs={{0,1},{1,0},{2,3},{3,2},{4,5},{5,4},{6,7},{7,6},{8,9},{9,8},{10,11... | collective-permute-start | bytes 98312 | tf_op jit(solution)/shard_map/ppermute | solution.py:365
  81.3 12.3 %collective-permute-start.28 = (bf16[64,2048]{1,0:T(8,128)(2,1)S(1)}, bf16[64,2048]{1,0:T(8,128)(2,1)S(1)}, u32[]{:S(2)}, u32[]{:S(2)}) collective-permute-start(bf16[64,2048]{1,0:T(8,128)(2,1)S(1)} %get-tuple-element.41), channel_id=1, source_target_pairs={{0,14},{2,0},{4,2},{6,4},{8,6},{10,8},{12,10},{14,12},{1,15},{3,1}... | collective-permute-start | bytes 786440 | tf_op jit(solution)/shard_map/ppermute | solution.py:439
  83.7 13.3 %collective-permute-start.25 = (bf16[64,2048]{1,0:T(8,128)(2,1)S(1)}, bf16[64,2048]{1,0:T(8,128)(2,1)S(1)}, u32[]{:S(2)}, u32[]{:S(2)}) collective-permute-start(bf16[64,2048]{1,0:T(8,128)(2,1)S(1)} %get-tuple-element.38), channel_id=1, source_target_pairs={{0,2},{2,4},{4,6},{6,8},{8,10},{10,12},{12,14},{14,0},{1,3},{3,5},... | collective-permute-start | bytes 786440 | tf_op jit(solution)/shard_map/ppermute | solution.py:444
  83.7 13.5 %collective-permute-start.22 = (bf16[64,2048]{1,0:T(8,128)(2,1)S(1)}, bf16[64,2048]{1,0:T(8,128)(2,1)S(1)}, u32[]{:S(2)}, u32[]{:S(2)}) collective-permute-start(bf16[64,2048]{1,0:T(8,128)(2,1)S(1)} %get-tuple-element.34), channel_id=1, source_target_pairs={{0,14},{2,0},{4,2},{6,4},{8,6},{10,8},{12,10},{14,12},{1,15},{3,1}... | collective-permute-start | bytes 786440 | tf_op jit(solution)/shard_map/ppermute | solution.py:445
  87.0 13.6 %collective-permute-start.18 = (bf16[64,2048]{1,0:T(8,128)(2,1)S(1)}, bf16[64,2048]{1,0:T(8,128)(2,1)S(1)}, u32[]{:S(2)}, u32[]{:S(2)}) collective-permute-start(bf16[64,2048]{1,0:T(8,128)(2,1)S(1)} %get-tuple-element.29.refs_5_), channel_id=1, source_target_pairs={{0,2},{2,4},{4,6},{6,8},{8,10},{10,12},{12,14},{14,0},{1,3},{3,5},... | collective-permute-start | bytes 786440 | tf_op jit(solution)/shard_map/ppermute | solution.py:438
  93.7 10.1 %collective-permute-start.29 = (bf16[64,2048]{1,0:T(8,128)(2,1)S(1)}, bf16[64,2048]{1,0:T(8,128)(2,1)S(1)}, u32[]{:S(2)}, u32[]{:S(2)}) collective-permute-start(bf16[64,2048]{1,0:T(8,128)(2,1)S(1)} %add_convert_fusion.2), channel_id=1, source_target_pairs={{0,14},{2,0},{4,2},{6,4},{8,6},{10,8},{12,10},{14,12},{1,15},{3,1}... | collective-permute-start | bytes 786440 | tf_op jit(solution)/shard_map/ppermute | solution.py:445
  97.1 10.5 %collective-permute-start.26 = (bf16[64,2048]{1,0:T(8,128)(2,1)S(1)}, bf16[64,2048]{1,0:T(8,128)(2,1)S(1)}, u32[]{:S(2)}, u32[]{:S(2)}) collective-permute-start(bf16[64,2048]{1,0:T(8,128)(2,1)S(1)} %add_convert_fusion.4), channel_id=1, source_target_pairs={{0,2},{2,4},{4,6},{6,8},{8,10},{10,12},{12,14},{14,0},{1,3},{3,5},... | collective-permute-start | bytes 786440 | tf_op jit(solution)/shard_map/ppermute | solution.py:444
  97.3 12.1 %collective-permute-start.23 = (bf16[64,2048]{1,0:T(8,128)(2,1)S(1)}, bf16[64,2048]{1,0:T(8,128)(2,1)S(1)}, u32[]{:S(2)}, u32[]{:S(2)}) collective-permute-start(bf16[64,2048]{1,0:T(8,128)(2,1)S(1)} %add_convert_fusion.6), channel_id=1, source_target_pairs={{0,14},{2,0},{4,2},{6,4},{8,6},{10,8},{12,10},{14,12},{1,15},{3,1}... | collective-permute-start | bytes 786440 | tf_op jit(solution)/shard_map/ppermute | solution.py:445
  100.7 12.6 %collective-permute-start.19 = (bf16[64,2048]{1,0:T(8,128)(2,1)S(1)}, bf16[64,2048]{1,0:T(8,128)(2,1)S(1)}, u32[]{:S(2)}, u32[]{:S(2)}) collective-permute-start(bf16[64,2048]{1,0:T(8,128)(2,1)S(1)} %add_convert_fusion.9), channel_id=1, source_target_pairs={{0,2},{2,4},{4,6},{6,8},{8,10},{10,12},{12,14},{14,0},{1,3},{3,5},... | collective-permute-start | bytes 786440 | tf_op jit(solution)/shard_map/ppermute | solution.py:444
  103.9 11.2 %collective-permute-start.30 = (bf16[64,2048]{1,0:T(8,128)(2,1)S(1)}, bf16[64,2048]{1,0:T(8,128)(2,1)S(1)}, u32[]{:S(2)}, u32[]{:S(2)}) collective-permute-start(bf16[64,2048]{1,0:T(8,128)(2,1)S(1)} %add_convert_fusion.1), channel_id=1, source_target_pairs={{0,14},{2,0},{4,2},{6,4},{8,6},{10,8},{12,10},{14,12},{1,15},{3,1}... | collective-permute-start | bytes 786440 | tf_op jit(solution)/shard_map/ppermute | solution.py:445
  107.7 14.1 %collective-permute-start.27 = (bf16[64,2048]{1,0:T(8,128)(2,1)S(1)}, bf16[64,2048]{1,0:T(8,128)(2,1)S(1)}, u32[]{:S(2)}, u32[]{:S(2)}) collective-permute-start(bf16[64,2048]{1,0:T(8,128)(2,1)S(1)} %add_convert_fusion.3), channel_id=1, source_target_pairs={{0,2},{2,4},{4,6},{6,8},{8,10},{10,12},{12,14},{14,0},{1,3},{3,5},... | collective-permute-start | bytes 786440 | tf_op jit(solution)/shard_map/ppermute | solution.py:448
  109.5 14.3 %collective-permute-start.24 = (bf16[64,2048]{1,0:T(8,128)(2,1)S(1)}, bf16[64,2048]{1,0:T(8,128)(2,1)S(1)}, u32[]{:S(2)}, u32[]{:S(2)}) collective-permute-start(bf16[64,2048]{1,0:T(8,128)(2,1)S(1)} %add_convert_fusion.5), channel_id=1, source_target_pairs={{0,14},{2,0},{4,2},{6,4},{8,6},{10,8},{12,10},{14,12},{1,15},{3,1}... | collective-permute-start | bytes 786440 | tf_op jit(solution)/shard_map/ppermute | solution.py:449
  113.3 8.3 %collective-permute-start.20 = (bf16[64,2048]{1,0:T(8,128)(2,1)S(1)}, bf16[64,2048]{1,0:T(8,128)(2,1)S(1)}, u32[]{:S(2)}, u32[]{:S(2)}) collective-permute-start(bf16[64,2048]{1,0:T(8,128)(2,1)S(1)} %add_convert_fusion.8), channel_id=1, source_target_pairs={{0,2},{2,4},{4,6},{6,8},{8,10},{10,12},{12,14},{14,0},{1,3},{3,5},... | collective-permute-start | bytes 786440 | tf_op jit(solution)/shard_map/ppermute | solution.py:444
  115.0 14.4 %copy-start.11 = (bf16[64,4096]{1,0:T(8,128)(2,1)S(1)}, bf16[64,4096]{1,0:T(8,128)(2,1)}, u32[]{:S(2)}) copy-start(bf16[64,4096]{1,0:T(8,128)(2,1)} %refs_0_.5) | copy-start | bytes 1572868
  115.1 8.6 %collective-permute-start.31 = (bf16[64,2048]{1,0:T(8,128)(2,1)S(1)}, bf16[64,2048]{1,0:T(8,128)(2,1)S(1)}, u32[]{:S(2)}, u32[]{:S(2)}) collective-permute-start(bf16[64,2048]{1,0:T(8,128)(2,1)S(1)} %add_convert_fusion), channel_id=1, source_target_pairs={{0,14},{2,0},{4,2},{6,4},{8,6},{10,8},{12,10},{14,12},{1,15},{3,1}... | collective-permute-start | bytes 786440 | tf_op jit(solution)/shard_map/ppermute | solution.py:449
  121.7 7.7 %collective-permute-start.21 = (bf16[64,2048]{1,0:T(8,128)(2,1)S(1)}, bf16[64,2048]{1,0:T(8,128)(2,1)S(1)}, u32[]{:S(2)}, u32[]{:S(2)}) collective-permute-start(bf16[64,2048]{1,0:T(8,128)(2,1)S(1)} %add_convert_fusion.7), channel_id=1, source_target_pairs={{0,2},{2,4},{4,6},{6,8},{8,10},{10,12},{12,14},{14,0},{1,3},{3,5},... | collective-permute-start | bytes 786440 | tf_op jit(solution)/shard_map/ppermute | solution.py:448
  (11 other events, 45.4 us)
